TPU v7x, 512 devices: a whole 4x8x8 slice. The times are simulated.
512 devices in a mesh: img: 32 (over x_hi, y, core), txt: 16 (over z, x_lo).
Axes of the slice: x: 4 (x_hi: 2, x_lo: 2; x = x_hi * 2 + x_lo), y: 8, z: 8, core: 2. Of those that a mesh axis runs over, the one named last changes fastest.
Arguments:
- image_student: bfloat16 [24576, 512], P(('img', 'txt')), may hold values from -16 to 16
- text_student: bfloat16 [24576, 512], P(('img', 'txt')), may hold values from -16 to 16
- image_teacher: bfloat16 [24576, 768], P(('img', 'txt')), may hold values from -16 to 16
- text_teacher: bfloat16 [24576, 768], P(('img', 'txt')), may hold values from -16 to 16
Outputs:
- image_loss: float32 [24576], P(('img', 'txt'))
- text_loss: float32 [24576], P(('img', 'txt'))
- mean_loss: float32 [], replicated
All inputs are finite; a program needn't handle non-finite values.
Results may differ from a plain program's by a relative error of at most 0.0003.
Values may be sent and summed in bfloat16 or wider, within the bound.
No kernel may reach another device: no remote copies, remote signals or barrier semaphores. Data moves between devices by JAX's collectives and lax.ppermute only.
A program may use at most 64 MiB of HBM per device.

v0:
```python
import math

import jax
import jax.numpy as jnp
from jax import lax
from jax.sharding import PartitionSpec as P

mixing = 0.5
floor_value = -1e30


def joined(x, axis, combine):
    everything = jax.tree.map(lambda part: lax.all_gather(part, axis), x)
    first = jax.tree.map(lambda part: part[0], everything)

    def turn(k, so_far):
        return combine(so_far, jax.tree.map(lambda part: part[k], everything))

    return lax.fori_loop(1, lax.axis_size(axis), turn, first)


def contract(left, right):
    return lax.dot_general(
        left, right, (((1,), (1,)), ((), ())), preferred_element_type=jnp.float32
    )


def partials(logits, gram, same, axis):
    peak = jnp.max(logits, axis=axis)
    total = jnp.sum(jnp.exp(logits - jnp.expand_dims(peak, axis)), axis=axis)
    masked = jnp.where(same, floor_value, gram)
    top = jnp.max(masked, axis=axis)
    weights = jnp.where(same, 0.0, jnp.exp(masked - jnp.expand_dims(top, axis)))
    mass = jnp.sum(weights, axis=axis)
    weighted = jnp.sum(weights * logits, axis=axis)
    diagonal = jnp.sum(jnp.where(same, logits, 0.0), axis=axis)
    return (peak, total, top, mass, weighted, diagonal)


def tile_stats(rows, row_index, columns, column_index):
    student_rows, image_rows, text_rows = rows
    student_cols, image_cols, text_cols = columns
    sfactor = 2.0 / math.sqrt(student_rows.shape[1])
    tfactor = 3.0 / math.sqrt(image_rows.shape[1])
    logits = contract(student_rows, student_cols) * sfactor
    same = row_index[:, None] == column_index[None, :]
    along_rows = partials(logits, contract(image_rows, image_cols) * tfactor, same, 1)
    along_cols = partials(logits, contract(text_rows, text_cols) * tfactor, same, 0)
    return (along_rows, along_cols)


def combine(first, second):
    peak_one, total_one, top_one, mass_one, weighted_one, diagonal_one = first
    peak_two, total_two, top_two, mass_two, weighted_two, diagonal_two = second
    peak = jnp.maximum(peak_one, peak_two)
    total = total_one * jnp.exp(peak_one - peak) + total_two * jnp.exp(peak_two - peak)
    top = jnp.maximum(top_one, top_two)
    factor_one = jnp.exp(top_one - top)
    factor_two = jnp.exp(top_two - top)
    mass = mass_one * factor_one + mass_two * factor_two
    weighted = weighted_one * factor_one + weighted_two * factor_two
    return (peak, total, top, mass, weighted, diagonal_one + diagonal_two)


def identity_of(count):
    lowest = jnp.full((count,), floor_value, jnp.float32)
    empty = jnp.zeros((count,), jnp.float32)
    return (lowest, empty, lowest, empty, empty, empty)


def take(stats, start, count):
    return tuple((lax.dynamic_slice_in_dim(value, start, count, 0) for value in stats))


def finish(stats):
    peak, total, top, mass, weighted, diagonal = stats
    return peak + jnp.log(total) - (1.0 - mixing) * diagonal - mixing * weighted / mass


def shards(image_student, text_student, image_teacher, text_teacher):
    shard = image_student.shape[0]
    text_devs = lax.axis_size("txt")
    image_devs = lax.axis_size("img")
    img_place = lax.axis_index("img")
    txt_place = lax.axis_index("txt")
    row_count = shard * text_devs
    rows = (
        lax.all_gather(image_student, "txt", axis=0, tiled=True),
        lax.all_gather(image_teacher, "txt", axis=0, tiled=True),
        lax.all_gather(text_teacher, "txt", axis=0, tiled=True),
    )
    row_index = img_place * row_count + jnp.arange(row_count, dtype=jnp.int32)
    piece = (
        lax.all_gather(text_student, "img", axis=0, tiled=True),
        lax.all_gather(image_teacher, "img", axis=0, tiled=True),
        lax.all_gather(text_teacher, "img", axis=0, tiled=True),
    )
    running = identity_of(row_count)
    offsets = jnp.arange(piece[0].shape[0], dtype=jnp.int32)
    along_rows, along_cols = tile_stats(
        rows, row_index, piece, (offsets // shard * text_devs + txt_place) * shard + offsets % shard
    )
    placed = tuple((part for part in along_cols))
    row_stats = combine(running, along_rows)
    row_all = joined(row_stats, "txt", combine)
    column_all = joined(placed, "img", combine)
    row_own = take(row_all, txt_place * shard, shard)
    column_own = take(column_all, img_place * shard, shard)
    image_loss = finish(row_own)
    text_loss = finish(column_own)
    overall = lax.psum(jnp.sum(image_loss) + jnp.sum(text_loss), ("img", "txt"))
    mean_loss = overall / (2.0 * shard * text_devs * image_devs)
    return (image_loss, text_loss, mean_loss)


def solution(mesh):
    return jax.shard_map(
        shards,
        mesh=mesh,
        in_specs=(
            P(("img", "txt"), None),
            P(("img", "txt"), None),
            P(("img", "txt"), None),
            P(("img", "txt"), None),
        ),
        out_specs=(P(("img", "txt")), P(("img", "txt")), P()),
        check_vma=False,
    )
```

profile of v0, /device:TPU:1, one launch (start us, length us, event | category | flops | bytes accessed | tf_op | source)
XLA Modules:
  0.0 931.7 jit_solution(17193611926347844069)
XLA Ops:
  7.2 0.7 all-gather.25.cloned.1.call-update
  7.9 0.7 all-gather.31.cloned.1.call-update
  8.7 0.7 all-gather.33.cloned.1.call-update
  9.4 0.5 all-gather.27.cloned.1.call-update
  10.0 0.0 all-gather.29.cloned.1.call-start
  10.0 0.5 all-gather.29.cloned.1.call-update
  10.6 38.2 %all_gather.80 = bf16[768,512]{1,0:T(8,128)(2,1)S(1)} all-gather(bf16[48,512]{1,0:T(8,128)(2,1)} %param.8), channel_id=1, replica_groups=mesh['img'=32,'txt'=16] {'txt'}, dimensions={0}, use_global_device_ids=true | all-gather | bytes 835584 | tf_op jit(solution)/shard_map/all_gather | solution.py:88
  48.8 52.6 %all-gather.25.cloned.1.call-done = bf16[1536,512]{1,0:T(8,128)(2,1)} async-done(((bf16[48,512]{1,0:T(8,128)(2,1)}), bf16[1536,512]{1,0:T(8,128)(2,1)}) %all-gather.25.cloned.1.call-update) | async-done | bytes 1572880 | tf_op jit(solution)/shard_map/all_gather | solution.py:94
  101.4 5.0 fusion.16
  106.3 38.7 %all-gather.13 = f32[32,1,1536]{2,1,0:T(1,128)S(1)} all-gather(f32[1,1,1536]{2,1,0:T(1,128)S(1)} %reshape.154), channel_id=3, replica_groups=mesh['img'=32,'txt'=16] {'img'}, dimensions={0}, use_global_device_ids=true | all-gather | bytes 202752 | tf_op jit(solution)/shard_map/all_gather | solution.py:13
  145.1 17.3 %all-gather.31.cloned.1.call-done = bf16[768,768]{1,0:T(8,128)(2,1)} async-done(((bf16[48,768]{1,0:T(8,128)(2,1)}), bf16[768,768]{1,0:T(8,128)(2,1)}) %all-gather.31.cloned.1.call-update) | async-done | bytes 1179664 | tf_op jit(solution)/shard_map/all_gather | solution.py:90
  162.4 99.6 %all-gather.33.cloned.1.call-done = bf16[1536,768]{1,0:T(8,128)(2,1)} async-done(((bf16[48,768]{1,0:T(8,128)(2,1)}), bf16[1536,768]{1,0:T(8,128)(2,1)}) %all-gather.33.cloned.1.call-update) | async-done | bytes 2359312 | tf_op jit(solution)/shard_map/all_gather | solution.py:96
  262.0 6.3 fusion.19
  268.3 54.6 %all-gather.27.cloned.1.call-done = bf16[768,768]{1,0:T(8,128)(2,1)} async-done(((bf16[48,768]{1,0:T(8,128)(2,1)}), bf16[768,768]{1,0:T(8,128)(2,1)}) %all-gather.27.cloned.1.call-update) | async-done | bytes 1179664 | tf_op jit(solution)/shard_map/all_gather | solution.py:89
  322.9 99.9 %all-gather.29.cloned.1.call-done = bf16[1536,768]{1,0:T(8,128)(2,1)} async-done(((bf16[48,768]{1,0:T(8,128)(2,1)}), bf16[1536,768]{1,0:T(8,128)(2,1)}) %all-gather.29.cloned.1.call-update) | async-done | bytes 2359312 | tf_op jit(solution)/shard_map/all_gather | solution.py:95
  422.8 4.4 fusion.20
  427.2 6.5 multiply_reduce_fusion
  433.8 26.7 %all-gather.11 = f32[16,1,768]{2,1,0:T(1,128)S(1)} all-gather(f32[1,1,768]{2,1,0:T(1,128)S(1)} %get-tuple-element.721), channel_id=1, replica_groups=mesh['img'=32,'txt'=16] {'txt'}, dimensions={0}, use_global_device_ids=true | all-gather | bytes 52224 | tf_op jit(solution)/shard_map/all_gather | solution.py:13
  460.5 22.8 %all-gather.10 = f32[16,1,768]{2,1,0:T(1,128)S(1)} all-gather(f32[1,1,768]{2,1,0:T(1,128)S(1)} %get-tuple-element.722), channel_id=1, replica_groups=mesh['img'=32,'txt'=16] {'txt'}, dimensions={0}, use_global_device_ids=true | all-gather | bytes 52224 | tf_op jit(solution)/shard_map/all_gather | solution.py:13
  483.3 24.5 %all-gather.9 = f32[16,1,768]{2,1,0:T(1,128)S(1)} all-gather(f32[1,1,768]{2,1,0:T(1,128)S(1)} %get-tuple-element.723), channel_id=1, replica_groups=mesh['img'=32,'txt'=16] {'txt'}, dimensions={0}, use_global_device_ids=true | all-gather | bytes 52224 | tf_op jit(solution)/shard_map/all_gather | solution.py:13
  507.9 23.1 %all-gather.8 = f32[16,1,768]{2,1,0:T(1,128)S(1)} all-gather(f32[1,1,768]{2,1,0:T(1,128)S(1)} %get-tuple-element.724), channel_id=1, replica_groups=mesh['img'=32,'txt'=16] {'txt'}, dimensions={0}, use_global_device_ids=true | all-gather | bytes 52224 | tf_op jit(solution)/shard_map/all_gather | solution.py:13
  531.0 24.4 %all-gather.7 = f32[16,1,768]{2,1,0:T(1,128)S(1)} all-gather(f32[1,1,768]{2,1,0:T(1,128)S(1)} %get-tuple-element.725), channel_id=1, replica_groups=mesh['img'=32,'txt'=16] {'txt'}, dimensions={0}, use_global_device_ids=true | all-gather | bytes 52224 | tf_op jit(solution)/shard_map/all_gather | solution.py:13
  555.4 22.8 %all-gather.12 = f32[16,1,768]{2,1,0:T(1,128)S(1)} all-gather(f32[1,1,768]{2,1,0:T(1,128)S(1)} %reshape.152), channel_id=2, replica_groups=mesh['img'=32,'txt'=16] {'txt'}, dimensions={0}, use_global_device_ids=true | all-gather | bytes 52224 | tf_op jit(solution)/shard_map/all_gather | solution.py:13
  578.3 82.5 %all-gather.18 = f32[32,1,1536]{2,1,0:T(1,128)S(1)} all-gather(f32[1,1,1536]{2,1,0:T(1,128)S(1)} %reshape.164), channel_id=8, replica_groups=mesh['img'=32,'txt'=16] {'img'}, dimensions={0}, use_global_device_ids=true | all-gather | bytes 202752 | tf_op jit(solution)/shard_map/all_gather | solution.py:13
  660.8 37.2 %all-gather.17 = f32[32,1,1536]{2,1,0:T(1,128)S(1)} all-gather(f32[1,1,1536]{2,1,0:T(1,128)S(1)} %reshape.162), channel_id=7, replica_groups=mesh['img'=32,'txt'=16] {'img'}, dimensions={0}, use_global_device_ids=true | all-gather | bytes 202752 | tf_op jit(solution)/shard_map/all_gather | solution.py:13
  698.1 38.6 %all-gather.16 = f32[32,1,1536]{2,1,0:T(1,128)S(1)} all-gather(f32[1,1,1536]{2,1,0:T(1,128)S(1)} %reshape.160), channel_id=6, replica_groups=mesh['img'=32,'txt'=16] {'img'}, dimensions={0}, use_global_device_ids=true | all-gather | bytes 202752 | tf_op jit(solution)/shard_map/all_gather | solution.py:13
  736.8 37.2 %all-gather.14 = f32[32,1,1536]{2,1,0:T(1,128)S(1)} all-gather(f32[1,1,1536]{2,1,0:T(1,128)S(1)} %reshape.156), channel_id=4, replica_groups=mesh['img'=32,'txt'=16] {'img'}, dimensions={0}, use_global_device_ids=true | all-gather | bytes 202752 | tf_op jit(solution)/shard_map/all_gather | solution.py:13
  774.1 38.6 %all-gather.15 = f32[32,1,1536]{2,1,0:T(1,128)S(1)} all-gather(f32[1,1,1536]{2,1,0:T(1,128)S(1)} %reshape.158), channel_id=5, replica_groups=mesh['img'=32,'txt'=16] {'img'}, dimensions={0}, use_global_device_ids=true | all-gather | bytes 202752 | tf_op jit(solution)/shard_map/all_gather | solution.py:13
  812.7 3.6 while.50
  816.3 9.1 while.51
  825.4 1.3 fusion.17
  828.1 95.3 %psum.7 = f32[]{:T(128)} all-reduce(f32[]{:T(128)S(6)} %add.266), channel_id=1, replica_groups=mesh['img'=32,'txt'=16] {'img','txt'}, use_global_device_ids=true, to_apply=%region_18.19 | all-reduce | flops 1 | bytes 8 | tf_op jit(solution)/shard_map/psum | solution.py:111
  (455 shorter events, 9.3 us)
Async XLA Ops:
  7.2 94.2 %all-gather.25.cloned.1.call-start = ((), (), s32[]{:S(2)}) async-start(), calls=%async_computation | async-start | bytes 1622016 | tf_op jit(solution)/shard_map/all_gather | solution.py:94
  7.9 154.5 %all-gather.31.cloned.1.call-start = ((), (), s32[]{:S(2)}) async-start(), calls=%async_computation.3 | async-start | bytes 1253376 | tf_op jit(solution)/shard_map/all_gather | solution.py:90
  8.6 253.3 %all-gather.33.cloned.1.call-start = ((), (), s32[]{:S(2)}) async-start(), calls=%async_computation.4 | async-start | bytes 2433024 | tf_op jit(solution)/shard_map/all_gather | solution.py:96
  9.4 313.5 %all-gather.27.cloned.1.call-start = ((), (), s32[]{:S(2)}) async-start(), calls=%async_computation.1 | async-start | bytes 1253376 | tf_op jit(solution)/shard_map/all_gather | solution.py:89
  10.0 412.8 %all-gather.29.cloned.1.call-start = ((), (), s32[]{:S(2)}) async-start(), calls=%async_computation.2 | async-start | bytes 2433024 | tf_op jit(solution)/shard_map/all_gather | solution.py:95
  422.8 4.4 copy-start
Sparse Core Ops, SparseCore 0:
  11.3 89.9 all-gather.24
  103.4 58.9 all-gather.30
  165.8 96.1 all-gather.32
  263.9 58.9 all-gather.26
  326.1 96.6 all-gather.28
where the time goes:
time: 932 us
  blocking collectives  551 us (59%)
  waiting for transfers between devices  327 us (35%)
  between operations  17.1 us (2%)
  matrix products  15.7 us (2%)
  other arithmetic  9.47 us (1%)
    all_gather x12, blocking collectives, joined(): everything = jax.tree.map(lambda part: lax.all_gather(part, axis), x)  417 us
    all_gather x1, waiting for transfers between devices, shards(): lax.all_gather(image_teacher, 'img', axis=0, tiled=True)  99.9 us
    all_gather x1, waiting for transfers between devices, shards(): lax.all_gather(text_teacher, 'img', axis=0, tiled=True)  99.6 us
    psum x1, blocking collectives, shards(): overall = lax.psum(jnp.sum(image_loss) + jnp.sum(text_loss), ('img', 'txt'))  95.3 us
    all_gather x1, waiting for transfers between devices, shards(): lax.all_gather(image_teacher, 'txt', axis=0, tiled=True)  54.6 us
    all_gather x1, waiting for transfers between devices, shards(): lax.all_gather(text_student, 'img', axis=0, tiled=True)  52.6 us
    all_gather x1, blocking collectives, shards(): lax.all_gather(image_student, 'txt', axis=0, tiled=True)  38.2 us
  transfers between devices with their start and end apart: 5, of which 5 were waited for; matrix products, arithmetic and copies ran while one was open for 1% of the time, Pallas kernels for 0%

commit v1 on v0

v1 whole, which is shorter than its diff:
```python
import functools
import math

import jax
import jax.numpy as jnp
from jax import lax
from jax.experimental import pallas as pl
from jax.experimental.pallas import tpu as pltpu
from jax.sharding import PartitionSpec as P

AXES = ("img", "txt")
LOG2E = 1.0 / math.log(2.0)
LOW = -1e30
SHARD = 48
BLOCK = 64
CHUNK = 256


def place(x, y, z, c):
    return (((x // 2) * 8 + y) * 2 + c) * 16 + z * 2 + x % 2


def everywhere():
    return [
        (x, y, z, c) for x in range(4) for y in range(8) for z in range(8) for c in range(2)
    ]


CORE_PAIRS = [(place(x, y, z, c), place(x, y, z, 1 - c)) for x, y, z, c in everywhere()]
X_PAIRS = [
    (place(x, y, z, c), place(x ^ 1 if c == 0 else 3 - x, y, z, c)) for x, y, z, c in everywhere()
]
LINES = [[place(x, y, z, 0) for z in range(8)] for x in range(4) for y in range(8)] + [
    [place(x, y, z, 1) for y in range(8)] for x in range(4) for z in range(8)
]
ROW_GROUPS = [
    [place(x, y, z, c) for z in range(8) for x in pair]
    for pair in ((0, 1), (3, 2))
    for y in range(8)
    for c in range(2)
]
COLUMN_GROUPS = [
    [place(x, y, z, c) for y in range(8) for x in pair for c in range(2)]
    for pair in ((0, 3), (1, 2))
    for z in range(8)
]


def dot(left, right):
    return lax.dot_general(
        left, right, (((1,), (1,)), ((), ())), preferred_element_type=jnp.float32
    )


def tile_kernel(ds, dt, own, other, row_out, col_out, a, b, l, g, h, ml, mg, colbuf, rowbuf, asem, bsem):
    rows, cols = a.shape[0], b.shape[0]
    chunks = cols // CHUNK
    blocks = rows // BLOCK
    img = lax.axis_index("img")
    txt = lax.axis_index("txt")
    core = img % 2
    y = (img // 2) % 8
    x_hi = img // 16
    x_lo = txt % 2
    z = txt // 2
    kl = 2.0 / math.sqrt(ds) * LOG2E
    kt = 3.0 / math.sqrt(dt) * LOG2E

    def copies(row_src, col_src, c):
        out = []
        for k in range(rows // SHARD):
            out.append(
                pltpu.make_async_copy(
                    row_src.at[k, c], a.at[pl.ds(k * SHARD, SHARD)], asem.at[k]
                )
            )
        for j in range(chunks):
            out.append(
                pltpu.make_async_copy(
                    col_src.at[pl.ds(j * CHUNK, CHUNK)], b.at[pl.ds(j * CHUNK, CHUNK)], bsem.at[j]
                )
            )
        return out

    flat_own = own.reshape(cols, own.shape[-1])
    flat_other = other.reshape(cols, own.shape[-1])

    @pl.when(core == 0)
    def _():
        for copy in copies(own, flat_other, 0):
            copy.start()

    @pl.when(core == 1)
    def _():
        for copy in copies(other, flat_own, 1):
            copy.start()

    ml[...] = jnp.full(ml.shape, LOW, jnp.float32)
    mg[...] = jnp.full(mg.shape, LOW, jnp.float32)
    waits = copies(own, flat_other, 0)
    for copy in waits[: rows // SHARD]:
        copy.wait()
    r0 = pl.multiple_of(z * (2 * SHARD), 2 * SHARD)
    c0 = y * (4 * SHARD) + (1 - core) * SHARD

    for j in range(chunks):
        waits[rows // SHARD + j].wait()
        span = pl.ds(j * CHUNK, CHUNK)
        l[j] = dot(a[:, :ds], b[span, :ds])
        g[j] = dot(a[:, ds : ds + dt], b[span, ds + dt :])
        h[...] = dot(a[:, ds + dt :], b[span, ds : ds + dt])

        @pl.when((c0 < (j + 1) * CHUNK) & (c0 + SHARD > j * CHUNK))
        def _():
            here = pl.ds(r0, SHARD)
            r = lax.broadcasted_iota(jnp.int32, (SHARD, CHUNK), 0)
            s = lax.broadcasted_iota(jnp.int32, (SHARD, CHUNK), 1) + (j * CHUNK - c0)
            same = r == s
            g[j, here, :] = jnp.where(same, LOW, g[j, here, :])
            h[here, :] = jnp.where(same, LOW, h[here, :])

        def peaks(i, so_far):
            cl, ch = so_far
            here = pl.ds(pl.multiple_of(i * BLOCK, BLOCK), BLOCK)
            lv = l[j, here, :]
            gv = g[j, here, :]
            hv = h[here, :]
            ml[here, :] = jnp.maximum(ml[here, :], jnp.maximum(lv[:, :128], lv[:, 128:]))
            mg[here, :] = jnp.maximum(mg[here, :], jnp.maximum(gv[:, :128], gv[:, 128:]))
            cl = jnp.maximum(cl, jnp.max(lv.reshape(BLOCK // 8, 8, CHUNK), axis=0))
            ch = jnp.maximum(ch, jnp.max(hv.reshape(BLOCK // 8, 8, CHUNK), axis=0))
            return cl, ch

        low = jnp.full((8, CHUNK), LOW, jnp.float32)
        cl, ch = lax.fori_loop(0, blocks, peaks, (low, low))
        cl = jnp.max(cl, axis=0, keepdims=True)
        ch = jnp.max(ch, axis=0, keepdims=True)

        def sums(i, so_far):
            total, mass, weighted = so_far
            here = pl.ds(pl.multiple_of(i * BLOCK, BLOCK), BLOCK)
            lv = l[j, here, :]
            el = jnp.exp2((lv - cl) * kl)
            eh = jnp.exp2((h[here, :] - ch) * kt)
            wh = eh * lv
            fold = lambda v: jnp.sum(v.reshape(BLOCK // 8, 8, CHUNK), axis=0)
            return total + fold(el), mass + fold(eh), weighted + fold(wh)

        zero = jnp.zeros((8, CHUNK), jnp.float32)
        total, mass, weighted = lax.fori_loop(0, blocks, sums, (zero, zero, zero))
        total = jnp.sum(total, axis=0, keepdims=True)
        mass = jnp.sum(mass, axis=0, keepdims=True)
        weighted = jnp.sum(weighted, axis=0, keepdims=True)
        colbuf[0:1, span] = cl * (kl / LOG2E) + jnp.log(total)
        colbuf[1:2, span] = ch * (kt / LOG2E) + jnp.log(mass)
        colbuf[2:3, span] = weighted / mass * (kl / LOG2E)

    lane = lax.broadcasted_iota(jnp.int32, (BLOCK, 128), 1)

    def along(i, _):
        here = pl.ds(pl.multiple_of(i * BLOCK, BLOCK), BLOCK)
        pl_ = jnp.max(ml[here, :], axis=1, keepdims=True)
        pg = jnp.max(mg[here, :], axis=1, keepdims=True)
        total = jnp.zeros((BLOCK, 128), jnp.float32)
        mass = jnp.zeros((BLOCK, 128), jnp.float32)
        weighted = jnp.zeros((BLOCK, 128), jnp.float32)
        for j in range(chunks):
            for q in range(CHUNK // 128):
                lanes = pl.ds(q * 128, 128)
                lv = l[j, here, lanes]
                total += jnp.exp2((lv - pl_) * kl)
                eg = jnp.exp2((g[j, here, lanes] - pg) * kt)
                mass += eg
                weighted += eg * lv
        total = jnp.sum(total, axis=1, keepdims=True)
        mass = jnp.sum(mass, axis=1, keepdims=True)
        weighted = jnp.sum(weighted, axis=1, keepdims=True)
        one = pl_ * (kl / LOG2E) + jnp.log(total)
        two = pg * (kt / LOG2E) + jnp.log(mass)
        three = weighted / mass * (kl / LOG2E)
        rowbuf[here, :] = jnp.where(lane == 0, one, jnp.where(lane == 1, two, three))
        return 0

    lax.fori_loop(0, blocks, along, 0)

    xi_row = x_lo ^ x_hi
    xi_col = x_hi
    for k in range(rows // SHARD):
        piece = rowbuf[k * SHARD : (k + 1) * SHARD, :]
        turned = jnp.swapaxes(piece, 0, 1)[:8, :]
        row_out[(k // 2) * 2 + (xi_row ^ (k % 2))] = turned
    for k in range(cols // SHARD):
        rel, other_core = (k // 2) % 2, k % 2
        col_out[(k // 4) * 4 + 2 * (xi_col ^ rel) + (1 - other_core)] = colbuf[
            :, k * SHARD : (k + 1) * SHARD
        ]


def tile(own, other, ds, dt):
    width = own.shape[-1]
    rows, cols = 16 * SHARD, 32 * SHARD
    chunks = cols // CHUNK
    return pl.pallas_call(
        functools.partial(tile_kernel, ds, dt),
        out_shape=(
            jax.ShapeDtypeStruct((rows // SHARD, 8, SHARD), jnp.float32),
            jax.ShapeDtypeStruct((cols // SHARD, 8, SHARD), jnp.float32),
        ),
        in_specs=[pl.BlockSpec(memory_space=pl.ANY)] * 2,
        out_specs=[pl.BlockSpec(memory_space=pltpu.VMEM)] * 2,
        scratch_shapes=[
            pltpu.VMEM((rows, width), jnp.bfloat16),
            pltpu.VMEM((cols, width), jnp.bfloat16),
            pltpu.VMEM((chunks, rows, CHUNK), jnp.float32),
            pltpu.VMEM((chunks, rows, CHUNK), jnp.float32),
            pltpu.VMEM((rows, CHUNK), jnp.float32),
            pltpu.VMEM((rows, 128), jnp.float32),
            pltpu.VMEM((rows, 128), jnp.float32),
            pltpu.VMEM((8, cols), jnp.float32),
            pltpu.VMEM((rows, 128), jnp.float32),
            pltpu.SemaphoreType.DMA((rows // SHARD,)),
            pltpu.SemaphoreType.DMA((chunks,)),
        ],
        compiler_params=pltpu.CompilerParams(vmem_limit_bytes=40 * 1024 * 1024),
        cost_estimate=pl.CostEstimate(
            flops=2 * rows * cols * width, bytes_accessed=2 * (rows + cols) * width, transcendentals=4 * rows * cols
        ),
    )(own, other)


def joined(parts):
    lse, mark, mean = parts[:, 0], parts[:, 1], parts[:, 2]
    peak = jnp.max(lse, axis=0)
    spread = peak + jnp.log(jnp.sum(jnp.exp(lse - peak), axis=0))
    weight = jnp.exp(mark - jnp.max(mark, axis=0))
    return spread, jnp.sum(weight * mean, axis=0) / jnp.sum(weight, axis=0)


def shared_sum(value, groups):
    count = len(groups[0])
    sent = jnp.full((count, 1, 128), value)
    return jnp.sum(lax.all_to_all(sent, AXES, 0, 0, axis_index_groups=groups)[:, 0, 0])


def shards(image_student, text_student, image_teacher, text_teacher):
    ds, dt = image_student.shape[1], image_teacher.shape[1]
    core = lax.axis_index("img") % 2
    image_side = jnp.concatenate([image_student, image_teacher, text_teacher], axis=1)
    text_side = jnp.concatenate([text_student, text_teacher, image_teacher], axis=1)
    mine = jnp.where(core == 0, image_side, text_side)
    theirs = jnp.where(core == 0, text_side, image_side)
    chip = jnp.concatenate([mine, lax.ppermute(theirs, AXES, CORE_PAIRS)], axis=0)
    pair = jnp.concatenate([chip, lax.ppermute(chip, AXES, X_PAIRS)], axis=0)
    line = lax.all_gather(pair, AXES, axis=0, tiled=True, axis_index_groups=LINES)
    other = lax.ppermute(line, AXES, CORE_PAIRS)
    shape = (16, 2, SHARD, line.shape[1])
    row_stats, col_stats = tile(line.reshape(shape), other.reshape(shape), ds, dt)
    row_parts = lax.all_to_all(row_stats, AXES, 0, 0, axis_index_groups=ROW_GROUPS)
    col_parts = lax.all_to_all(col_stats, AXES, 0, 0, axis_index_groups=COLUMN_GROUPS)
    diagonal = jnp.sum(
        image_student.astype(jnp.float32) * text_student.astype(jnp.float32), axis=1
    ) * (2.0 / math.sqrt(ds))
    image_spread, image_soft = joined(row_parts)
    text_spread, text_soft = joined(col_parts)
    image_loss = image_spread - 0.5 * diagonal - 0.5 * image_soft
    text_loss = text_spread - 0.5 * diagonal - 0.5 * text_soft
    overall = jnp.sum(image_loss) + jnp.sum(text_loss)
    overall = shared_sum(shared_sum(overall, COLUMN_GROUPS), ROW_GROUPS)
    return image_loss, text_loss, overall / (2.0 * SHARD * 512)


def solution(mesh):
    spec = P(("img", "txt"), None)
    return jax.shard_map(
        shards,
        mesh=mesh,
        in_specs=(spec, spec, spec, spec),
        out_specs=(P(("img", "txt")), P(("img", "txt")), P()),
        check_vma=False,
    )
```

time: 932 us -> 184 us (0.20)
  blocking collectives: 551 us -> 22.1 us
  waiting for transfers between devices: 327 us -> 80 us
  starting transfers between devices: 0.19 us -> 29.9 us
  Pallas kernels: 0 us -> 19.3 us
  matrix products: 15.7 us -> 0 us
    all_gather x13 -> x0, blocking collectives: 455 us -> none  [the longest x12 417 us: joined(): everything = jax.tree.map(lambda part: lax.all_gather(part, axis), x)]
    all_gather x5 -> x1, waiting for transfers between devices: 324 us -> 46.6 us  [shards(): lax.all_gather(pair, AXES, axis=0, tiled=True, axis_index_groups=LINES)]
    psum x1 -> x0, blocking collectives: 95.3 us -> none  [shards(): overall = lax.psum(jnp.sum(image_loss) + jnp.sum(text_loss), ('img', 'txt'))]
    all_to_all x0 -> x2, blocking collectives: none -> 22.1 us  [shared_sum(): lax.all_to_all(sent, AXES, 0, 0, axis_index_groups=groups)[:, 0, 0]]
    pallas_call x0 -> x1, Pallas kernels: none -> 19.3 us  [tile(): pl.pallas_call(functools.partial(tile_kernel, ds, dt), out_shape=(jax.Sha...]
    ppermute x0 -> x3, waiting for transfers between devices: none -> 18.8 us  [the longest x1 9.97 us: shards(): other = lax.ppermute(line, AXES, CORE_PAIRS)]
    dot_general x3 -> x0, matrix products: 15.7 us -> none  [contract(): lax.dot_general(left, right, (((1,), (1,)), ((), ())), preferred_element_...]
    all_to_all x0 -> x2, starting transfers between devices: none -> 15.2 us  [the longest x1 9.03 us: shards(): lax.all_to_all(col_stats, AXES, 0, 0, axis_index_groups=COLUMN_GROUPS)]
  transfers between devices with their start and end apart: 5 -> 6, of which waited for: 5 -> 6; matrix products, arithmetic and copies ran while one was open for 1% -> 1% of each run, Pallas kernels for 0% -> 0%
where the time goes in v1:
time: 184 us
  waiting for transfers between devices  80 us (43%)
  starting transfers between devices  29.9 us (16%)
  blocking collectives  22.1 us (12%)
  Pallas kernels  19.3 us (10%)
  between operations  17.3 us (9%)
  local copies, waits for them, and re-layouts  9.92 us (5%)
  other arithmetic  5.28 us (3%)
    all_gather x1, waiting for transfers between devices, shards(): lax.all_gather(pair, AXES, axis=0, tiled=True, axis_index_groups=LINES)  46.6 us
    all_to_all x2, blocking collectives, shared_sum(): lax.all_to_all(sent, AXES, 0, 0, axis_index_groups=groups)[:, 0, 0]  22.1 us
    pallas_call x1, Pallas kernels, tile(): pl.pallas_call(functools.partial(tile_kernel, ds, dt), out_shape=(jax.Sha...  19.3 us
    ppermute x1, waiting for transfers between devices, shards(): other = lax.ppermute(line, AXES, CORE_PAIRS)  9.97 us
    all_to_all x1, starting transfers between devices, shards(): lax.all_to_all(col_stats, AXES, 0, 0, axis_index_groups=COLUMN_GROUPS)  9.03 us
    ppermute x1, starting transfers between devices, shards(): lax.ppermute(theirs, AXES, CORE_PAIRS)  8.79 us
    all_to_all x1, waiting for transfers between devices, shards(): lax.all_to_all(col_stats, AXES, 0, 0, axis_index_groups=COLUMN_GROUPS)  7.95 us
    ppermute x1, waiting for transfers between devices, shards(): pair = jnp.concatenate([chip, lax.ppermute(chip, AXES, X_PAIRS)], axis=0)  7.8 us
  transfers between devices with their start and end apart: 6, of which 6 were waited for; matrix products, arithmetic and copies ran while one was open for 1% of the time, Pallas kernels for 0%

profile of v1, /device:TPU:1, one launch (start us, length us, event | category | flops | bytes accessed | tf_op | source)
XLA Modules:
  0.0 183.8 jit_solution(13247900980714403854)
XLA Ops:
  7.2 0.8 constant_dynamic-update-slice_fusion.2
  8.0 0.8 constant_dynamic-update-slice_fusion.5
  8.8 0.9 constant_dynamic-update-slice_fusion.1
  9.7 0.9 constant_dynamic-update-slice_fusion
  10.6 0.9 constant_dynamic-update-slice_fusion.3
  11.5 8.8 %collective-permute-start = (bf16[48,2048]{1,0:T(8,128)(2,1)S(1)}, bf16[48,2048]{1,0:T(8,128)(2,1)S(1)}, u32[]{:S(2)}, u32[]{:S(2)}) collective-permute-start(bf16[48,2048]{1,0:T(8,128)(2,1)S(1)} %get-tuple-element.16), channel_id=1, source_target_pairs={{0,16},{16,0},{2,18},{18,2},{4,20},{20,4},{6,22},{22,6},{8,24},{24... | collective-permute-start | bytes 589832 | tf_op jit(solution)/shard_map/ppermute | solution.py:252
  20.3 1.0 collective-permute-done
  21.4 1.9 %collective-permute-start.1 = (bf16[96,2048]{1,0:T(8,128)(2,1)S(1)}, bf16[96,2048]{1,0:T(8,128)(2,1)S(1)}, u32[]{:S(2)}, u32[]{:S(2)}) collective-permute-start(bf16[96,2048]{1,0:T(8,128)(2,1)S(1)} %pad_maximum_fusion.1), channel_id=1, source_target_pairs={{0,1},{16,273},{2,3},{18,275},{4,5},{20,277},{6,7},{22,279},{8,9},... | collective-permute-start | bytes 1179656 | tf_op jit(solution)/shard_map/ppermute | solution.py:253
  23.3 7.8 %collective-permute-done.1 = bf16[96,2048]{1,0:T(8,128)(2,1)S(1)} collective-permute-done((bf16[96,2048]{1,0:T(8,128)(2,1)S(1)}, bf16[96,2048]{1,0:T(8,128)(2,1)S(1)}, u32[]{:S(2)}, u32[]{:S(2)}) %collective-permute-start.1) | collective-permute-done | bytes 393248 | tf_op jit(solution)/shard_map/ppermute | solution.py:253
  31.1 0.9 pad_maximum_fusion
  32.1 46.6 %all-gather.2.cloned.1.call-done = bf16[1536,2048]{1,0:T(8,128)(2,1)} async-done(((bf16[192,2048]{1,0:T(8,128)(2,1)}), bf16[1536,2048]{1,0:T(8,128)(2,1)}) %all-gather.2.cloned.1.call-update) | async-done | bytes 6291472 | tf_op jit(solution)/shard_map/all_gather | solution.py:254
  78.7 3.9 %collective-permute-start.2 = (bf16[1536,2048]{1,0:T(8,128)(2,1)}, bf16[1536,2048]{1,0:T(8,128)(2,1)S(1)}, u32[]{:S(2)}, u32[]{:S(2)}) collective-permute-start(bf16[1536,2048]{1,0:T(8,128)(2,1)} %all-gather.2.cloned.1.call-done), channel_id=1, source_target_pairs={{0,16},{16,0},{2,18},{18,2},{4,20},{20,4},{6,22},{22,6},{8,24},{24... | collective-permute-start | bytes 18874376 | tf_op jit(solution)/shard_map/ppermute | solution.py:255
  82.6 10.0 %collective-permute-done.2 = bf16[1536,2048]{1,0:T(8,128)(2,1)S(1)} collective-permute-done((bf16[1536,2048]{1,0:T(8,128)(2,1)}, bf16[1536,2048]{1,0:T(8,128)(2,1)S(1)}, u32[]{:S(2)}, u32[]{:S(2)}) %collective-permute-start.2) | collective-permute-done | bytes 6291488 | tf_op jit(solution)/shard_map/ppermute | solution.py:255
  92.6 2.8 %copy-done = bf16[1536,2048]{1,0:T(8,128)(2,1)S(1)} copy-done((bf16[1536,2048]{1,0:T(8,128)(2,1)S(1)}, bf16[1536,2048]{1,0:T(8,128)(2,1)}, u32[]{:S(2)}) %copy-start) | copy-done | bytes 6291480
  95.4 19.3 %shard_map.67 = (f32[16,8,48]{2,1,0:T(8,128)S(1)}, f32[32,8,48]{2,1,0:T(8,128)S(1)}) custom-call(bf16[16,2,48,2048]{3,2,1,0:T(8,128)(2,1)S(1)} %bitcast.12, bf16[16,2,48,2048]{3,2,1,0:T(8,128)(2,1)S(1)} %bitcast.13), custom_call_target="tpu_custom_call" | custom-call | flops 4831838208 | bytes 9437184 | tf_op jit(solution)/shard_map/pallas_call | solution.py:203
  114.7 0.7 reshape.18
  115.4 6.2 %all-to-all-start = ((f32[16,1,384]{2,1,0:T(1,128)}), f32[16,1,384]{2,1,0:T(1,128)S(1)}, u32[]{:S(2)}, u32[]{:S(2)}) async-start(f32[16,1,384]{2,1,0:T(1,128)} %reshape.18), calls=%async_computation | async-start | bytes 49152 | tf_op jit(solution)/shard_map/all_to_all | solution.py:258
  121.6 0.1 multiply_reduce_fusion
  121.8 0.8 reshape.20
  122.5 6.6 %all-to-all-done = f32[16,1,384]{2,1,0:T(1,128)S(1)} async-done(((f32[16,1,384]{2,1,0:T(1,128)}), f32[16,1,384]{2,1,0:T(1,128)S(1)}, u32[]{:S(2)}, u32[]{:S(2)}) %all-to-all-start) | async-done | bytes 24608 | tf_op jit(solution)/shard_map/all_to_all | solution.py:258
  129.2 9.0 %all-to-all-start.1 = ((f32[32,1,384]{2,1,0:T(1,128)}), f32[32,1,384]{2,1,0:T(1,128)S(1)}, u32[]{:S(2)}, u32[]{:S(2)}) async-start(f32[32,1,384]{2,1,0:T(1,128)} %reshape.20), calls=%async_computation.1 | async-start | bytes 98304 | tf_op jit(solution)/shard_map/all_to_all | solution.py:259
  138.2 0.5 broadcast.14
  138.7 0.7 reduce.7
  139.6 7.9 %all-to-all-done.1 = f32[32,1,384]{2,1,0:T(1,128)S(1)} async-done(((f32[32,1,384]{2,1,0:T(1,128)}), f32[32,1,384]{2,1,0:T(1,128)S(1)}, u32[]{:S(2)}, u32[]{:S(2)}) %all-to-all-start.1) | async-done | bytes 49184 | tf_op jit(solution)/shard_map/all_to_all | solution.py:259
  147.6 0.8 reduce.6
  148.3 0.1 reshape.21
  148.6 1.2 fusion.2
  151.1 12.2 %all_to_all.20 = f32[32,1,128]{2,1,0:T(1,128)S(1)} all-to-all(f32[32,1,128]{2,1,0:T(1,128)S(1)} %broadcast_in_dim.4), channel_id=1, replica_groups={{0,16,257,273,32,48,289,305,64,80,321,337,96,112,353,369,128,144,385,40..., dimensions={0} | all-to-all | bytes 32768 | tf_op jit(solution)/shard_map/all_to_all | solution.py:242
  163.4 0.6 slice_reduce_fusion
  164.0 0.6 broadcast_in_dim.5
  164.6 9.9 %all_to_all.21 = f32[16,1,128]{2,1,0:T(1,128)S(1)} all-to-all(f32[16,1,128]{2,1,0:T(1,128)S(1)} %broadcast_in_dim.5), channel_id=1, replica_groups={{0,1,2,3,4,5,6,7,8,9,10,11,12,13,14,15},{16,17,18,19,20,21,22,23,24,25,..., dimensions={0} | all-to-all | bytes 16384 | tf_op jit(solution)/shard_map/all_to_all | solution.py:242
  174.5 0.6 slice_reduce_fusion.1
  (19 shorter events, 0.5 us)
Async XLA Ops:
  7.2 71.6 %all-gather.2.cloned.1.call-start = ((), (), s32[]{:S(2)}) async-start(), calls=%async_computation.4 | async-start | bytes 7077888 | tf_op jit(solution)/shard_map/all_gather | solution.py:254
  11.5 9.8 %collective-permute-start = (bf16[48,2048]{1,0:T(8,128)(2,1)S(1)}, bf16[48,2048]{1,0:T(8,128)(2,1)S(1)}, u32[]{:S(2)}, u32[]{:S(2)}) collective-permute-start(bf16[48,2048]{1,0:T(8,128)(2,1)S(1)} %get-tuple-element.16), channel_id=1, source_target_pairs={{0,16},{16,0},{2,18},{18,2},{4,20},{20,4},{6,22},{22,6},{8,24},{24... | collective-permute-start | bytes 589832 | tf_op jit(solution)/shard_map/ppermute | solution.py:252
  21.4 9.7 %collective-permute-start.1 = (bf16[96,2048]{1,0:T(8,128)(2,1)S(1)}, bf16[96,2048]{1,0:T(8,128)(2,1)S(1)}, u32[]{:S(2)}, u32[]{:S(2)}) collective-permute-start(bf16[96,2048]{1,0:T(8,128)(2,1)S(1)} %pad_maximum_fusion.1), channel_id=1, source_target_pairs={{0,1},{16,273},{2,3},{18,275},{4,5},{20,277},{6,7},{22,279},{8,9},... | collective-permute-start | bytes 1179656 | tf_op jit(solution)/shard_map/ppermute | solution.py:253
  78.7 13.9 %collective-permute-start.2 = (bf16[1536,2048]{1,0:T(8,128)(2,1)}, bf16[1536,2048]{1,0:T(8,128)(2,1)S(1)}, u32[]{:S(2)}, u32[]{:S(2)}) collective-permute-start(bf16[1536,2048]{1,0:T(8,128)(2,1)} %all-gather.2.cloned.1.call-done), channel_id=1, source_target_pairs={{0,16},{16,0},{2,18},{18,2},{4,20},{20,4},{6,22},{22,6},{8,24},{24... | collective-permute-start | bytes 18874376 | tf_op jit(solution)/shard_map/ppermute | solution.py:255
  92.6 2.8 %copy-start = (bf16[1536,2048]{1,0:T(8,128)(2,1)S(1)}, bf16[1536,2048]{1,0:T(8,128)(2,1)}, u32[]{:S(2)}) copy-start(bf16[1536,2048]{1,0:T(8,128)(2,1)} %all-gather.2.cloned.1.call-done) | copy-start | bytes 18874372
  95.4 26.3 %copy-start.1 = (bf16[48,512]{1,0:T(8,128)(2,1)S(1)}, bf16[48,512]{1,0:T(8,128)(2,1)}, u32[]{:S(2)}) copy-start(bf16[48,512]{1,0:T(8,128)(2,1)} %param.4) | copy-start | bytes 147460
  95.4 26.3 %copy-start.2 = (bf16[48,512]{1,0:T(8,128)(2,1)S(1)}, bf16[48,512]{1,0:T(8,128)(2,1)}, u32[]{:S(2)}) copy-start(bf16[48,512]{1,0:T(8,128)(2,1)} %param.5) | copy-start | bytes 147460
  115.4 13.8 %all-to-all-start = ((f32[16,1,384]{2,1,0:T(1,128)}), f32[16,1,384]{2,1,0:T(1,128)S(1)}, u32[]{:S(2)}, u32[]{:S(2)}) async-start(f32[16,1,384]{2,1,0:T(1,128)} %reshape.18), calls=%async_computation | async-start | bytes 49152 | tf_op jit(solution)/shard_map/all_to_all | solution.py:258
  129.2 18.4 %all-to-all-start.1 = ((f32[32,1,384]{2,1,0:T(1,128)}), f32[32,1,384]{2,1,0:T(1,128)S(1)}, u32[]{:S(2)}, u32[]{:S(2)}) async-start(f32[32,1,384]{2,1,0:T(1,128)} %reshape.20), calls=%async_computation.1 | async-start | bytes 98304 | tf_op jit(solution)/shard_map/all_to_all | solution.py:259
Sparse Core Ops, SparseCore 0:
  32.2 46.4 all-gather.1

commit v2 on v0

v2 whole, which is shorter than its diff:
```python
import functools
import math

import jax
import jax.numpy as jnp
from jax import lax
from jax.experimental import pallas as pl
from jax.experimental.pallas import tpu as pltpu
from jax.sharding import PartitionSpec as P

AXES = ("img", "txt")
LOG2E = 1.0 / math.log(2.0)
LOW = -1e30
SHARD = 48
CHUNK = 256
BLOCK = 128


def place(x, y, z, c):
    return (((x // 2) * 8 + y) * 2 + c) * 16 + z * 2 + x % 2


def everywhere():
    return [
        (x, y, z, c) for x in range(4) for y in range(8) for z in range(8) for c in range(2)
    ]


ROW_X = ((0, 1), (3, 2))
COL_X = ((0, 3), (1, 2))
CORE_PAIRS = [(place(x, y, z, c), place(x, y, z, 1 - c)) for x, y, z, c in everywhere()]
X_PAIRS = [
    (place(x, y, z, c), place(x ^ 1 if c == 0 else 3 - x, y, z, c)) for x, y, z, c in everywhere()
]
UP, DOWN = (
    [
        (place(x, y, z, c), place(x, y, (z + s) % 8, c) if c == 0 else place(x, (y + s) % 8, z, c))
        for x, y, z, c in everywhere()
    ]
    for s in (1, -1)
)
STAT_GROUPS = [[place(x, y, z, 0) for z in range(8) for x in pair] for pair in ROW_X for y in range(8)] + [
    [place(x, y, z, 1) for y in range(8) for x in pair] for pair in COL_X for z in range(8)
]
SUM_GROUPS = [
    [place(pair[e], y, k, 0) for y in range(8) for pair in ROW_X]
    + [place(pair[e], k, z, 1) for z in range(8) for pair in COL_X]
    for k in range(8)
    for e in range(2)
]


def where_am_i():
    img = lax.axis_index("img")
    txt = lax.axis_index("txt")
    x_hi, x_lo = img // 16, txt % 2
    core = img % 2
    return jnp.where(core == 0, txt // 2, (img // 2) % 8), jnp.where(core == 0, x_hi ^ x_lo, x_hi)


def dot(left, right):
    return lax.dot_general(
        left, right, (((1,), (1,)), ((), ())), preferred_element_type=jnp.float32
    )


def pack_kernel(image_s, text_s, image_t, text_t, mine, theirs):
    ds, dt = image_s.shape[1], image_t.shape[1]
    core = lax.axis_index("img") % 2

    def fill(out, student, first, second):
        out[:, :ds] = student[...]
        out[:, ds : ds + dt] = first[...]
        out[:, ds + dt :] = second[...]

    @pl.when(core == 0)
    def _():
        fill(mine, image_s, image_t, text_t)
        fill(theirs, text_s, text_t, image_t)

    @pl.when(core == 1)
    def _():
        fill(mine, text_s, text_t, image_t)
        fill(theirs, image_s, image_t, text_t)


def pack(image_s, text_s, image_t, text_t):
    shape = jax.ShapeDtypeStruct((SHARD, image_s.shape[1] + 2 * image_t.shape[1]), jnp.bfloat16)
    vmem = pl.BlockSpec(memory_space=pltpu.VMEM)
    return pl.pallas_call(
        pack_kernel,
        out_shape=(shape, shape),
        in_specs=[vmem] * 4,
        out_specs=[vmem] * 2,
        compiler_params=pltpu.CompilerParams(vmem_limit_bytes=4 * 1024 * 1024),
    )(image_s, text_s, image_t, text_t)


def tile_kernel(ds, dt, units, *refs):
    own, other = refs[:units], refs[units : 2 * units]
    out, l, g, stats = refs[2 * units :]
    rows = 32 * SHARD
    chunks = rows // CHUNK
    line, xi = where_am_i()
    kl = 2.0 / math.sqrt(ds) * LOG2E
    kt = 3.0 / math.sqrt(dt) * LOG2E

    def piece(refs, start, stop, low, high):
        parts, at = [], 0
        for ref in refs:
            size = ref.shape[0]
            a, b = max(start - at, 0), min(stop - at, size)
            if a < b:
                parts.append(ref[a:b, low:high])
            at += size
        return jnp.concatenate(parts, axis=0) if len(parts) > 1 else parts[0]

    def products(j):
        n = j % 2
        a, b = j * CHUNK, (j + 1) * CHUNK
        l[n] = dot(piece(other, 0, rows, 0, ds), piece(own, a, b, 0, ds))
        g[n] = dot(piece(other, 0, rows, ds + dt, ds + 2 * dt), piece(own, a, b, ds, ds + dt))

    def summary(j):
        n = j % 2
        diagonal = jnp.zeros((1, CHUNK), jnp.float32)
        if j == 0:
            s = lax.broadcasted_iota(jnp.int32, (2 * SHARD, CHUNK), 0)
            r = lax.broadcasted_iota(jnp.int32, (2 * SHARD, CHUNK), 1)
            same = (r < 2 * SHARD) & (s == jnp.where(r < SHARD, r + SHARD, r - SHARD))
            g[n, : 2 * SHARD, :] = jnp.where(same, LOW, g[n, : 2 * SHARD, :])
            diagonal = jnp.sum(jnp.where(same, l[n, : 2 * SHARD, :], 0.0), axis=0, keepdims=True)
        blocks = [slice(i, i + BLOCK) for i in range(0, rows, BLOCK)]

        def eights(v):
            return v.reshape(BLOCK // 8, 8, CHUNK)

        pl_ = pg = jnp.full((8, CHUNK), LOW, jnp.float32)
        for here in blocks:
            pl_ = jnp.maximum(pl_, jnp.max(eights(l[n, here, :]), axis=0))
            pg = jnp.maximum(pg, jnp.max(eights(g[n, here, :]), axis=0))
        pl_ = jnp.max(pl_, axis=0, keepdims=True)
        pg = jnp.max(pg, axis=0, keepdims=True)
        total = mass = weighted = jnp.zeros((8, CHUNK), jnp.float32)
        for here in blocks:
            lv = l[n, here, :]
            e = jnp.exp2((g[n, here, :] - pg) * kt)
            total += jnp.sum(eights(jnp.exp2((lv - pl_) * kl)), axis=0)
            mass += jnp.sum(eights(e), axis=0)
            weighted += jnp.sum(eights(e * lv), axis=0)
        total = jnp.sum(total, axis=0, keepdims=True)
        mass = jnp.sum(mass, axis=0, keepdims=True)
        weighted = jnp.sum(weighted, axis=0, keepdims=True)
        to = slice(j * CHUNK, (j + 1) * CHUNK)
        stats[0:1, to] = pl_ * (kl / LOG2E) + jnp.log(total)
        stats[1:2, to] = pg * (kt / LOG2E) + jnp.log(mass)
        stats[2:3, to] = weighted / mass * (kl / LOG2E)
        stats[3:4, to] = diagonal * (kl / LOG2E)

    products(0)
    for j in range(1, chunks):
        products(j)
        summary(j - 1)
    summary(chunks - 1)

    for k, step in enumerate((0, 7, 1, 6, 2, 5, 3, 4)):
        v = stats[:4, k * 4 * SHARD : (k + 1) * 4 * SHARD]
        v = jnp.where(xi == 0, v, jnp.concatenate([v[:, 2 * SHARD :], v[:, : 2 * SHARD]], axis=1))
        row = pl.ds(lax.rem(line + step, 8), 1)
        for n in range(4):
            out[0, n, row, :] = v[n : n + 1, :128]
            out[0, 4 + n // 2, row, (n % 2) * 64 : (n % 2 + 1) * 64] = v[n : n + 1, 128:]
    for k in range(1, out.shape[0]):
        out[k] = out[0]


def tile(own, other, ds, dt):
    rows = 32 * SHARD
    vmem = pl.BlockSpec(memory_space=pltpu.VMEM)
    return pl.pallas_call(
        functools.partial(tile_kernel, ds, dt, len(own)),
        out_shape=jax.ShapeDtypeStruct((16, 6, 8, 128), jnp.float32),
        in_specs=[vmem] * (len(own) + len(other)),
        out_specs=vmem,
        scratch_shapes=[
            pltpu.VMEM((2, rows, CHUNK), jnp.float32),
            pltpu.VMEM((2, rows, CHUNK), jnp.float32),
            pltpu.VMEM((8, rows), jnp.float32),
        ],
        compiler_params=pltpu.CompilerParams(vmem_limit_bytes=24 * 1024 * 1024),
        cost_estimate=pl.CostEstimate(
            flops=2 * rows * rows * (ds + dt), bytes_accessed=8 * rows * (ds + dt), transcendentals=2 * rows * rows
        ),
    )(*own, *other)


def finish_kernel(parts, mine, total, held):
    line, xi = where_am_i()
    count = parts.shape[0]

    def losses(lse, mark, mean, diagonal):
        top, high = lse(0), mark(0)
        for k in range(1, count):
            top = jnp.maximum(top, lse(k))
            high = jnp.maximum(high, mark(k))
        spread = mass = weighted = own = jnp.zeros_like(top)
        for k in range(count):
            e = jnp.exp(mark(k) - high)
            spread += jnp.exp(lse(k) - top)
            mass += e
            weighted += e * mean(k)
            own += diagonal(k)
        return top + jnp.log(spread) - 0.5 * own - 0.5 * weighted / mass

    one = losses(*(lambda k, n=n: parts[k, n] for n in range(4)))
    two = losses(*(lambda k, n=n: parts[k, 4 + n // 2][:, (n % 2) * 64 : (n % 2 + 1) * 64] for n in range(4)))
    held[:, :128] = one
    held[:, 128:] = jnp.concatenate([two, two], axis=1)
    v = held[pl.ds(line, 1), :]
    mine[...] = jnp.where(xi == 0, v[:, :128], v[:, 2 * SHARD : 2 * SHARD + 128])
    total[...] = jnp.full(total.shape, jnp.sum(one) + jnp.sum(two), jnp.float32)


def finish(parts):
    vmem = pl.BlockSpec(memory_space=pltpu.VMEM)
    return pl.pallas_call(
        finish_kernel,
        out_shape=(
            jax.ShapeDtypeStruct((1, 128), jnp.float32),
            jax.ShapeDtypeStruct((32, 1, 128), jnp.float32),
        ),
        in_specs=[vmem],
        out_specs=[vmem] * 2,
        scratch_shapes=[pltpu.VMEM((8, 256), jnp.float32)],
        compiler_params=pltpu.CompilerParams(vmem_limit_bytes=4 * 1024 * 1024),
    )(parts)


def shards(image_student, text_student, image_teacher, text_teacher):
    ds, dt = image_student.shape[1], image_teacher.shape[1]
    core = lax.axis_index("img") % 2

    def swap(v):
        return lax.ppermute(v, AXES, CORE_PAIRS)

    mine, theirs = pack(image_student, text_student, image_teacher, text_teacher)
    chip = jnp.concatenate([mine, swap(theirs)], axis=0)
    pair = jnp.concatenate([chip, lax.ppermute(chip, AXES, X_PAIRS)], axis=0)
    own, other = [pair], [swap(pair)]
    up = down = pair
    for _ in range(3):
        up, down = lax.ppermute(up, AXES, UP), lax.ppermute(down, AXES, DOWN)
        own += [up, down]
        other += [swap(up), swap(down)]
    half = pair.shape[0] // 2
    up, down = lax.ppermute(up[:half], AXES, UP), lax.ppermute(down[half:], AXES, DOWN)
    own += [up, down]
    other += [swap(up), swap(down)]
    stats = tile(own, other, ds, dt)
    parts = lax.all_to_all(stats, AXES, 0, 0, axis_index_groups=STAT_GROUPS)
    losses, total = finish(parts)
    first, second = losses[0, :SHARD], swap(losses)[0, SHARD : 2 * SHARD]
    image_loss = jnp.where(core == 0, first, second)
    text_loss = jnp.where(core == 0, second, first)
    totals = lax.all_to_all(total, AXES, 0, 0, axis_index_groups=SUM_GROUPS)
    return image_loss, text_loss, jnp.sum(totals[:, 0, 0]) / (2.0 * SHARD * 512)


def solution(mesh):
    spec = P(("img", "txt"), None)
    return jax.shard_map(
        shards,
        mesh=mesh,
        in_specs=(spec, spec, spec, spec),
        out_specs=(P(("img", "txt")), P(("img", "txt")), P()),
        check_vma=False,
    )
```

time: 932 us -> 143 us (0.15)
  blocking collectives: 551 us -> 0 us
  waiting for transfers between devices: 327 us -> 46.4 us
  starting transfers between devices: 0.19 us -> 77 us
  matrix products: 15.7 us -> 0 us
  between operations: 17.1 us -> 2.76 us
  Pallas kernels: 0 us -> 11.6 us
    all_gather x13 -> x0, blocking collectives: 455 us -> none  [the longest x12 417 us: joined(): everything = jax.tree.map(lambda part: lax.all_gather(part, axis), x)]
    all_gather x5 -> x0, waiting for transfers between devices: 324 us -> none  [the longest x1 99.9 us: shards(): lax.all_gather(image_teacher, 'img', axis=0, tiled=True)]
    psum x1 -> x0, blocking collectives: 95.3 us -> none  [shards(): overall = lax.psum(jnp.sum(image_loss) + jnp.sum(text_loss), ('img', 'txt'))]
    ppermute x0 -> x20, starting transfers between devices: none -> 62.6 us  [the longest x11 34.2 us: swap(): return lax.ppermute(v, AXES, CORE_PAIRS)]
    ppermute x0 -> x20, waiting for transfers between devices: none -> 26 us  [the longest x6 15.5 us: shards(): up, down = (lax.ppermute(up, AXES, UP), lax.ppermute(down, AXES, DOWN))]
    all_to_all x0 -> x2, waiting for transfers between devices: none -> 20.4 us  [the longest x1 12 us: shards(): parts = lax.all_to_all(stats, AXES, 0, 0, axis_index_groups=STAT_GROUPS)]
    dot_general x3 -> x0, matrix products: 15.7 us -> none  [contract(): lax.dot_general(left, right, (((1,), (1,)), ((), ())), preferred_element_...]
    all_to_all x0 -> x2, starting transfers between devices: none -> 14.4 us  [the longest x1 9.12 us: shards(): parts = lax.all_to_all(stats, AXES, 0, 0, axis_index_groups=STAT_GROUPS)]
  transfers between devices with their start and end apart: 5 -> 22, of which waited for: 5 -> 7; matrix products, arithmetic and copies ran while one was open for 1% -> 0% of each run, Pallas kernels for 0% -> 0%
where the time goes in v2:
time: 143 us; the launch traced here: 142 us
  starting transfers between devices  77 us (54%)
  waiting for transfers between devices  46.4 us (32%)
  Pallas kernels  11.6 us (8%)
  local copies, waits for them, and re-layouts  3.47 us (2%)
  between operations  2.76 us (2%)
    ppermute x11, starting transfers between devices, swap(): return lax.ppermute(v, AXES, CORE_PAIRS)  34.2 us
    ppermute x6, starting transfers between devices, shards(): up, down = (lax.ppermute(up, AXES, UP), lax.ppermute(down, AXES, DOWN))  19.5 us
    ppermute x6, waiting for transfers between devices, shards(): up, down = (lax.ppermute(up, AXES, UP), lax.ppermute(down, AXES, DOWN))  15.5 us
    all_to_all x1, waiting for transfers between devices, shards(): parts = lax.all_to_all(stats, AXES, 0, 0, axis_index_groups=STAT_GROUPS)  12 us
    pallas_call x1, Pallas kernels, tile(): pl.pallas_call(functools.partial(tile_kernel, ds, dt, len(own)), out_shap...  10.7 us
    all_to_all x1, starting transfers between devices, shards(): parts = lax.all_to_all(stats, AXES, 0, 0, axis_index_groups=STAT_GROUPS)  9.12 us
    all_to_all x1, waiting for transfers between devices, shards(): totals = lax.all_to_all(total, AXES, 0, 0, axis_index_groups=SUM_GROUPS)  8.45 us
    ppermute x1, waiting for transfers between devices, shards(): pair = jnp.concatenate([chip, lax.ppermute(chip, AXES, X_PAIRS)], axis=0)  7.76 us
  transfers between devices with their start and end apart: 22, of which 7 were waited for; matrix products, arithmetic and copies ran while one was open for 0% of the time, Pallas kernels for 0%

profile of v2, /device:TPU:1, one launch (start us, length us, event | category | flops | bytes accessed | tf_op | source)
XLA Modules:
  0.0 142.5 jit_solution(12193988851184899052)
XLA Ops:
  1.5 0.9 copy-done.1
  4.0 8.8 %collective-permute-start = (bf16[48,2048]{1,0:T(8,128)(2,1)S(1)}, bf16[48,2048]{1,0:T(8,128)(2,1)S(1)}, u32[]{:S(2)}, u32[]{:S(2)}) collective-permute-start(bf16[48,2048]{1,0:T(8,128)(2,1)S(1)} %get-tuple-element.8), channel_id=1, source_target_pairs={{0,16},{16,0},{2,18},{18,2},{4,20},{20,4},{6,22},{22,6},{8,24},{24... | collective-permute-start | bytes 589832 | tf_op jit(solution)/shard_map/ppermute | solution.py:244
  12.8 1.0 collective-permute-done
  13.9 1.9 %collective-permute-start.1 = (bf16[96,2048]{1,0:T(8,128)(2,1)S(1)}, bf16[96,2048]{1,0:T(8,128)(2,1)S(1)}, u32[]{:S(2)}, u32[]{:S(2)}) collective-permute-start(bf16[96,2048]{1,0:T(8,128)(2,1)S(1)} %pad_maximum_fusion), channel_id=1, source_target_pairs={{0,1},{16,273},{2,3},{18,275},{4,5},{20,277},{6,7},{22,279},{8,9},... | collective-permute-start | bytes 1179656 | tf_op jit(solution)/shard_map/ppermute | solution.py:248
  15.9 7.8 %collective-permute-done.1 = bf16[96,2048]{1,0:T(8,128)(2,1)S(1)} collective-permute-done((bf16[96,2048]{1,0:T(8,128)(2,1)S(1)}, bf16[96,2048]{1,0:T(8,128)(2,1)S(1)}, u32[]{:S(2)}, u32[]{:S(2)}) %collective-permute-start.1) | collective-permute-done | bytes 393248 | tf_op jit(solution)/shard_map/ppermute | solution.py:248
  23.7 1.9 %collective-permute-start.2 = (bf16[192,2048]{1,0:T(8,128)(2,1)S(1)}, bf16[192,2048]{1,0:T(8,128)(2,1)S(1)}, u32[]{:S(2)}, u32[]{:S(2)}) collective-permute-start(bf16[192,2048]{1,0:T(8,128)(2,1)S(1)} %constant_dynamic-update-slice_fusion.refs_0_), channel_id=1, source_target_pairs={{0,2},{16,48},{2,4},{18,50},{4,6},{20,52},{6,8},{22,54},{8,10},{24... | collective-permute-start | bytes 2359304 | tf_op jit(solution)/shard_map/ppermute | solution.py:252
  25.6 4.6 %collective-permute-start.3 = (bf16[192,2048]{1,0:T(8,128)(2,1)S(1)}, bf16[192,2048]{1,0:T(8,128)(2,1)S(1)}, u32[]{:S(2)}, u32[]{:S(2)}) collective-permute-start(bf16[192,2048]{1,0:T(8,128)(2,1)S(1)} %constant_dynamic-update-slice_fusion.refs_0_), channel_id=1, source_target_pairs={{0,14},{16,240},{2,0},{18,242},{4,2},{20,244},{6,4},{22,246},{8,6}... | collective-permute-start | bytes 2359304 | tf_op jit(solution)/shard_map/ppermute | solution.py:252
  30.2 7.7 %collective-permute-done.2.refs_1_ = bf16[192,2048]{1,0:T(8,128)(2,1)S(1)} collective-permute-done((bf16[192,2048]{1,0:T(8,128)(2,1)S(1)}, bf16[192,2048]{1,0:T(8,128)(2,1)S(1)}, u32[]{:S(2)}, u32[]{:S(2)}) %collective-permute-start.2) | collective-permute-done | bytes 786464 | tf_op jit(solution)/shard_map/ppermute | solution.py:252
  37.9 1.9 %collective-permute-start.4 = (bf16[192,2048]{1,0:T(8,128)(2,1)S(1)}, bf16[192,2048]{1,0:T(8,128)(2,1)S(1)}, u32[]{:S(2)}, u32[]{:S(2)}) collective-permute-start(bf16[192,2048]{1,0:T(8,128)(2,1)S(1)} %collective-permute-done.2.refs_1_), channel_id=1, source_target_pairs={{0,2},{16,48},{2,4},{18,50},{4,6},{20,52},{6,8},{22,54},{8,10},{24... | collective-permute-start | bytes 2359304 | tf_op jit(solution)/shard_map/ppermute | solution.py:252
  39.8 4.6 %collective-permute-start.5 = (bf16[192,2048]{1,0:T(8,128)(2,1)S(1)}, bf16[192,2048]{1,0:T(8,128)(2,1)S(1)}, u32[]{:S(2)}, u32[]{:S(2)}) collective-permute-start(bf16[192,2048]{1,0:T(8,128)(2,1)S(1)} %collective-permute-done.3.refs_2_), channel_id=1, source_target_pairs={{0,14},{16,240},{2,0},{18,242},{4,2},{20,244},{6,4},{22,246},{8,6}... | collective-permute-start | bytes 2359304 | tf_op jit(solution)/shard_map/ppermute | solution.py:252
  44.4 7.7 %collective-permute-done.4.refs_3_ = bf16[192,2048]{1,0:T(8,128)(2,1)S(1)} collective-permute-done((bf16[192,2048]{1,0:T(8,128)(2,1)S(1)}, bf16[192,2048]{1,0:T(8,128)(2,1)S(1)}, u32[]{:S(2)}, u32[]{:S(2)}) %collective-permute-start.4) | collective-permute-done | bytes 786464 | tf_op jit(solution)/shard_map/ppermute | solution.py:252
  52.1 1.9 %collective-permute-start.6 = (bf16[192,2048]{1,0:T(8,128)(2,1)S(1)}, bf16[192,2048]{1,0:T(8,128)(2,1)S(1)}, u32[]{:S(2)}, u32[]{:S(2)}) collective-permute-start(bf16[192,2048]{1,0:T(8,128)(2,1)S(1)} %collective-permute-done.4.refs_3_), channel_id=1, source_target_pairs={{0,2},{16,48},{2,4},{18,50},{4,6},{20,52},{6,8},{22,54},{8,10},{24... | collective-permute-start | bytes 2359304 | tf_op jit(solution)/shard_map/ppermute | solution.py:252
  54.1 4.6 %collective-permute-start.7 = (bf16[192,2048]{1,0:T(8,128)(2,1)S(1)}, bf16[192,2048]{1,0:T(8,128)(2,1)S(1)}, u32[]{:S(2)}, u32[]{:S(2)}) collective-permute-start(bf16[192,2048]{1,0:T(8,128)(2,1)S(1)} %collective-permute-done.5.refs_4_), channel_id=1, source_target_pairs={{0,14},{16,240},{2,0},{18,242},{4,2},{20,244},{6,4},{22,246},{8,6}... | collective-permute-start | bytes 2359304 | tf_op jit(solution)/shard_map/ppermute | solution.py:252
  58.6 4.9 %collective-permute-start.10 = (bf16[192,2048]{1,0:T(8,128)(2,1)S(1)}, bf16[192,2048]{1,0:T(8,128)(2,1)S(1)}, u32[]{:S(2)}, u32[]{:S(2)}) collective-permute-start(bf16[192,2048]{1,0:T(8,128)(2,1)S(1)} %constant_dynamic-update-slice_fusion.refs_0_), channel_id=1, source_target_pairs={{0,16},{16,0},{2,18},{18,2},{4,20},{20,4},{6,22},{22,6},{8,24},{24... | collective-permute-start | bytes 2359304 | tf_op jit(solution)/shard_map/ppermute | solution.py:244
  63.6 1.9 %collective-permute-start.11 = (bf16[192,2048]{1,0:T(8,128)(2,1)S(1)}, bf16[192,2048]{1,0:T(8,128)(2,1)S(1)}, u32[]{:S(2)}, u32[]{:S(2)}) collective-permute-start(bf16[192,2048]{1,0:T(8,128)(2,1)S(1)} %collective-permute-done.2.refs_1_), channel_id=1, source_target_pairs={{0,16},{16,0},{2,18},{18,2},{4,20},{20,4},{6,22},{22,6},{8,24},{24... | collective-permute-start | bytes 2359304 | tf_op jit(solution)/shard_map/ppermute | solution.py:244
  65.5 2.4 %collective-permute-start.12 = (bf16[192,2048]{1,0:T(8,128)(2,1)S(1)}, bf16[192,2048]{1,0:T(8,128)(2,1)S(1)}, u32[]{:S(2)}, u32[]{:S(2)}) collective-permute-start(bf16[192,2048]{1,0:T(8,128)(2,1)S(1)} %collective-permute-done.3.refs_2_), channel_id=1, source_target_pairs={{0,16},{16,0},{2,18},{18,2},{4,20},{20,4},{6,22},{22,6},{8,24},{24... | collective-permute-start | bytes 2359304 | tf_op jit(solution)/shard_map/ppermute | solution.py:244
  67.9 3.6 %collective-permute-start.13 = (bf16[192,2048]{1,0:T(8,128)(2,1)S(1)}, bf16[192,2048]{1,0:T(8,128)(2,1)S(1)}, u32[]{:S(2)}, u32[]{:S(2)}) collective-permute-start(bf16[192,2048]{1,0:T(8,128)(2,1)S(1)} %collective-permute-done.4.refs_3_), channel_id=1, source_target_pairs={{0,16},{16,0},{2,18},{18,2},{4,20},{20,4},{6,22},{22,6},{8,24},{24... | collective-permute-start | bytes 2359304 | tf_op jit(solution)/shard_map/ppermute | solution.py:244
  71.6 1.9 %collective-permute-start.14 = (bf16[192,2048]{1,0:T(8,128)(2,1)S(1)}, bf16[192,2048]{1,0:T(8,128)(2,1)S(1)}, u32[]{:S(2)}, u32[]{:S(2)}) collective-permute-start(bf16[192,2048]{1,0:T(8,128)(2,1)S(1)} %collective-permute-done.5.refs_4_), channel_id=1, source_target_pairs={{0,16},{16,0},{2,18},{18,2},{4,20},{20,4},{6,22},{22,6},{8,24},{24... | collective-permute-start | bytes 2359304 | tf_op jit(solution)/shard_map/ppermute | solution.py:244
  73.6 3.2 %collective-permute-start.8 = (bf16[96,2048]{1,0:T(8,128)(2,1)S(1)}, bf16[96,2048]{1,0:T(8,128)(2,1)S(1)}, u32[]{:S(2)}, u32[]{:S(2)}) collective-permute-start(bf16[96,2048]{1,0:T(8,128)(2,1)S(1)} %slice.20), channel_id=1, source_target_pairs={{0,2},{16,48},{2,4},{18,50},{4,6},{20,52},{6,8},{22,54},{8,10},{24... | collective-permute-start | bytes 1179656 | tf_op jit(solution)/shard_map/ppermute | solution.py:256
  76.8 3.8 %collective-permute-start.9 = (bf16[96,2048]{1,0:T(8,128)(2,1)S(1)}, bf16[96,2048]{1,0:T(8,128)(2,1)S(1)}, u32[]{:S(2)}, u32[]{:S(2)}) collective-permute-start(bf16[96,2048]{1,0:T(8,128)(2,1)S(1)} %slice.21), channel_id=1, source_target_pairs={{0,14},{16,240},{2,0},{18,242},{4,2},{20,244},{6,4},{22,246},{8,6}... | collective-permute-start | bytes 1179656 | tf_op jit(solution)/shard_map/ppermute | solution.py:256
  80.7 2.4 %collective-permute-start.15 = (bf16[192,2048]{1,0:T(8,128)(2,1)S(1)}, bf16[192,2048]{1,0:T(8,128)(2,1)S(1)}, u32[]{:S(2)}, u32[]{:S(2)}) collective-permute-start(bf16[192,2048]{1,0:T(8,128)(2,1)S(1)} %collective-permute-done.6.refs_5_), channel_id=1, source_target_pairs={{0,16},{16,0},{2,18},{18,2},{4,20},{20,4},{6,22},{22,6},{8,24},{24... | collective-permute-start | bytes 2359304 | tf_op jit(solution)/shard_map/ppermute | solution.py:244
  83.1 1.9 %collective-permute-start.16 = (bf16[192,2048]{1,0:T(8,128)(2,1)S(1)}, bf16[192,2048]{1,0:T(8,128)(2,1)S(1)}, u32[]{:S(2)}, u32[]{:S(2)}) collective-permute-start(bf16[192,2048]{1,0:T(8,128)(2,1)S(1)} %collective-permute-done.7.refs_6_), channel_id=1, source_target_pairs={{0,16},{16,0},{2,18},{18,2},{4,20},{20,4},{6,22},{22,6},{8,24},{24... | collective-permute-start | bytes 2359304 | tf_op jit(solution)/shard_map/ppermute | solution.py:244
  85.1 2.4 %collective-permute-start.17 = (bf16[96,2048]{1,0:T(8,128)(2,1)S(1)}, bf16[96,2048]{1,0:T(8,128)(2,1)S(1)}, u32[]{:S(2)}, u32[]{:S(2)}) collective-permute-start(bf16[96,2048]{1,0:T(8,128)(2,1)S(1)} %collective-permute-done.8.refs_7_), channel_id=1, source_target_pairs={{0,16},{16,0},{2,18},{18,2},{4,20},{20,4},{6,22},{22,6},{8,24},{24... | collective-permute-start | bytes 1179656 | tf_op jit(solution)/shard_map/ppermute | solution.py:244
  87.5 1.9 %collective-permute-start.18 = (bf16[96,2048]{1,0:T(8,128)(2,1)S(1)}, bf16[96,2048]{1,0:T(8,128)(2,1)S(1)}, u32[]{:S(2)}, u32[]{:S(2)}) collective-permute-start(bf16[96,2048]{1,0:T(8,128)(2,1)S(1)} %collective-permute-done.9.refs_8_), channel_id=1, source_target_pairs={{0,16},{16,0},{2,18},{18,2},{4,20},{20,4},{6,22},{22,6},{8,24},{24... | collective-permute-start | bytes 1179656 | tf_op jit(solution)/shard_map/ppermute | solution.py:244
  89.4 1.7 %collective-permute-done.18.refs_17_ = bf16[96,2048]{1,0:T(8,128)(2,1)S(1)} collective-permute-done((bf16[96,2048]{1,0:T(8,128)(2,1)S(1)}, bf16[96,2048]{1,0:T(8,128)(2,1)S(1)}, u32[]{:S(2)}, u32[]{:S(2)}) %collective-permute-start.18) | collective-permute-done | bytes 393248 | tf_op jit(solution)/shard_map/ppermute | solution.py:244
  91.1 10.7 %shard_map.68 = f32[16,6,8,128]{3,2,1,0:T(8,128)} custom-call(bf16[192,2048]{1,0:T(8,128)(2,1)S(1)} %constant_dynamic-update-slice_fusion.refs_0_, bf16[192,2048]{1,0:T(8,128)(2,1)S(1)} %collective-permute-done.2.refs_1_, bf16[192,2048]{1,0:T(8,128)(2,1)S(1)} %collective-permute-done.3.refs_2_, bf16[192,2048]{1,0:T(8,128)(2,1)S(1)} %collective-permute-done.4.refs_3_, ...), custom_call_target="tpu_custom_call" | custom-call | flops 6039797760 | bytes 15728640 | tf_op jit(solution)/shard_map/pallas_call | solution.py:180
  101.8 9.1 %all-to-all-start = ((f32[16,6,8,128]{3,2,1,0:T(8,128)}), f32[16,6,8,128]{3,2,1,0:T(8,128)S(1)}, u32[]{:S(2)}, u32[]{:S(2)}) async-start(f32[16,6,8,128]{3,2,1,0:T(8,128)} %shard_map.68), calls=%async_computation | async-start | bytes 786432 | tf_op jit(solution)/shard_map/all_to_all | solution.py:260
  111.0 12.0 %all-to-all-done.parts = f32[16,6,8,128]{3,2,1,0:T(8,128)S(1)} async-done(((f32[16,6,8,128]{3,2,1,0:T(8,128)}), f32[16,6,8,128]{3,2,1,0:T(8,128)S(1)}, u32[]{:S(2)}, u32[]{:S(2)}) %all-to-all-start) | async-done | bytes 393248 | tf_op jit(solution)/shard_map/all_to_all | solution.py:260
  122.9 0.9 shard_map.69
  123.8 1.9 %collective-permute-start.19 = (f32[1,128]{1,0:T(1,128)S(1)}, f32[1,128]{1,0:T(1,128)S(1)}, u32[]{:S(2)}, u32[]{:S(2)}) collective-permute-start(f32[1,128]{1,0:T(1,128)S(1)} %get-tuple-element.9), channel_id=1, source_target_pairs={{0,16},{16,0},{2,18},{18,2},{4,20},{20,4},{6,22},{22,6},{8,24},{24... | collective-permute-start | bytes 1544 | tf_op jit(solution)/shard_map/ppermute | solution.py:244
  125.7 5.3 %all-to-all-start.1 = ((f32[32,1,128]{2,1,0:T(1,128)}), f32[32,1,128]{2,1,0:T(1,128)S(1)}, u32[]{:S(2)}, u32[]{:S(2)}) async-start(f32[32,1,128]{2,1,0:T(1,128)} %get-tuple-element.10), calls=%async_computation.1 | async-start | bytes 32768 | tf_op jit(solution)/shard_map/all_to_all | solution.py:265
  131.6 8.4 %all-to-all-done.1 = f32[32,1,128]{2,1,0:T(1,128)S(1)} async-done(((f32[32,1,128]{2,1,0:T(1,128)}), f32[32,1,128]{2,1,0:T(1,128)S(1)}, u32[]{:S(2)}, u32[]{:S(2)}) %all-to-all-start.1) | async-done | bytes 16416 | tf_op jit(solution)/shard_map/all_to_all | solution.py:265
  (31 shorter events, 3.9 us)
Async XLA Ops:
  0.6 0.9 copy-start
  1.5 0.9 copy-start.1
  2.4 0.8 copy-start.2
  3.2 0.8 copy-start.3
  4.0 9.8 %collective-permute-start = (bf16[48,2048]{1,0:T(8,128)(2,1)S(1)}, bf16[48,2048]{1,0:T(8,128)(2,1)S(1)}, u32[]{:S(2)}, u32[]{:S(2)}) collective-permute-start(bf16[48,2048]{1,0:T(8,128)(2,1)S(1)} %get-tuple-element.8), channel_id=1, source_target_pairs={{0,16},{16,0},{2,18},{18,2},{4,20},{20,4},{6,22},{22,6},{8,24},{24... | collective-permute-start | bytes 589832 | tf_op jit(solution)/shard_map/ppermute | solution.py:244
  13.9 9.7 %collective-permute-start.1 = (bf16[96,2048]{1,0:T(8,128)(2,1)S(1)}, bf16[96,2048]{1,0:T(8,128)(2,1)S(1)}, u32[]{:S(2)}, u32[]{:S(2)}) collective-permute-start(bf16[96,2048]{1,0:T(8,128)(2,1)S(1)} %pad_maximum_fusion), channel_id=1, source_target_pairs={{0,1},{16,273},{2,3},{18,275},{4,5},{20,277},{6,7},{22,279},{8,9},... | collective-permute-start | bytes 1179656 | tf_op jit(solution)/shard_map/ppermute | solution.py:248
  23.7 14.2 %collective-permute-start.2 = (bf16[192,2048]{1,0:T(8,128)(2,1)S(1)}, bf16[192,2048]{1,0:T(8,128)(2,1)S(1)}, u32[]{:S(2)}, u32[]{:S(2)}) collective-permute-start(bf16[192,2048]{1,0:T(8,128)(2,1)S(1)} %constant_dynamic-update-slice_fusion.refs_0_), channel_id=1, source_target_pairs={{0,2},{16,48},{2,4},{18,50},{4,6},{20,52},{6,8},{22,54},{8,10},{24... | collective-permute-start | bytes 2359304 | tf_op jit(solution)/shard_map/ppermute | solution.py:252
  25.6 14.2 %collective-permute-start.3 = (bf16[192,2048]{1,0:T(8,128)(2,1)S(1)}, bf16[192,2048]{1,0:T(8,128)(2,1)S(1)}, u32[]{:S(2)}, u32[]{:S(2)}) collective-permute-start(bf16[192,2048]{1,0:T(8,128)(2,1)S(1)} %constant_dynamic-update-slice_fusion.refs_0_), channel_id=1, source_target_pairs={{0,14},{16,240},{2,0},{18,242},{4,2},{20,244},{6,4},{22,246},{8,6}... | collective-permute-start | bytes 2359304 | tf_op jit(solution)/shard_map/ppermute | solution.py:252
  37.9 14.2 %collective-permute-start.4 = (bf16[192,2048]{1,0:T(8,128)(2,1)S(1)}, bf16[192,2048]{1,0:T(8,128)(2,1)S(1)}, u32[]{:S(2)}, u32[]{:S(2)}) collective-permute-start(bf16[192,2048]{1,0:T(8,128)(2,1)S(1)} %collective-permute-done.2.refs_1_), channel_id=1, source_target_pairs={{0,2},{16,48},{2,4},{18,50},{4,6},{20,52},{6,8},{22,54},{8,10},{24... | collective-permute-start | bytes 2359304 | tf_op jit(solution)/shard_map/ppermute | solution.py:252
  39.8 14.2 %collective-permute-start.5 = (bf16[192,2048]{1,0:T(8,128)(2,1)S(1)}, bf16[192,2048]{1,0:T(8,128)(2,1)S(1)}, u32[]{:S(2)}, u32[]{:S(2)}) collective-permute-start(bf16[192,2048]{1,0:T(8,128)(2,1)S(1)} %collective-permute-done.3.refs_2_), channel_id=1, source_target_pairs={{0,14},{16,240},{2,0},{18,242},{4,2},{20,244},{6,4},{22,246},{8,6}... | collective-permute-start | bytes 2359304 | tf_op jit(solution)/shard_map/ppermute | solution.py:252
  52.1 15.8 %collective-permute-start.6 = (bf16[192,2048]{1,0:T(8,128)(2,1)S(1)}, bf16[192,2048]{1,0:T(8,128)(2,1)S(1)}, u32[]{:S(2)}, u32[]{:S(2)}) collective-permute-start(bf16[192,2048]{1,0:T(8,128)(2,1)S(1)} %collective-permute-done.4.refs_3_), channel_id=1, source_target_pairs={{0,2},{16,48},{2,4},{18,50},{4,6},{20,52},{6,8},{22,54},{8,10},{24... | collective-permute-start | bytes 2359304 | tf_op jit(solution)/shard_map/ppermute | solution.py:252
  54.1 17.6 %collective-permute-start.7 = (bf16[192,2048]{1,0:T(8,128)(2,1)S(1)}, bf16[192,2048]{1,0:T(8,128)(2,1)S(1)}, u32[]{:S(2)}, u32[]{:S(2)}) collective-permute-start(bf16[192,2048]{1,0:T(8,128)(2,1)S(1)} %collective-permute-done.5.refs_4_), channel_id=1, source_target_pairs={{0,14},{16,240},{2,0},{18,242},{4,2},{20,244},{6,4},{22,246},{8,6}... | collective-permute-start | bytes 2359304 | tf_op jit(solution)/shard_map/ppermute | solution.py:252
  58.6 15.0 %collective-permute-start.10 = (bf16[192,2048]{1,0:T(8,128)(2,1)S(1)}, bf16[192,2048]{1,0:T(8,128)(2,1)S(1)}, u32[]{:S(2)}, u32[]{:S(2)}) collective-permute-start(bf16[192,2048]{1,0:T(8,128)(2,1)S(1)} %constant_dynamic-update-slice_fusion.refs_0_), channel_id=1, source_target_pairs={{0,16},{16,0},{2,18},{18,2},{4,20},{20,4},{6,22},{22,6},{8,24},{24... | collective-permute-start | bytes 2359304 | tf_op jit(solution)/shard_map/ppermute | solution.py:244
  63.6 13.2 %collective-permute-start.11 = (bf16[192,2048]{1,0:T(8,128)(2,1)S(1)}, bf16[192,2048]{1,0:T(8,128)(2,1)S(1)}, u32[]{:S(2)}, u32[]{:S(2)}) collective-permute-start(bf16[192,2048]{1,0:T(8,128)(2,1)S(1)} %collective-permute-done.2.refs_1_), channel_id=1, source_target_pairs={{0,16},{16,0},{2,18},{18,2},{4,20},{20,4},{6,22},{22,6},{8,24},{24... | collective-permute-start | bytes 2359304 | tf_op jit(solution)/shard_map/ppermute | solution.py:244
  65.5 15.1 %collective-permute-start.12 = (bf16[192,2048]{1,0:T(8,128)(2,1)S(1)}, bf16[192,2048]{1,0:T(8,128)(2,1)S(1)}, u32[]{:S(2)}, u32[]{:S(2)}) collective-permute-start(bf16[192,2048]{1,0:T(8,128)(2,1)S(1)} %collective-permute-done.3.refs_2_), channel_id=1, source_target_pairs={{0,16},{16,0},{2,18},{18,2},{4,20},{20,4},{6,22},{22,6},{8,24},{24... | collective-permute-start | bytes 2359304 | tf_op jit(solution)/shard_map/ppermute | solution.py:244
  67.9 15.2 %collective-permute-start.13 = (bf16[192,2048]{1,0:T(8,128)(2,1)S(1)}, bf16[192,2048]{1,0:T(8,128)(2,1)S(1)}, u32[]{:S(2)}, u32[]{:S(2)}) collective-permute-start(bf16[192,2048]{1,0:T(8,128)(2,1)S(1)} %collective-permute-done.4.refs_3_), channel_id=1, source_target_pairs={{0,16},{16,0},{2,18},{18,2},{4,20},{20,4},{6,22},{22,6},{8,24},{24... | collective-permute-start | bytes 2359304 | tf_op jit(solution)/shard_map/ppermute | solution.py:244
  71.6 17.8 %collective-permute-start.14 = (bf16[192,2048]{1,0:T(8,128)(2,1)S(1)}, bf16[192,2048]{1,0:T(8,128)(2,1)S(1)}, u32[]{:S(2)}, u32[]{:S(2)}) collective-permute-start(bf16[192,2048]{1,0:T(8,128)(2,1)S(1)} %collective-permute-done.5.refs_4_), channel_id=1, source_target_pairs={{0,16},{16,0},{2,18},{18,2},{4,20},{20,4},{6,22},{22,6},{8,24},{24... | collective-permute-start | bytes 2359304 | tf_op jit(solution)/shard_map/ppermute | solution.py:244
  73.6 11.4 %collective-permute-start.8 = (bf16[96,2048]{1,0:T(8,128)(2,1)S(1)}, bf16[96,2048]{1,0:T(8,128)(2,1)S(1)}, u32[]{:S(2)}, u32[]{:S(2)}) collective-permute-start(bf16[96,2048]{1,0:T(8,128)(2,1)S(1)} %slice.20), channel_id=1, source_target_pairs={{0,2},{16,48},{2,4},{18,50},{4,6},{20,52},{6,8},{22,54},{8,10},{24... | collective-permute-start | bytes 1179656 | tf_op jit(solution)/shard_map/ppermute | solution.py:256
  76.8 10.6 %collective-permute-start.9 = (bf16[96,2048]{1,0:T(8,128)(2,1)S(1)}, bf16[96,2048]{1,0:T(8,128)(2,1)S(1)}, u32[]{:S(2)}, u32[]{:S(2)}) collective-permute-start(bf16[96,2048]{1,0:T(8,128)(2,1)S(1)} %slice.21), channel_id=1, source_target_pairs={{0,14},{16,240},{2,0},{18,242},{4,2},{20,244},{6,4},{22,246},{8,6}... | collective-permute-start | bytes 1179656 | tf_op jit(solution)/shard_map/ppermute | solution.py:256
  80.7 10.4 %collective-permute-start.15 = (bf16[192,2048]{1,0:T(8,128)(2,1)S(1)}, bf16[192,2048]{1,0:T(8,128)(2,1)S(1)}, u32[]{:S(2)}, u32[]{:S(2)}) collective-permute-start(bf16[192,2048]{1,0:T(8,128)(2,1)S(1)} %collective-permute-done.6.refs_5_), channel_id=1, source_target_pairs={{0,16},{16,0},{2,18},{18,2},{4,20},{20,4},{6,22},{22,6},{8,24},{24... | collective-permute-start | bytes 2359304 | tf_op jit(solution)/shard_map/ppermute | solution.py:244
  83.1 8.0 %collective-permute-start.16 = (bf16[192,2048]{1,0:T(8,128)(2,1)S(1)}, bf16[192,2048]{1,0:T(8,128)(2,1)S(1)}, u32[]{:S(2)}, u32[]{:S(2)}) collective-permute-start(bf16[192,2048]{1,0:T(8,128)(2,1)S(1)} %collective-permute-done.7.refs_6_), channel_id=1, source_target_pairs={{0,16},{16,0},{2,18},{18,2},{4,20},{20,4},{6,22},{22,6},{8,24},{24... | collective-permute-start | bytes 2359304 | tf_op jit(solution)/shard_map/ppermute | solution.py:244
  85.1 4.4 %collective-permute-start.17 = (bf16[96,2048]{1,0:T(8,128)(2,1)S(1)}, bf16[96,2048]{1,0:T(8,128)(2,1)S(1)}, u32[]{:S(2)}, u32[]{:S(2)}) collective-permute-start(bf16[96,2048]{1,0:T(8,128)(2,1)S(1)} %collective-permute-done.8.refs_7_), channel_id=1, source_target_pairs={{0,16},{16,0},{2,18},{18,2},{4,20},{20,4},{6,22},{22,6},{8,24},{24... | collective-permute-start | bytes 1179656 | tf_op jit(solution)/shard_map/ppermute | solution.py:244
  87.5 3.6 %collective-permute-start.18 = (bf16[96,2048]{1,0:T(8,128)(2,1)S(1)}, bf16[96,2048]{1,0:T(8,128)(2,1)S(1)}, u32[]{:S(2)}, u32[]{:S(2)}) collective-permute-start(bf16[96,2048]{1,0:T(8,128)(2,1)S(1)} %collective-permute-done.9.refs_8_), channel_id=1, source_target_pairs={{0,16},{16,0},{2,18},{18,2},{4,20},{20,4},{6,22},{22,6},{8,24},{24... | collective-permute-start | bytes 1179656 | tf_op jit(solution)/shard_map/ppermute | solution.py:244
  101.8 21.1 %all-to-all-start = ((f32[16,6,8,128]{3,2,1,0:T(8,128)}), f32[16,6,8,128]{3,2,1,0:T(8,128)S(1)}, u32[]{:S(2)}, u32[]{:S(2)}) async-start(f32[16,6,8,128]{3,2,1,0:T(8,128)} %shard_map.68), calls=%async_computation | async-start | bytes 786432 | tf_op jit(solution)/shard_map/all_to_all | solution.py:260
  123.8 7.2 %collective-permute-start.19 = (f32[1,128]{1,0:T(1,128)S(1)}, f32[1,128]{1,0:T(1,128)S(1)}, u32[]{:S(2)}, u32[]{:S(2)}) collective-permute-start(f32[1,128]{1,0:T(1,128)S(1)} %get-tuple-element.9), channel_id=1, source_target_pairs={{0,16},{16,0},{2,18},{18,2},{4,20},{20,4},{6,22},{22,6},{8,24},{24... | collective-permute-start | bytes 1544 | tf_op jit(solution)/shard_map/ppermute | solution.py:244
  125.7 14.3 %all-to-all-start.1 = ((f32[32,1,128]{2,1,0:T(1,128)}), f32[32,1,128]{2,1,0:T(1,128)S(1)}, u32[]{:S(2)}, u32[]{:S(2)}) async-start(f32[32,1,128]{2,1,0:T(1,128)} %get-tuple-element.10), calls=%async_computation.1 | async-start | bytes 32768 | tf_op jit(solution)/shard_map/all_to_all | solution.py:265

commit v3 on v2

v3 whole, which is shorter than its diff:
```python
import functools
import math

import jax
import jax.numpy as jnp
from jax import lax
from jax.experimental import pallas as pl
from jax.experimental.pallas import tpu as pltpu
from jax.sharding import PartitionSpec as P

AXES = ("img", "txt")
LOG2E = 1.0 / math.log(2.0)
LOW = -1e30
SHARD = 48
CHUNK = 256
BLOCK = 128


def place(x, y, z, c):
    return (((x // 2) * 8 + y) * 2 + c) * 16 + z * 2 + x % 2


def everywhere():
    return [
        (x, y, z, c) for x in range(4) for y in range(8) for z in range(8) for c in range(2)
    ]


ROW_X = ((0, 1), (3, 2))
COL_X = ((0, 3), (1, 2))
CORE_PAIRS = [(place(x, y, z, c), place(x, y, z, 1 - c)) for x, y, z, c in everywhere()]
X_PAIRS = [
    (place(x, y, z, c), place(x ^ 1 if c == 0 else 3 - x, y, z, c)) for x, y, z, c in everywhere()
]
X_CROSS = [
    (place(x, y, z, c), place(x ^ 1 if c == 1 else 3 - x, y, z, 1 - c)) for x, y, z, c in everywhere()
]
UP, DOWN = (
    [
        (place(x, y, z, c), place(x, y, (z + s) % 8, c) if c == 0 else place(x, (y + s) % 8, z, c))
        for x, y, z, c in everywhere()
    ]
    for s in (1, -1)
)
STAT_GROUPS = [[place(x, y, z, 0) for z in range(8) for x in pair] for pair in ROW_X for y in range(8)] + [
    [place(x, y, z, 1) for y in range(8) for x in pair] for pair in COL_X for z in range(8)
]
SUM_GROUPS = [
    [place(pair[e], y, k, 0) for y in range(8) for pair in ROW_X]
    + [place(pair[e], k, z, 1) for z in range(8) for pair in COL_X]
    for k in range(8)
    for e in range(2)
]


def where_am_i():
    img = lax.axis_index("img")
    txt = lax.axis_index("txt")
    x_hi, x_lo = img // 16, txt % 2
    core = img % 2
    return jnp.where(core == 0, txt // 2, (img // 2) % 8), jnp.where(core == 0, x_hi ^ x_lo, x_hi)


def dot(left, right):
    return lax.dot_general(
        left, right, (((1,), (1,)), ((), ())), preferred_element_type=jnp.float32
    )


def pack_kernel(image_s, text_s, image_t, text_t, mine, theirs, sems):
    ds, dt = image_s.shape[1], image_t.shape[1]
    core = lax.axis_index("img") % 2

    def copies(image_out, text_out):
        parts = (pl.ds(0, ds), pl.ds(ds, dt), pl.ds(ds + dt, dt))
        out = []
        for n, source in enumerate((image_s, image_t, text_t)):
            out.append(pltpu.make_async_copy(source, image_out.at[:, parts[n]], sems.at[n]))
        for n, source in enumerate((text_s, text_t, image_t)):
            out.append(pltpu.make_async_copy(source, text_out.at[:, parts[n]], sems.at[3 + n]))
        return out

    @pl.when(core == 0)
    def _():
        for copy in copies(mine, theirs):
            copy.start()

    @pl.when(core == 1)
    def _():
        for copy in copies(theirs, mine):
            copy.start()

    for copy in copies(mine, theirs):
        copy.wait()


def pack(image_s, text_s, image_t, text_t):
    shape = jax.ShapeDtypeStruct((SHARD, image_s.shape[1] + 2 * image_t.shape[1]), jnp.bfloat16)
    return pl.pallas_call(
        pack_kernel,
        out_shape=(shape, shape),
        in_specs=[pl.BlockSpec(memory_space=pl.ANY)] * 4,
        out_specs=[pl.BlockSpec(memory_space=pltpu.VMEM)] * 2,
        scratch_shapes=[pltpu.SemaphoreType.DMA((6,))],
        compiler_params=pltpu.CompilerParams(vmem_limit_bytes=60 * 1024 * 1024),
    )(image_s, text_s, image_t, text_t)


def piece(refs, start, stop, low, high):
    parts, at = [], 0
    for ref in refs:
        size = ref.shape[0]
        a, b = max(start - at, 0), min(stop - at, size)
        if a < b:
            parts.append(ref[a:b, low:high])
        at += size
    return jnp.concatenate(parts, axis=0) if len(parts) > 1 else parts[0]


def products(ds, dt, own, other, lanes, rows, l, g):
    l[: rows[1] - rows[0], :] = dot(piece(other, *rows, 0, ds), piece(own, *lanes, 0, ds))
    g[: rows[1] - rows[0], :] = dot(piece(other, *rows, ds + dt, ds + 2 * dt), piece(own, *lanes, ds, ds + dt))


def summary(ds, dt, l, g, rows, first):
    kl = 2.0 / math.sqrt(ds) * LOG2E
    kt = 3.0 / math.sqrt(dt) * LOG2E
    diagonal = jnp.zeros((1, CHUNK), jnp.float32)
    if first:
        s = lax.broadcasted_iota(jnp.int32, (2 * SHARD, CHUNK), 0)
        r = lax.broadcasted_iota(jnp.int32, (2 * SHARD, CHUNK), 1)
        same = (r < 2 * SHARD) & (s == jnp.where(r < SHARD, r + SHARD, r - SHARD))
        g[: 2 * SHARD, :] = jnp.where(same, LOW, g[: 2 * SHARD, :])
        diagonal = jnp.sum(jnp.where(same, l[: 2 * SHARD, :], 0.0), axis=0, keepdims=True)
    blocks = [slice(i, min(i + BLOCK, rows)) for i in range(0, rows, BLOCK)]

    def eights(v):
        return v.reshape(v.shape[0] // 8, 8, CHUNK)

    top = high = jnp.full((8, CHUNK), LOW, jnp.float32)
    for here in blocks:
        top = jnp.maximum(top, jnp.max(eights(l[here, :]), axis=0))
        high = jnp.maximum(high, jnp.max(eights(g[here, :]), axis=0))
    top = jnp.max(top, axis=0, keepdims=True)
    high = jnp.max(high, axis=0, keepdims=True)
    total = mass = weighted = jnp.zeros((8, CHUNK), jnp.float32)
    for here in blocks:
        lv = l[here, :]
        e = jnp.exp2((g[here, :] - high) * kt)
        total += jnp.sum(eights(jnp.exp2((lv - top) * kl)), axis=0)
        mass += jnp.sum(eights(e), axis=0)
        weighted += jnp.sum(eights(e * lv), axis=0)
    total = jnp.sum(total, axis=0, keepdims=True)
    mass = jnp.sum(mass, axis=0, keepdims=True)
    weighted = jnp.sum(weighted, axis=0, keepdims=True)
    return (
        top * (kl / LOG2E) + jnp.log(total),
        high * (kt / LOG2E) + jnp.log(mass),
        weighted / mass * (kl / LOG2E),
        diagonal * (kl / LOG2E),
    )


def early_kernel(ds, dt, units, *refs):
    own, other = refs[:units], refs[units : 2 * units]
    out, l, g = refs[2 * units :]
    rows = units * 4 * SHARD
    chunks = rows // CHUNK

    def multiply(j):
        products(ds, dt, own, other, (j * CHUNK, (j + 1) * CHUNK), (0, rows), l.at[j % 2], g.at[j % 2])

    multiply(0)
    for j in range(chunks):
        if j + 1 < chunks:
            multiply(j + 1)
        for n, v in enumerate(summary(ds, dt, l.at[j % 2], g.at[j % 2], rows, j == 0)):
            out[n : n + 1, j * CHUNK : (j + 1) * CHUNK] = v


def early(own, other, ds, dt):
    rows = len(own) * 4 * SHARD
    chunks = rows // CHUNK
    vmem = pl.BlockSpec(memory_space=pltpu.VMEM)
    work = rows * chunks * CHUNK
    return pl.pallas_call(
        functools.partial(early_kernel, ds, dt, len(own)),
        out_shape=jax.ShapeDtypeStruct((8, chunks * CHUNK), jnp.float32),
        in_specs=[vmem] * (len(own) + len(other)),
        out_specs=vmem,
        scratch_shapes=[pltpu.VMEM((2, rows, CHUNK), jnp.float32)] * 2,
        compiler_params=pltpu.CompilerParams(vmem_limit_bytes=20 * 1024 * 1024),
        cost_estimate=pl.CostEstimate(
            flops=2 * work * (ds + dt), bytes_accessed=8 * rows * (ds + dt), transcendentals=2 * work
        ),
    )(*own, *other)


def late_kernel(ds, dt, units, known, *refs):
    own, other = refs[:units], refs[units : 2 * units]
    before, out, l, g, ls, gs, stats = refs[2 * units :]
    rows = units * 4 * SHARD
    chunks = rows // CHUNK
    done = known // CHUNK
    line, xi = where_am_i()

    def lanes(j):
        return j * CHUNK, (j + 1) * CHUNK

    for j in range(done):
        products(ds, dt, own, other, lanes(j), (known, rows), ls.at[j], gs.at[j])
    for j in range(done, chunks):
        products(ds, dt, own, other, lanes(j), (0, rows), l.at[j % 2], g.at[j % 2])
        if j == done:
            for i in range(done):
                to = slice(*lanes(i))
                lse, mark, mean, _ = summary(ds, dt, ls.at[i], gs.at[i], rows - known, False)
                old_lse, old_mark, old_mean = (before[n : n + 1, to] for n in range(3))
                top = jnp.maximum(lse, old_lse)
                stats[0:1, to] = top + jnp.log(jnp.exp(lse - top) + jnp.exp(old_lse - top))
                top = jnp.maximum(mark, old_mark)
                one, two = jnp.exp(mark - top), jnp.exp(old_mark - top)
                stats[1:2, to] = top + jnp.log(one + two)
                stats[2:3, to] = (one * mean + two * old_mean) / (one + two)
                stats[3:4, to] = before[3:4, to]
        else:
            for n, v in enumerate(summary(ds, dt, l.at[(j - 1) % 2], g.at[(j - 1) % 2], rows, False)):
                stats[n : n + 1, slice(*lanes(j - 1))] = v
    for n, v in enumerate(summary(ds, dt, l.at[(chunks - 1) % 2], g.at[(chunks - 1) % 2], rows, False)):
        stats[n : n + 1, slice(*lanes(chunks - 1))] = v

    for k, step in enumerate((0, 7, 1, 6, 2, 5, 3, 4)):
        v = stats[:4, k * 4 * SHARD : (k + 1) * 4 * SHARD]
        v = jnp.where(xi == 0, v, jnp.concatenate([v[:, 2 * SHARD :], v[:, : 2 * SHARD]], axis=1))
        row = pl.ds(lax.rem(line + step, 8), 1)
        for n in range(4):
            out[0, n, row, :] = v[n : n + 1, :128]
            out[0, 4 + n // 2, row, (n % 2) * 64 : (n % 2 + 1) * 64] = v[n : n + 1, 128:]
    for k in range(1, out.shape[0]):
        out[k] = out[0]


def late(own, other, before, known, ds, dt):
    rows = len(own) * 4 * SHARD
    chunks, done = rows // CHUNK, known // CHUNK
    vmem = pl.BlockSpec(memory_space=pltpu.VMEM)
    work = rows * rows - known * done * CHUNK
    return pl.pallas_call(
        functools.partial(late_kernel, ds, dt, len(own), known),
        out_shape=jax.ShapeDtypeStruct((16, 6, 8, 128), jnp.float32),
        in_specs=[vmem] * (len(own) + len(other) + 1),
        out_specs=vmem,
        scratch_shapes=[pltpu.VMEM((2, rows, CHUNK), jnp.float32)] * 2
        + [pltpu.VMEM((done, rows - known, CHUNK), jnp.float32)] * 2
        + [pltpu.VMEM((8, rows), jnp.float32)],
        compiler_params=pltpu.CompilerParams(vmem_limit_bytes=20 * 1024 * 1024),
        cost_estimate=pl.CostEstimate(
            flops=2 * work * (ds + dt), bytes_accessed=8 * rows * (ds + dt), transcendentals=2 * work
        ),
    )(*own, *other, before)


def losses(parts, count, lse, mark, mean, diagonal):
    top, high = lse(0), mark(0)
    for k in range(1, count):
        top = jnp.maximum(top, lse(k))
        high = jnp.maximum(high, mark(k))
    spread = mass = weighted = own = jnp.zeros_like(top)
    for k in range(count):
        e = jnp.exp(mark(k) - high)
        spread += jnp.exp(lse(k) - top)
        mass += e
        weighted += e * mean(k)
        own += diagonal(k)
    return top + jnp.log(spread) - 0.5 * own - 0.5 * weighted / mass


def halves(parts, rows):
    count = parts.shape[0]
    return (
        losses(parts, count, *(lambda k, n=n: parts[k, n, rows, :] for n in range(4))),
        losses(
            parts,
            count,
            *(lambda k, n=n: parts[k, 4 + n // 2, rows, (n % 2) * 64 : (n % 2 + 1) * 64] for n in range(4)),
        ),
    )


def finish_kernel(parts, mine, total, held):
    line, xi = where_am_i()
    one, two = halves(parts, slice(0, 8))
    held[:, :128] = one
    held[:, 128:] = jnp.concatenate([two, two], axis=1)
    v = held[pl.ds(line, 1), :]
    mine[...] = jnp.where(xi == 0, v[:, :128], v[:, 2 * SHARD : 2 * SHARD + 128])
    total[...] = jnp.full(total.shape, jnp.sum(one) + jnp.sum(two), jnp.float32)


def finish(parts):
    vmem = pl.BlockSpec(memory_space=pltpu.VMEM)
    return pl.pallas_call(
        finish_kernel,
        out_shape=(
            jax.ShapeDtypeStruct((1, 128), jnp.float32),
            jax.ShapeDtypeStruct((32, 1, 128), jnp.float32),
        ),
        in_specs=[vmem],
        out_specs=[vmem] * 2,
        scratch_shapes=[pltpu.VMEM((8, 256), jnp.float32)],
        compiler_params=pltpu.CompilerParams(vmem_limit_bytes=4 * 1024 * 1024),
    )(parts)


def shards(image_student, text_student, image_teacher, text_teacher):
    ds, dt = image_student.shape[1], image_teacher.shape[1]
    core = lax.axis_index("img") % 2

    def swap(v):
        return lax.ppermute(v, AXES, CORE_PAIRS)

    mine, theirs = pack(image_student, text_student, image_teacher, text_teacher)
    across = lax.ppermute(mine, AXES, X_PAIRS)
    beyond = lax.ppermute(theirs, AXES, X_CROSS)
    pair = jnp.concatenate([mine, swap(theirs), across, beyond], axis=0)
    own, other = [pair], []
    ready, sent, up, down = [pair], [], pair, pair
    for _ in range(3):
        up, sent = lax.optimization_barrier((up, sent))
        other += sent
        up, down = lax.ppermute(up, AXES, UP), lax.ppermute(down, AXES, DOWN)
        sent = [swap(v) for v in ready]
        ready = [up, down]
        own += ready
    up, sent = lax.optimization_barrier((up, sent))
    last = lax.ppermute(up, AXES, UP)
    other += sent
    before, last = lax.optimization_barrier((early(own[:5], other[:5], ds, dt), last))
    known = 5 * pair.shape[0]
    other += [swap(v) for v in ready + [last]]
    stats = late(own + [last], other, before, known, ds, dt)
    parts = lax.all_to_all(stats, AXES, 0, 0, axis_index_groups=STAT_GROUPS)
    chip, total = finish(parts)
    first, second = chip[0, :SHARD], swap(chip)[0, SHARD : 2 * SHARD]
    image_loss = jnp.where(core == 0, first, second)
    text_loss = jnp.where(core == 0, second, first)
    totals = lax.all_to_all(total, AXES, 0, 0, axis_index_groups=SUM_GROUPS)
    return image_loss, text_loss, jnp.sum(totals[:, 0, 0]) / (2.0 * SHARD * 512)


def solution(mesh):
    spec = P(("img", "txt"), None)
    return jax.shard_map(
        shards,
        mesh=mesh,
        in_specs=(spec, spec, spec, spec),
        out_specs=(P(("img", "txt")), P(("img", "txt")), P()),
        check_vma=False,
    )
```

time: 143 us -> 136 us (0.951)
  waiting for transfers between devices: 46.4 us -> 37.3 us
  local copies, waits for them, and re-layouts: 3.47 us -> 1 us
  Pallas kernels: 11.6 us -> 13.9 us
  starting transfers between devices: 77 us -> 79 us
    ppermute x11 -> x10, starting transfers between devices: 34.2 us -> 40.3 us  [swap(): return lax.ppermute(v, AXES, CORE_PAIRS)]
    ppermute x6, waiting for transfers between devices: 15.5 us -> 9.48 us  [shards(): up, down = (lax.ppermute(up, AXES, UP), lax.ppermute(down, AXES, DOWN))]
    ppermute x3, starting transfers between devices: 8.94 us -> 5.76 us  [the longest x1 1.92 us: shards(): last = lax.ppermute(up, AXES, UP)]
    unnamed x10 -> x3, local copies, waits for them, and re-layouts: 3.39 us -> 0.98 us
    pallas_call x2 -> x3, Pallas kernels: 10.7 us -> 13 us  [the longest x1 7.89 us: late(): pl.pallas_call(functools.partial(late_kernel, ds, dt, len(own), known), o...]
    all_to_all x1, starting transfers between devices: 9.12 us -> 6.92 us  [shards(): parts = lax.all_to_all(stats, AXES, 0, 0, axis_index_groups=STAT_GROUPS)]
    ppermute x3, waiting for transfers between devices: 7.76 us -> 5.68 us  [the longest x1 5.67 us: shards(): across = lax.ppermute(mine, AXES, X_PAIRS)]
  transfers between devices with their start and end apart: 22 -> 21, of which waited for: 7 -> 7; matrix products, arithmetic and copies ran while one was open for 0% -> 1% of each run, Pallas kernels for 0% -> 2%
where the time goes in v3:
time: 136 us; the launch traced here: 135 us
  starting transfers between devices  79 us (58%)
  waiting for transfers between devices  37.3 us (27%)
  Pallas kernels  13.9 us (10%)
  between operations  2.73 us (2%)
    ppermute x10, starting transfers between devices, swap(): return lax.ppermute(v, AXES, CORE_PAIRS)  40.3 us
    ppermute x6, starting transfers between devices, shards(): up, down = (lax.ppermute(up, AXES, UP), lax.ppermute(down, AXES, DOWN))  20.5 us
    all_to_all x1, waiting for transfers between devices, shards(): parts = lax.all_to_all(stats, AXES, 0, 0, axis_index_groups=STAT_GROUPS)  12 us
    ppermute x6, waiting for transfers between devices, shards(): up, down = (lax.ppermute(up, AXES, UP), lax.ppermute(down, AXES, DOWN))  9.48 us
    all_to_all x1, waiting for transfers between devices, shards(): totals = lax.all_to_all(total, AXES, 0, 0, axis_index_groups=SUM_GROUPS)  8.45 us
    pallas_call x1, Pallas kernels, late(): pl.pallas_call(functools.partial(late_kernel, ds, dt, len(own), known), o...  7.89 us
    all_to_all x1, starting transfers between devices, shards(): parts = lax.all_to_all(stats, AXES, 0, 0, axis_index_groups=STAT_GROUPS)  6.92 us
    ppermute x1, waiting for transfers between devices, shards(): across = lax.ppermute(mine, AXES, X_PAIRS)  5.67 us
  transfers between devices with their start and end apart: 21, of which 7 were waited for; matrix products, arithmetic and copies ran while one was open for 1% of the time, Pallas kernels for 2%

profile of v3, /device:TPU:1, one launch (start us, length us, event | category | flops | bytes accessed | tf_op | source)
XLA Modules:
  0.0 135.1 jit_solution(10044700707254204446)
XLA Ops:
  0.6 1.9 %shard_map.67 = (bf16[48,2048]{1,0:T(8,128)(2,1)}, bf16[48,2048]{1,0:T(8,128)(2,1)}) custom-call(bf16[48,512]{1,0:T(8,128)(2,1)} %image_s.1, bf16[48,512]{1,0:T(8,128)(2,1)} %text_s.1, bf16[48,768]{1,0:T(8,128)(2,1)} %image_t.1, bf16[48,768]{1,0:T(8,128)(2,1)} %text_t.1), custom_call_target="tpu_custom_call" | custom-call | tf_op jit(solution)/shard_map/pallas_call | solution.py:99
  2.5 8.8 %collective-permute-start = (bf16[48,2048]{1,0:T(8,128)(2,1)}, bf16[48,2048]{1,0:T(8,128)(2,1)S(1)}, u32[]{:S(2)}, u32[]{:S(2)}) collective-permute-start(bf16[48,2048]{1,0:T(8,128)(2,1)} %get-tuple-element.18), channel_id=1, source_target_pairs={{0,16},{16,0},{2,18},{18,2},{4,20},{20,4},{6,22},{22,6},{8,24},{24... | collective-permute-start | bytes 589832 | tf_op jit(solution)/shard_map/ppermute | solution.py:320
  11.3 1.9 %collective-permute-start.2 = (bf16[48,2048]{1,0:T(8,128)(2,1)}, bf16[48,2048]{1,0:T(8,128)(2,1)S(1)}, u32[]{:S(2)}, u32[]{:S(2)}) collective-permute-start(bf16[48,2048]{1,0:T(8,128)(2,1)} %get-tuple-element.18), channel_id=1, source_target_pairs={{0,273},{16,1},{2,275},{18,3},{4,277},{20,5},{6,279},{22,7},{8,281... | collective-permute-start | bytes 589832 | tf_op jit(solution)/shard_map/ppermute | solution.py:324
  13.2 1.9 %collective-permute-start.1 = (bf16[48,2048]{1,0:T(8,128)(2,1)}, bf16[48,2048]{1,0:T(8,128)(2,1)S(1)}, u32[]{:S(2)}, u32[]{:S(2)}) collective-permute-start(bf16[48,2048]{1,0:T(8,128)(2,1)} %get-tuple-element.17), channel_id=1, source_target_pairs={{0,1},{16,273},{2,3},{18,275},{4,5},{20,277},{6,7},{22,279},{8,9},... | collective-permute-start | bytes 589832 | tf_op jit(solution)/shard_map/ppermute | solution.py:323
  15.1 1.0 constant_dynamic-update-slice_fusion.3
  16.1 5.7 %collective-permute-done.1 = bf16[48,2048]{1,0:T(8,128)(2,1)S(1)} collective-permute-done((bf16[48,2048]{1,0:T(8,128)(2,1)}, bf16[48,2048]{1,0:T(8,128)(2,1)S(1)}, u32[]{:S(2)}, u32[]{:S(2)}) %collective-permute-start.1) | collective-permute-done | bytes 196640 | tf_op jit(solution)/shard_map/ppermute | solution.py:323
  21.9 1.9 %collective-permute-start.3 = (bf16[192,2048]{1,0:T(8,128)(2,1)S(1)}, bf16[192,2048]{1,0:T(8,128)(2,1)S(1)}, u32[]{:S(2)}, u32[]{:S(2)}) collective-permute-start(bf16[192,2048]{1,0:T(8,128)(2,1)S(1)} %constant_dynamic-update-slice_fusion.refs_0_), channel_id=1, source_target_pairs={{0,2},{16,48},{2,4},{18,50},{4,6},{20,52},{6,8},{22,54},{8,10},{24... | collective-permute-start | bytes 2359304 | tf_op jit(solution)/shard_map/ppermute | solution.py:331
  23.8 1.9 %collective-permute-start.5 = (bf16[192,2048]{1,0:T(8,128)(2,1)S(1)}, bf16[192,2048]{1,0:T(8,128)(2,1)S(1)}, u32[]{:S(2)}, u32[]{:S(2)}) collective-permute-start(bf16[192,2048]{1,0:T(8,128)(2,1)S(1)} %constant_dynamic-update-slice_fusion.refs_0_), channel_id=1, source_target_pairs={{0,16},{16,0},{2,18},{18,2},{4,20},{20,4},{6,22},{22,6},{8,24},{24... | collective-permute-start | bytes 2359304 | tf_op jit(solution)/shard_map/ppermute | solution.py:320
  25.7 4.6 %collective-permute-start.4 = (bf16[192,2048]{1,0:T(8,128)(2,1)S(1)}, bf16[192,2048]{1,0:T(8,128)(2,1)S(1)}, u32[]{:S(2)}, u32[]{:S(2)}) collective-permute-start(bf16[192,2048]{1,0:T(8,128)(2,1)S(1)} %constant_dynamic-update-slice_fusion.refs_0_), channel_id=1, source_target_pairs={{0,14},{16,240},{2,0},{18,242},{4,2},{20,244},{6,4},{22,246},{8,6}... | collective-permute-start | bytes 2359304 | tf_op jit(solution)/shard_map/ppermute | solution.py:331
  30.3 5.8 %collective-permute-done.3.refs_1_ = bf16[192,2048]{1,0:T(8,128)(2,1)S(1)} collective-permute-done((bf16[192,2048]{1,0:T(8,128)(2,1)S(1)}, bf16[192,2048]{1,0:T(8,128)(2,1)S(1)}, u32[]{:S(2)}, u32[]{:S(2)}) %collective-permute-start.3) | collective-permute-done | bytes 786464 | tf_op jit(solution)/shard_map/ppermute | solution.py:331
  36.1 1.9 %collective-permute-start.6 = (bf16[192,2048]{1,0:T(8,128)(2,1)S(1)}, bf16[192,2048]{1,0:T(8,128)(2,1)S(1)}, u32[]{:S(2)}, u32[]{:S(2)}) collective-permute-start(bf16[192,2048]{1,0:T(8,128)(2,1)S(1)} %collective-permute-done.3.refs_1_), channel_id=1, source_target_pairs={{0,2},{16,48},{2,4},{18,50},{4,6},{20,52},{6,8},{22,54},{8,10},{24... | collective-permute-start | bytes 2359304 | tf_op jit(solution)/shard_map/ppermute | solution.py:331
  38.0 5.3 %collective-permute-start.8 = (bf16[192,2048]{1,0:T(8,128)(2,1)S(1)}, bf16[192,2048]{1,0:T(8,128)(2,1)S(1)}, u32[]{:S(2)}, u32[]{:S(2)}) collective-permute-start(bf16[192,2048]{1,0:T(8,128)(2,1)S(1)} %collective-permute-done.3.refs_1_), channel_id=1, source_target_pairs={{0,16},{16,0},{2,18},{18,2},{4,20},{20,4},{6,22},{22,6},{8,24},{24... | collective-permute-start | bytes 2359304 | tf_op jit(solution)/shard_map/ppermute | solution.py:320
  43.3 1.9 %collective-permute-start.9 = (bf16[192,2048]{1,0:T(8,128)(2,1)S(1)}, bf16[192,2048]{1,0:T(8,128)(2,1)S(1)}, u32[]{:S(2)}, u32[]{:S(2)}) collective-permute-start(bf16[192,2048]{1,0:T(8,128)(2,1)S(1)} %collective-permute-done.4.refs_2_), channel_id=1, source_target_pairs={{0,16},{16,0},{2,18},{18,2},{4,20},{20,4},{6,22},{22,6},{8,24},{24... | collective-permute-start | bytes 2359304 | tf_op jit(solution)/shard_map/ppermute | solution.py:320
  45.2 5.1 %collective-permute-start.7 = (bf16[192,2048]{1,0:T(8,128)(2,1)S(1)}, bf16[192,2048]{1,0:T(8,128)(2,1)S(1)}, u32[]{:S(2)}, u32[]{:S(2)}) collective-permute-start(bf16[192,2048]{1,0:T(8,128)(2,1)S(1)} %collective-permute-done.4.refs_2_), channel_id=1, source_target_pairs={{0,14},{16,240},{2,0},{18,242},{4,2},{20,244},{6,4},{22,246},{8,6}... | collective-permute-start | bytes 2359304 | tf_op jit(solution)/shard_map/ppermute | solution.py:331
  50.4 1.9 %collective-permute-start.10 = (bf16[192,2048]{1,0:T(8,128)(2,1)S(1)}, bf16[192,2048]{1,0:T(8,128)(2,1)S(1)}, u32[]{:S(2)}, u32[]{:S(2)}) collective-permute-start(bf16[192,2048]{1,0:T(8,128)(2,1)S(1)} %collective-permute-done.6.refs_3_), channel_id=1, source_target_pairs={{0,2},{16,48},{2,4},{18,50},{4,6},{20,52},{6,8},{22,54},{8,10},{24... | collective-permute-start | bytes 2359304 | tf_op jit(solution)/shard_map/ppermute | solution.py:331
  52.3 6.1 %collective-permute-start.12 = (bf16[192,2048]{1,0:T(8,128)(2,1)S(1)}, bf16[192,2048]{1,0:T(8,128)(2,1)S(1)}, u32[]{:S(2)}, u32[]{:S(2)}) collective-permute-start(bf16[192,2048]{1,0:T(8,128)(2,1)S(1)} %collective-permute-done.6.refs_3_), channel_id=1, source_target_pairs={{0,16},{16,0},{2,18},{18,2},{4,20},{20,4},{6,22},{22,6},{8,24},{24... | collective-permute-start | bytes 2359304 | tf_op jit(solution)/shard_map/ppermute | solution.py:320
  59.2 3.0 %collective-permute-start.13 = (bf16[192,2048]{1,0:T(8,128)(2,1)S(1)}, bf16[192,2048]{1,0:T(8,128)(2,1)S(1)}, u32[]{:S(2)}, u32[]{:S(2)}) collective-permute-start(bf16[192,2048]{1,0:T(8,128)(2,1)S(1)} %collective-permute-done.7.refs_4_), channel_id=1, source_target_pairs={{0,16},{16,0},{2,18},{18,2},{4,20},{20,4},{6,22},{22,6},{8,24},{24... | collective-permute-start | bytes 2359304 | tf_op jit(solution)/shard_map/ppermute | solution.py:320
  62.2 5.1 %collective-permute-start.11 = (bf16[192,2048]{1,0:T(8,128)(2,1)S(1)}, bf16[192,2048]{1,0:T(8,128)(2,1)S(1)}, u32[]{:S(2)}, u32[]{:S(2)}) collective-permute-start(bf16[192,2048]{1,0:T(8,128)(2,1)S(1)} %collective-permute-done.7.refs_4_), channel_id=1, source_target_pairs={{0,14},{16,240},{2,0},{18,242},{4,2},{20,244},{6,4},{22,246},{8,6}... | collective-permute-start | bytes 2359304 | tf_op jit(solution)/shard_map/ppermute | solution.py:331
  67.4 1.9 %collective-permute-start.14 = (bf16[192,2048]{1,0:T(8,128)(2,1)S(1)}, bf16[192,2048]{1,0:T(8,128)(2,1)S(1)}, u32[]{:S(2)}, u32[]{:S(2)}) collective-permute-start(bf16[192,2048]{1,0:T(8,128)(2,1)S(1)} %collective-permute-done.10.refs_5_), channel_id=1, source_target_pairs={{0,2},{16,48},{2,4},{18,50},{4,6},{20,52},{6,8},{22,54},{8,10},{24... | collective-permute-start | bytes 2359304 | tf_op jit(solution)/shard_map/ppermute | solution.py:336
  69.3 4.1 %collective-permute-start.15 = (bf16[192,2048]{1,0:T(8,128)(2,1)S(1)}, bf16[192,2048]{1,0:T(8,128)(2,1)S(1)}, u32[]{:S(2)}, u32[]{:S(2)}) collective-permute-start(bf16[192,2048]{1,0:T(8,128)(2,1)S(1)} %collective-permute-done.10.refs_5_), channel_id=1, source_target_pairs={{0,16},{16,0},{2,18},{18,2},{4,20},{20,4},{6,22},{22,6},{8,24},{24... | collective-permute-start | bytes 2359304 | tf_op jit(solution)/shard_map/ppermute | solution.py:320
  73.5 2.8 %collective-permute-done.11.refs_6_ = bf16[192,2048]{1,0:T(8,128)(2,1)S(1)} collective-permute-done((bf16[192,2048]{1,0:T(8,128)(2,1)S(1)}, bf16[192,2048]{1,0:T(8,128)(2,1)S(1)}, u32[]{:S(2)}, u32[]{:S(2)}) %collective-permute-start.11) | collective-permute-done | bytes 786464 | tf_op jit(solution)/shard_map/ppermute | solution.py:331
  76.3 3.0 %collective-permute-start.16 = (bf16[192,2048]{1,0:T(8,128)(2,1)S(1)}, bf16[192,2048]{1,0:T(8,128)(2,1)S(1)}, u32[]{:S(2)}, u32[]{:S(2)}) collective-permute-start(bf16[192,2048]{1,0:T(8,128)(2,1)S(1)} %collective-permute-done.11.refs_6_), channel_id=1, source_target_pairs={{0,16},{16,0},{2,18},{18,2},{4,20},{20,4},{6,22},{22,6},{8,24},{24... | collective-permute-start | bytes 2359304 | tf_op jit(solution)/shard_map/ppermute | solution.py:320
  79.3 3.2 %shard_map.68.refs_16_ = f32[8,768]{1,0:T(8,128)S(1)} custom-call(bf16[192,2048]{1,0:T(8,128)(2,1)S(1)} %constant_dynamic-update-slice_fusion.refs_0_, bf16[192,2048]{1,0:T(8,128)(2,1)S(1)} %collective-permute-done.3.refs_1_, bf16[192,2048]{1,0:T(8,128)(2,1)S(1)} %collective-permute-done.4.refs_2_, bf16[192,2048]{1,0:T(8,128)(2,1)S(1)} %collective-permute-done.6.refs_3_, ...), custom_call_target="tpu_custom_call" | custom-call | flops 1887436800 | bytes 9830400 | tf_op jit(solution)/shard_map/pallas_call | solution.py:186
  82.5 4.3 %collective-permute-start.17 = (bf16[192,2048]{1,0:T(8,128)(2,1)S(1)}, bf16[192,2048]{1,0:T(8,128)(2,1)S(1)}, u32[]{:S(2)}, u32[]{:S(2)}) collective-permute-start(bf16[192,2048]{1,0:T(8,128)(2,1)S(1)} %collective-permute-done.14.refs_7_), channel_id=1, source_target_pairs={{0,16},{16,0},{2,18},{18,2},{4,20},{20,4},{6,22},{22,6},{8,24},{24... | collective-permute-start | bytes 2359304 | tf_op jit(solution)/shard_map/ppermute | solution.py:320
  86.8 1.7 %collective-permute-done.17.refs_15_ = bf16[192,2048]{1,0:T(8,128)(2,1)S(1)} collective-permute-done((bf16[192,2048]{1,0:T(8,128)(2,1)S(1)}, bf16[192,2048]{1,0:T(8,128)(2,1)S(1)}, u32[]{:S(2)}, u32[]{:S(2)}) %collective-permute-start.17) | collective-permute-done | bytes 786464 | tf_op jit(solution)/shard_map/ppermute | solution.py:320
  88.5 7.9 %shard_map.69 = f32[16,6,8,128]{3,2,1,0:T(8,128)} custom-call(bf16[192,2048]{1,0:T(8,128)(2,1)S(1)} %constant_dynamic-update-slice_fusion.refs_0_, bf16[192,2048]{1,0:T(8,128)(2,1)S(1)} %collective-permute-done.3.refs_1_, bf16[192,2048]{1,0:T(8,128)(2,1)S(1)} %collective-permute-done.4.refs_2_, bf16[192,2048]{1,0:T(8,128)(2,1)S(1)} %collective-permute-done.6.refs_3_, ...), custom_call_target="tpu_custom_call" | custom-call | flops 4152360960 | bytes 15728640 | tf_op jit(solution)/shard_map/pallas_call | solution.py:248
  96.4 6.9 %all-to-all-start = ((f32[16,6,8,128]{3,2,1,0:T(8,128)}), f32[16,6,8,128]{3,2,1,0:T(8,128)S(1)}, u32[]{:S(2)}, u32[]{:S(2)}) async-start(f32[16,6,8,128]{3,2,1,0:T(8,128)} %shard_map.69), calls=%async_computation | async-start | bytes 786432 | tf_op jit(solution)/shard_map/all_to_all | solution.py:342
  103.3 12.0 %all-to-all-done.parts = f32[16,6,8,128]{3,2,1,0:T(8,128)S(1)} async-done(((f32[16,6,8,128]{3,2,1,0:T(8,128)}), f32[16,6,8,128]{3,2,1,0:T(8,128)S(1)}, u32[]{:S(2)}, u32[]{:S(2)}) %all-to-all-start) | async-done | bytes 393248 | tf_op jit(solution)/shard_map/all_to_all | solution.py:342
  115.3 0.9 shard_map.70
  116.2 1.9 %collective-permute-start.18 = (f32[1,128]{1,0:T(1,128)S(1)}, f32[1,128]{1,0:T(1,128)S(1)}, u32[]{:S(2)}, u32[]{:S(2)}) collective-permute-start(f32[1,128]{1,0:T(1,128)S(1)} %get-tuple-element.29), channel_id=1, source_target_pairs={{0,16},{16,0},{2,18},{18,2},{4,20},{20,4},{6,22},{22,6},{8,24},{24... | collective-permute-start | bytes 1544 | tf_op jit(solution)/shard_map/ppermute | solution.py:320
  118.1 5.5 %all-to-all-start.1 = ((f32[32,1,128]{2,1,0:T(1,128)}), f32[32,1,128]{2,1,0:T(1,128)S(1)}, u32[]{:S(2)}, u32[]{:S(2)}) async-start(f32[32,1,128]{2,1,0:T(1,128)} %get-tuple-element.30), calls=%async_computation.1 | async-start | bytes 32768 | tf_op jit(solution)/shard_map/all_to_all | solution.py:347
  124.2 8.4 %all-to-all-done.1 = f32[32,1,128]{2,1,0:T(1,128)S(1)} async-done(((f32[32,1,128]{2,1,0:T(1,128)}), f32[32,1,128]{2,1,0:T(1,128)S(1)}, u32[]{:S(2)}, u32[]{:S(2)}) %all-to-all-start.1) | async-done | bytes 16416 | tf_op jit(solution)/shard_map/all_to_all | solution.py:347
  (20 shorter events, 2.2 us)
Async XLA Ops:
  2.5 13.6 %collective-permute-start = (bf16[48,2048]{1,0:T(8,128)(2,1)}, bf16[48,2048]{1,0:T(8,128)(2,1)S(1)}, u32[]{:S(2)}, u32[]{:S(2)}) collective-permute-start(bf16[48,2048]{1,0:T(8,128)(2,1)} %get-tuple-element.18), channel_id=1, source_target_pairs={{0,16},{16,0},{2,18},{18,2},{4,20},{20,4},{6,22},{22,6},{8,24},{24... | collective-permute-start | bytes 589832 | tf_op jit(solution)/shard_map/ppermute | solution.py:320
  11.3 10.5 %collective-permute-start.2 = (bf16[48,2048]{1,0:T(8,128)(2,1)}, bf16[48,2048]{1,0:T(8,128)(2,1)S(1)}, u32[]{:S(2)}, u32[]{:S(2)}) collective-permute-start(bf16[48,2048]{1,0:T(8,128)(2,1)} %get-tuple-element.18), channel_id=1, source_target_pairs={{0,273},{16,1},{2,275},{18,3},{4,277},{20,5},{6,279},{22,7},{8,281... | collective-permute-start | bytes 589832 | tf_op jit(solution)/shard_map/ppermute | solution.py:324
  13.2 8.6 %collective-permute-start.1 = (bf16[48,2048]{1,0:T(8,128)(2,1)}, bf16[48,2048]{1,0:T(8,128)(2,1)S(1)}, u32[]{:S(2)}, u32[]{:S(2)}) collective-permute-start(bf16[48,2048]{1,0:T(8,128)(2,1)} %get-tuple-element.17), channel_id=1, source_target_pairs={{0,1},{16,273},{2,3},{18,275},{4,5},{20,277},{6,7},{22,279},{8,9},... | collective-permute-start | bytes 589832 | tf_op jit(solution)/shard_map/ppermute | solution.py:323
  21.9 14.2 %collective-permute-start.3 = (bf16[192,2048]{1,0:T(8,128)(2,1)S(1)}, bf16[192,2048]{1,0:T(8,128)(2,1)S(1)}, u32[]{:S(2)}, u32[]{:S(2)}) collective-permute-start(bf16[192,2048]{1,0:T(8,128)(2,1)S(1)} %constant_dynamic-update-slice_fusion.refs_0_), channel_id=1, source_target_pairs={{0,2},{16,48},{2,4},{18,50},{4,6},{20,52},{6,8},{22,54},{8,10},{24... | collective-permute-start | bytes 2359304 | tf_op jit(solution)/shard_map/ppermute | solution.py:331
  23.8 12.3 %collective-permute-start.5 = (bf16[192,2048]{1,0:T(8,128)(2,1)S(1)}, bf16[192,2048]{1,0:T(8,128)(2,1)S(1)}, u32[]{:S(2)}, u32[]{:S(2)}) collective-permute-start(bf16[192,2048]{1,0:T(8,128)(2,1)S(1)} %constant_dynamic-update-slice_fusion.refs_0_), channel_id=1, source_target_pairs={{0,16},{16,0},{2,18},{18,2},{4,20},{20,4},{6,22},{22,6},{8,24},{24... | collective-permute-start | bytes 2359304 | tf_op jit(solution)/shard_map/ppermute | solution.py:320
  25.7 17.6 %collective-permute-start.4 = (bf16[192,2048]{1,0:T(8,128)(2,1)S(1)}, bf16[192,2048]{1,0:T(8,128)(2,1)S(1)}, u32[]{:S(2)}, u32[]{:S(2)}) collective-permute-start(bf16[192,2048]{1,0:T(8,128)(2,1)S(1)} %constant_dynamic-update-slice_fusion.refs_0_), channel_id=1, source_target_pairs={{0,14},{16,240},{2,0},{18,242},{4,2},{20,244},{6,4},{22,246},{8,6}... | collective-permute-start | bytes 2359304 | tf_op jit(solution)/shard_map/ppermute | solution.py:331
  36.1 14.2 %collective-permute-start.6 = (bf16[192,2048]{1,0:T(8,128)(2,1)S(1)}, bf16[192,2048]{1,0:T(8,128)(2,1)S(1)}, u32[]{:S(2)}, u32[]{:S(2)}) collective-permute-start(bf16[192,2048]{1,0:T(8,128)(2,1)S(1)} %collective-permute-done.3.refs_1_), channel_id=1, source_target_pairs={{0,2},{16,48},{2,4},{18,50},{4,6},{20,52},{6,8},{22,54},{8,10},{24... | collective-permute-start | bytes 2359304 | tf_op jit(solution)/shard_map/ppermute | solution.py:331
  38.0 12.3 %collective-permute-start.8 = (bf16[192,2048]{1,0:T(8,128)(2,1)S(1)}, bf16[192,2048]{1,0:T(8,128)(2,1)S(1)}, u32[]{:S(2)}, u32[]{:S(2)}) collective-permute-start(bf16[192,2048]{1,0:T(8,128)(2,1)S(1)} %collective-permute-done.3.refs_1_), channel_id=1, source_target_pairs={{0,16},{16,0},{2,18},{18,2},{4,20},{20,4},{6,22},{22,6},{8,24},{24... | collective-permute-start | bytes 2359304 | tf_op jit(solution)/shard_map/ppermute | solution.py:320
  43.3 7.1 %collective-permute-start.9 = (bf16[192,2048]{1,0:T(8,128)(2,1)S(1)}, bf16[192,2048]{1,0:T(8,128)(2,1)S(1)}, u32[]{:S(2)}, u32[]{:S(2)}) collective-permute-start(bf16[192,2048]{1,0:T(8,128)(2,1)S(1)} %collective-permute-done.4.refs_2_), channel_id=1, source_target_pairs={{0,16},{16,0},{2,18},{18,2},{4,20},{20,4},{6,22},{22,6},{8,24},{24... | collective-permute-start | bytes 2359304 | tf_op jit(solution)/shard_map/ppermute | solution.py:320
  45.2 14.0 %collective-permute-start.7 = (bf16[192,2048]{1,0:T(8,128)(2,1)S(1)}, bf16[192,2048]{1,0:T(8,128)(2,1)S(1)}, u32[]{:S(2)}, u32[]{:S(2)}) collective-permute-start(bf16[192,2048]{1,0:T(8,128)(2,1)S(1)} %collective-permute-done.4.refs_2_), channel_id=1, source_target_pairs={{0,14},{16,240},{2,0},{18,242},{4,2},{20,244},{6,4},{22,246},{8,6}... | collective-permute-start | bytes 2359304 | tf_op jit(solution)/shard_map/ppermute | solution.py:331
  50.4 17.0 %collective-permute-start.10 = (bf16[192,2048]{1,0:T(8,128)(2,1)S(1)}, bf16[192,2048]{1,0:T(8,128)(2,1)S(1)}, u32[]{:S(2)}, u32[]{:S(2)}) collective-permute-start(bf16[192,2048]{1,0:T(8,128)(2,1)S(1)} %collective-permute-done.6.refs_3_), channel_id=1, source_target_pairs={{0,2},{16,48},{2,4},{18,50},{4,6},{20,52},{6,8},{22,54},{8,10},{24... | collective-permute-start | bytes 2359304 | tf_op jit(solution)/shard_map/ppermute | solution.py:331
  52.3 15.1 %collective-permute-start.12 = (bf16[192,2048]{1,0:T(8,128)(2,1)S(1)}, bf16[192,2048]{1,0:T(8,128)(2,1)S(1)}, u32[]{:S(2)}, u32[]{:S(2)}) collective-permute-start(bf16[192,2048]{1,0:T(8,128)(2,1)S(1)} %collective-permute-done.6.refs_3_), channel_id=1, source_target_pairs={{0,16},{16,0},{2,18},{18,2},{4,20},{20,4},{6,22},{22,6},{8,24},{24... | collective-permute-start | bytes 2359304 | tf_op jit(solution)/shard_map/ppermute | solution.py:320
  59.2 8.1 %collective-permute-start.13 = (bf16[192,2048]{1,0:T(8,128)(2,1)S(1)}, bf16[192,2048]{1,0:T(8,128)(2,1)S(1)}, u32[]{:S(2)}, u32[]{:S(2)}) collective-permute-start(bf16[192,2048]{1,0:T(8,128)(2,1)S(1)} %collective-permute-done.7.refs_4_), channel_id=1, source_target_pairs={{0,16},{16,0},{2,18},{18,2},{4,20},{20,4},{6,22},{22,6},{8,24},{24... | collective-permute-start | bytes 2359304 | tf_op jit(solution)/shard_map/ppermute | solution.py:320
  62.2 14.0 %collective-permute-start.11 = (bf16[192,2048]{1,0:T(8,128)(2,1)S(1)}, bf16[192,2048]{1,0:T(8,128)(2,1)S(1)}, u32[]{:S(2)}, u32[]{:S(2)}) collective-permute-start(bf16[192,2048]{1,0:T(8,128)(2,1)S(1)} %collective-permute-done.7.refs_4_), channel_id=1, source_target_pairs={{0,14},{16,240},{2,0},{18,242},{4,2},{20,244},{6,4},{22,246},{8,6}... | collective-permute-start | bytes 2359304 | tf_op jit(solution)/shard_map/ppermute | solution.py:331
  67.4 15.1 %collective-permute-start.14 = (bf16[192,2048]{1,0:T(8,128)(2,1)S(1)}, bf16[192,2048]{1,0:T(8,128)(2,1)S(1)}, u32[]{:S(2)}, u32[]{:S(2)}) collective-permute-start(bf16[192,2048]{1,0:T(8,128)(2,1)S(1)} %collective-permute-done.10.refs_5_), channel_id=1, source_target_pairs={{0,2},{16,48},{2,4},{18,50},{4,6},{20,52},{6,8},{22,54},{8,10},{24... | collective-permute-start | bytes 2359304 | tf_op jit(solution)/shard_map/ppermute | solution.py:336
  69.3 17.5 %collective-permute-start.15 = (bf16[192,2048]{1,0:T(8,128)(2,1)S(1)}, bf16[192,2048]{1,0:T(8,128)(2,1)S(1)}, u32[]{:S(2)}, u32[]{:S(2)}) collective-permute-start(bf16[192,2048]{1,0:T(8,128)(2,1)S(1)} %collective-permute-done.10.refs_5_), channel_id=1, source_target_pairs={{0,16},{16,0},{2,18},{18,2},{4,20},{20,4},{6,22},{22,6},{8,24},{24... | collective-permute-start | bytes 2359304 | tf_op jit(solution)/shard_map/ppermute | solution.py:320
  76.3 10.5 %collective-permute-start.16 = (bf16[192,2048]{1,0:T(8,128)(2,1)S(1)}, bf16[192,2048]{1,0:T(8,128)(2,1)S(1)}, u32[]{:S(2)}, u32[]{:S(2)}) collective-permute-start(bf16[192,2048]{1,0:T(8,128)(2,1)S(1)} %collective-permute-done.11.refs_6_), channel_id=1, source_target_pairs={{0,16},{16,0},{2,18},{18,2},{4,20},{20,4},{6,22},{22,6},{8,24},{24... | collective-permute-start | bytes 2359304 | tf_op jit(solution)/shard_map/ppermute | solution.py:320
  82.5 6.0 %collective-permute-start.17 = (bf16[192,2048]{1,0:T(8,128)(2,1)S(1)}, bf16[192,2048]{1,0:T(8,128)(2,1)S(1)}, u32[]{:S(2)}, u32[]{:S(2)}) collective-permute-start(bf16[192,2048]{1,0:T(8,128)(2,1)S(1)} %collective-permute-done.14.refs_7_), channel_id=1, source_target_pairs={{0,16},{16,0},{2,18},{18,2},{4,20},{20,4},{6,22},{22,6},{8,24},{24... | collective-permute-start | bytes 2359304 | tf_op jit(solution)/shard_map/ppermute | solution.py:320
  96.4 18.9 %all-to-all-start = ((f32[16,6,8,128]{3,2,1,0:T(8,128)}), f32[16,6,8,128]{3,2,1,0:T(8,128)S(1)}, u32[]{:S(2)}, u32[]{:S(2)}) async-start(f32[16,6,8,128]{3,2,1,0:T(8,128)} %shard_map.69), calls=%async_computation | async-start | bytes 786432 | tf_op jit(solution)/shard_map/all_to_all | solution.py:342
  116.2 7.4 %collective-permute-start.18 = (f32[1,128]{1,0:T(1,128)S(1)}, f32[1,128]{1,0:T(1,128)S(1)}, u32[]{:S(2)}, u32[]{:S(2)}) collective-permute-start(f32[1,128]{1,0:T(1,128)S(1)} %get-tuple-element.29), channel_id=1, source_target_pairs={{0,16},{16,0},{2,18},{18,2},{4,20},{20,4},{6,22},{22,6},{8,24},{24... | collective-permute-start | bytes 1544 | tf_op jit(solution)/shard_map/ppermute | solution.py:320
  118.1 14.5 %all-to-all-start.1 = ((f32[32,1,128]{2,1,0:T(1,128)}), f32[32,1,128]{2,1,0:T(1,128)S(1)}, u32[]{:S(2)}, u32[]{:S(2)}) async-start(f32[32,1,128]{2,1,0:T(1,128)} %get-tuple-element.30), calls=%async_computation.1 | async-start | bytes 32768 | tf_op jit(solution)/shard_map/all_to_all | solution.py:347

commit v4 on v3

--- a/solution.py
+++ b/solution.py
@@ -14,6 +14,7 @@
 SHARD = 48
 CHUNK = 256
 BLOCK = 128
+ORDER = (((0, 7, 1), 0), ((0, 7, 1), 1), ((6, 2), 0), ((6, 2), 1), ((5, 3, 4), 0), ((5, 3, 4), 1))
 
 
 def place(x, y, z, c):
@@ -31,9 +32,6 @@
 CORE_PAIRS = [(place(x, y, z, c), place(x, y, z, 1 - c)) for x, y, z, c in everywhere()]
 X_PAIRS = [
     (place(x, y, z, c), place(x ^ 1 if c == 0 else 3 - x, y, z, c)) for x, y, z, c in everywhere()
-]
-X_CROSS = [
-    (place(x, y, z, c), place(x ^ 1 if c == 1 else 3 - x, y, z, 1 - c)) for x, y, z, c in everywhere()
 ]
 UP, DOWN = (
     [
@@ -104,6 +102,10 @@
         scratch_shapes=[pltpu.SemaphoreType.DMA((6,))],
         compiler_params=pltpu.CompilerParams(vmem_limit_bytes=60 * 1024 * 1024),
     )(image_s, text_s, image_t, text_t)
+
+
+def total_rows(refs):
+    return sum(ref.shape[0] for ref in refs)
 
 
 def piece(refs, start, stop, low, high):
@@ -164,7 +166,7 @@
 def early_kernel(ds, dt, units, *refs):
     own, other = refs[:units], refs[units : 2 * units]
     out, l, g = refs[2 * units :]
-    rows = units * 4 * SHARD
+    rows = total_rows(own)
     chunks = rows // CHUNK
 
     def multiply(j):
@@ -179,7 +181,7 @@
 
 
 def early(own, other, ds, dt):
-    rows = len(own) * 4 * SHARD
+    rows = total_rows(own)
     chunks = rows // CHUNK
     vmem = pl.BlockSpec(memory_space=pltpu.VMEM)
     work = rows * chunks * CHUNK
@@ -199,7 +201,7 @@
 def late_kernel(ds, dt, units, known, *refs):
     own, other = refs[:units], refs[units : 2 * units]
     before, out, l, g, ls, gs, stats = refs[2 * units :]
-    rows = units * 4 * SHARD
+    rows = total_rows(own)
     chunks = rows // CHUNK
     done = known // CHUNK
     line, xi = where_am_i()
@@ -229,9 +231,15 @@
     for n, v in enumerate(summary(ds, dt, l.at[(chunks - 1) % 2], g.at[(chunks - 1) % 2], rows, False)):
         stats[n : n + 1, slice(*lanes(chunks - 1))] = v
 
-    for k, step in enumerate((0, 7, 1, 6, 2, 5, 3, 4)):
-        v = stats[:4, k * 4 * SHARD : (k + 1) * 4 * SHARD]
-        v = jnp.where(xi == 0, v, jnp.concatenate([v[:, 2 * SHARD :], v[:, : 2 * SHARD]], axis=1))
+    places = {}
+    at = 0
+    for steps, partner in ORDER:
+        for step in steps:
+            places[step, partner] = at
+            at += 2 * SHARD
+    for step in range(8):
+        mine, across = (stats[:4, places[step, p] : places[step, p] + 2 * SHARD] for p in (0, 1))
+        v = jnp.concatenate([jnp.where(xi == 0, mine, across), jnp.where(xi == 0, across, mine)], axis=1)
         row = pl.ds(lax.rem(line + step, 8), 1)
         for n in range(4):
             out[0, n, row, :] = v[n : n + 1, :128]
@@ -241,7 +249,7 @@
 
 
 def late(own, other, before, known, ds, dt):
-    rows = len(own) * 4 * SHARD
+    rows = total_rows(own)
     chunks, done = rows // CHUNK, known // CHUNK
     vmem = pl.BlockSpec(memory_space=pltpu.VMEM)
     work = rows * rows - known * done * CHUNK
@@ -320,25 +328,35 @@
         return lax.ppermute(v, AXES, CORE_PAIRS)
 
     mine, theirs = pack(image_student, text_student, image_teacher, text_teacher)
-    across = lax.ppermute(mine, AXES, X_PAIRS)
-    beyond = lax.ppermute(theirs, AXES, X_CROSS)
-    pair = jnp.concatenate([mine, swap(theirs), across, beyond], axis=0)
-    own, other = [pair], []
-    ready, sent, up, down = [pair], [], pair, pair
+    def pass_on(v):
+        return lax.ppermute(v, AXES, X_PAIRS)
+
+    def joined(*v):
+        return jnp.concatenate(v, axis=0)
+
+    def after(v, *others):
+        return lax.optimization_barrier((v, others))[0]
+
+    chip = joined(mine, swap(theirs))
+    up, down = [chip], [chip]
     for _ in range(3):
-        up, sent = lax.optimization_barrier((up, sent))
-        other += sent
-        up, down = lax.ppermute(up, AXES, UP), lax.ppermute(down, AXES, DOWN)
-        sent = [swap(v) for v in ready]
-        ready = [up, down]
-        own += ready
-    up, sent = lax.optimization_barrier((up, sent))
-    last = lax.ppermute(up, AXES, UP)
-    other += sent
-    before, last = lax.optimization_barrier((early(own[:5], other[:5], ds, dt), last))
-    known = 5 * pair.shape[0]
-    other += [swap(v) for v in ready + [last]]
-    stats = late(own + [last], other, before, known, ds, dt)
+        up.append(lax.ppermute(up[-1], AXES, UP))
+        down.append(lax.ppermute(down[-1], AXES, DOWN))
+    near = joined(chip, up[1], down[1])
+    near_across = pass_on(near)
+    middle = after(joined(up[2], down[2]), near_across)
+    middle_across = pass_on(middle)
+    last = lax.ppermute(up[3], AXES, UP)
+    end = after(joined(up[3], down[3], last), middle_across)
+    end_across = pass_on(end)
+    own = [near, near_across, middle, middle_across]
+    known = total_rows(own)
+    other = [swap(v) for v in own]
+    before = early(own, other, ds, dt)
+    end_other = swap(end)
+    own += [end, end_across]
+    other += [end_other, swap(after(end_across, before, end_other))]
+    stats = late(own, other, before, known, ds, dt)
     parts = lax.all_to_all(stats, AXES, 0, 0, axis_index_groups=STAT_GROUPS)
     chip, total = finish(parts)
     first, second = chip[0, :SHARD], swap(chip)[0, SHARD : 2 * SHARD]

time: 136 us -> 136 us (level)
  starting transfers between devices: 79 us -> 72.9 us
  waiting for transfers between devices: 37.3 us -> 42.9 us
    ppermute x10 -> x8, starting transfers between devices: 40.3 us -> 27.6 us  [swap(): return lax.ppermute(v, AXES, CORE_PAIRS)]
    ppermute x9 -> x10, starting transfers between devices: 26.3 us -> 30.9 us  [the longest x3 14.9 us: shards(): down.append(lax.ppermute(down[-1], AXES, DOWN))]
    ppermute x10 -> x8, waiting for transfers between devices: 1.71 us -> 4.57 us  [swap(): return lax.ppermute(v, AXES, CORE_PAIRS)]
    ppermute x9 -> x10, waiting for transfers between devices: 15.2 us -> 18 us  [the longest x3 7.04 us: shards(): up.append(lax.ppermute(up[-1], AXES, UP))]
    all_to_all x1, starting transfers between devices: 6.92 us -> 8.45 us  [shards(): parts = lax.all_to_all(stats, AXES, 0, 0, axis_index_groups=STAT_GROUPS)]
  transfers between devices with their start and end apart: 21 -> 20, of which waited for: 7 -> 11; matrix products, arithmetic and copies ran while one was open for 1% -> 1% of each run, Pallas kernels for 2% -> 2%
where the time goes in v4:
time: 136 us; the launch traced here: 135 us
  starting transfers between devices  72.9 us (54%)
  waiting for transfers between devices  42.9 us (32%)
  Pallas kernels  13.9 us (10%)
  between operations  2.71 us (2%)
  other arithmetic  1.37 us (1%)
    ppermute x8, starting transfers between devices, swap(): return lax.ppermute(v, AXES, CORE_PAIRS)  27.6 us
    ppermute x3, starting transfers between devices, shards(): down.append(lax.ppermute(down[-1], AXES, DOWN))  14.9 us
    all_to_all x1, waiting for transfers between devices, shards(): parts = lax.all_to_all(stats, AXES, 0, 0, axis_index_groups=STAT_GROUPS)  12 us
    all_to_all x1, starting transfers between devices, shards(): parts = lax.all_to_all(stats, AXES, 0, 0, axis_index_groups=STAT_GROUPS)  8.45 us
    all_to_all x1, waiting for transfers between devices, shards(): totals = lax.all_to_all(total, AXES, 0, 0, axis_index_groups=SUM_GROUPS)  8.44 us
    ppermute x3, starting transfers between devices, pass_on(): return lax.ppermute(v, AXES, X_PAIRS)  8.41 us
    pallas_call x1, Pallas kernels, late(): pl.pallas_call(functools.partial(late_kernel, ds, dt, len(own), known), o...  7.87 us
    ppermute x3, waiting for transfers between devices, shards(): up.append(lax.ppermute(up[-1], AXES, UP))  7.04 us
  transfers between devices with their start and end apart: 20, of which 11 were waited for; matrix products, arithmetic and copies ran while one was open for 1% of the time, Pallas kernels for 2%

profile of v4, /device:TPU:1, one launch (start us, length us, event | category | flops | bytes accessed | tf_op | source)
XLA Modules:
  0.0 134.8 jit_solution(13539828560877984172)
XLA Ops:
  0.6 1.9 %shard_map.67 = (bf16[48,2048]{1,0:T(8,128)(2,1)}, bf16[48,2048]{1,0:T(8,128)(2,1)}) custom-call(bf16[48,512]{1,0:T(8,128)(2,1)} %image_s.1, bf16[48,512]{1,0:T(8,128)(2,1)} %text_s.1, bf16[48,768]{1,0:T(8,128)(2,1)} %image_t.1, bf16[48,768]{1,0:T(8,128)(2,1)} %text_t.1), custom_call_target="tpu_custom_call" | custom-call | tf_op jit(solution)/shard_map/pallas_call | solution.py:97
  2.5 8.8 %collective-permute-start = (bf16[48,2048]{1,0:T(8,128)(2,1)}, bf16[48,2048]{1,0:T(8,128)(2,1)S(1)}, u32[]{:S(2)}, u32[]{:S(2)}) collective-permute-start(bf16[48,2048]{1,0:T(8,128)(2,1)} %get-tuple-element.11), channel_id=1, source_target_pairs={{0,16},{16,0},{2,18},{18,2},{4,20},{20,4},{6,22},{22,6},{8,24},{24... | collective-permute-start | bytes 589832 | tf_op jit(solution)/shard_map/ppermute | solution.py:328
  12.6 1.9 %collective-permute-start.1 = (bf16[96,2048]{1,0:T(8,128)(2,1)S(1)}, bf16[96,2048]{1,0:T(8,128)(2,1)S(1)}, u32[]{:S(2)}, u32[]{:S(2)}) collective-permute-start(bf16[96,2048]{1,0:T(8,128)(2,1)S(1)} %get-tuple-element.17), channel_id=1, source_target_pairs={{0,2},{16,48},{2,4},{18,50},{4,6},{20,52},{6,8},{22,54},{8,10},{24... | collective-permute-start | bytes 1179656 | tf_op jit(solution)/shard_map/ppermute | solution.py:343
  14.5 4.6 %collective-permute-start.2 = (bf16[96,2048]{1,0:T(8,128)(2,1)S(1)}, bf16[96,2048]{1,0:T(8,128)(2,1)S(1)}, u32[]{:S(2)}, u32[]{:S(2)}) collective-permute-start(bf16[96,2048]{1,0:T(8,128)(2,1)S(1)} %get-tuple-element.17), channel_id=1, source_target_pairs={{0,14},{16,240},{2,0},{18,242},{4,2},{20,244},{6,4},{22,246},{8,6}... | collective-permute-start | bytes 1179656 | tf_op jit(solution)/shard_map/ppermute | solution.py:344
  19.1 3.5 %collective-permute-done.1 = bf16[96,2048]{1,0:T(8,128)(2,1)S(1)} collective-permute-done((bf16[96,2048]{1,0:T(8,128)(2,1)S(1)}, bf16[96,2048]{1,0:T(8,128)(2,1)S(1)}, u32[]{:S(2)}, u32[]{:S(2)}) %collective-permute-start.1) | collective-permute-done | bytes 393248 | tf_op jit(solution)/shard_map/ppermute | solution.py:343
  22.6 1.2 collective-permute-done.2
  23.8 1.9 %collective-permute-start.3 = (bf16[288,2048]{1,0:T(8,128)(2,1)S(1)}, bf16[288,2048]{1,0:T(8,128)(2,1)S(1)}, u32[]{:S(2)}, u32[]{:S(2)}) collective-permute-start(bf16[288,2048]{1,0:T(8,128)(2,1)S(1)} %constant_dynamic-update-slice_fusion.2.refs_0_), channel_id=1, source_target_pairs={{0,1},{16,273},{2,3},{18,275},{4,5},{20,277},{6,7},{22,279},{8,9},... | collective-permute-start | bytes 3538952 | tf_op jit(solution)/shard_map/ppermute | solution.py:332
  25.8 1.9 %collective-permute-start.4 = (bf16[96,2048]{1,0:T(8,128)(2,1)S(1)}, bf16[96,2048]{1,0:T(8,128)(2,1)S(1)}, u32[]{:S(2)}, u32[]{:S(2)}) collective-permute-start(bf16[96,2048]{1,0:T(8,128)(2,1)S(1)} %collective-permute-done.1), channel_id=1, source_target_pairs={{0,2},{16,48},{2,4},{18,50},{4,6},{20,52},{6,8},{22,54},{8,10},{24... | collective-permute-start | bytes 1179656 | tf_op jit(solution)/shard_map/ppermute | solution.py:343
  27.7 5.2 %collective-permute-start.5 = (bf16[96,2048]{1,0:T(8,128)(2,1)S(1)}, bf16[96,2048]{1,0:T(8,128)(2,1)S(1)}, u32[]{:S(2)}, u32[]{:S(2)}) collective-permute-start(bf16[96,2048]{1,0:T(8,128)(2,1)S(1)} %collective-permute-done.2), channel_id=1, source_target_pairs={{0,14},{16,240},{2,0},{18,242},{4,2},{20,244},{6,4},{22,246},{8,6}... | collective-permute-start | bytes 1179656 | tf_op jit(solution)/shard_map/ppermute | solution.py:344
  32.9 3.5 %collective-permute-done.4 = bf16[96,2048]{1,0:T(8,128)(2,1)S(1)} collective-permute-done((bf16[96,2048]{1,0:T(8,128)(2,1)S(1)}, bf16[96,2048]{1,0:T(8,128)(2,1)S(1)}, u32[]{:S(2)}, u32[]{:S(2)}) %collective-permute-start.4) | collective-permute-done | bytes 393248 | tf_op jit(solution)/shard_map/ppermute | solution.py:343
  36.4 1.9 %collective-permute-start.7 = (bf16[96,2048]{1,0:T(8,128)(2,1)S(1)}, bf16[96,2048]{1,0:T(8,128)(2,1)S(1)}, u32[]{:S(2)}, u32[]{:S(2)}) collective-permute-start(bf16[96,2048]{1,0:T(8,128)(2,1)S(1)} %collective-permute-done.4), channel_id=1, source_target_pairs={{0,2},{16,48},{2,4},{18,50},{4,6},{20,52},{6,8},{22,54},{8,10},{24... | collective-permute-start | bytes 1179656 | tf_op jit(solution)/shard_map/ppermute | solution.py:343
  38.3 6.0 %collective-permute-start.11 = (bf16[288,2048]{1,0:T(8,128)(2,1)S(1)}, bf16[288,2048]{1,0:T(8,128)(2,1)S(1)}, u32[]{:S(2)}, u32[]{:S(2)}) collective-permute-start(bf16[288,2048]{1,0:T(8,128)(2,1)S(1)} %constant_dynamic-update-slice_fusion.2.refs_0_), channel_id=1, source_target_pairs={{0,16},{16,0},{2,18},{18,2},{4,20},{20,4},{6,22},{22,6},{8,24},{24... | collective-permute-start | bytes 3538952 | tf_op jit(solution)/shard_map/ppermute | solution.py:328
  44.4 3.7 %collective-permute-start.6 = (bf16[192,2048]{1,0:T(8,128)(2,1)S(1)}, bf16[192,2048]{1,0:T(8,128)(2,1)S(1)}, u32[]{:S(2)}, u32[]{:S(2)}) collective-permute-start(bf16[192,2048]{1,0:T(8,128)(2,1)S(1)} %pad_maximum_fusion.1.refs_2_), channel_id=1, source_target_pairs={{0,1},{16,273},{2,3},{18,275},{4,5},{20,277},{6,7},{22,279},{8,9},... | collective-permute-start | bytes 2359304 | tf_op jit(solution)/shard_map/ppermute | solution.py:332
  48.2 5.1 %collective-permute-start.8 = (bf16[96,2048]{1,0:T(8,128)(2,1)S(1)}, bf16[96,2048]{1,0:T(8,128)(2,1)S(1)}, u32[]{:S(2)}, u32[]{:S(2)}) collective-permute-start(bf16[96,2048]{1,0:T(8,128)(2,1)S(1)} %collective-permute-done.5), channel_id=1, source_target_pairs={{0,14},{16,240},{2,0},{18,242},{4,2},{20,244},{6,4},{22,246},{8,6}... | collective-permute-start | bytes 1179656 | tf_op jit(solution)/shard_map/ppermute | solution.py:344
  53.3 1.9 %collective-permute-start.9 = (bf16[96,2048]{1,0:T(8,128)(2,1)S(1)}, bf16[96,2048]{1,0:T(8,128)(2,1)S(1)}, u32[]{:S(2)}, u32[]{:S(2)}) collective-permute-start(bf16[96,2048]{1,0:T(8,128)(2,1)S(1)} %collective-permute-done.7), channel_id=1, source_target_pairs={{0,2},{16,48},{2,4},{18,50},{4,6},{20,52},{6,8},{22,54},{8,10},{24... | collective-permute-start | bytes 1179656 | tf_op jit(solution)/shard_map/ppermute | solution.py:349
  55.2 1.9 %collective-permute-start.12 = (bf16[288,2048]{1,0:T(8,128)(2,1)S(1)}, bf16[288,2048]{1,0:T(8,128)(2,1)S(1)}, u32[]{:S(2)}, u32[]{:S(2)}) collective-permute-start(bf16[288,2048]{1,0:T(8,128)(2,1)S(1)} %collective-permute-done.3.refs_1_), channel_id=1, source_target_pairs={{0,16},{16,0},{2,18},{18,2},{4,20},{20,4},{6,22},{22,6},{8,24},{24... | collective-permute-start | bytes 3538952 | tf_op jit(solution)/shard_map/ppermute | solution.py:328
  58.0 5.3 %collective-permute-done.9 = bf16[96,2048]{1,0:T(8,128)(2,1)S(1)} collective-permute-done((bf16[96,2048]{1,0:T(8,128)(2,1)S(1)}, bf16[96,2048]{1,0:T(8,128)(2,1)S(1)}, u32[]{:S(2)}, u32[]{:S(2)}) %collective-permute-start.9) | collective-permute-done | bytes 393248 | tf_op jit(solution)/shard_map/ppermute | solution.py:349
  63.4 2.8 %collective-permute-start.10 = (bf16[288,2048]{1,0:T(8,128)(2,1)S(1)}, bf16[288,2048]{1,0:T(8,128)(2,1)S(1)}, u32[]{:S(2)}, u32[]{:S(2)}) collective-permute-start(bf16[288,2048]{1,0:T(8,128)(2,1)S(1)} %pad_maximum_fusion.refs_4_), channel_id=1, source_target_pairs={{0,1},{16,273},{2,3},{18,275},{4,5},{20,277},{6,7},{22,279},{8,9},... | collective-permute-start | bytes 3538952 | tf_op jit(solution)/shard_map/ppermute | solution.py:332
  66.2 2.2 %collective-permute-start.15 = (bf16[288,2048]{1,0:T(8,128)(2,1)S(1)}, bf16[288,2048]{1,0:T(8,128)(2,1)S(1)}, u32[]{:S(2)}, u32[]{:S(2)}) collective-permute-start(bf16[288,2048]{1,0:T(8,128)(2,1)S(1)} %pad_maximum_fusion.refs_4_), channel_id=1, source_target_pairs={{0,16},{16,0},{2,18},{18,2},{4,20},{20,4},{6,22},{22,6},{8,24},{24... | collective-permute-start | bytes 3538952 | tf_op jit(solution)/shard_map/ppermute | solution.py:328
  68.4 2.2 %collective-permute-start.13 = (bf16[192,2048]{1,0:T(8,128)(2,1)S(1)}, bf16[192,2048]{1,0:T(8,128)(2,1)S(1)}, u32[]{:S(2)}, u32[]{:S(2)}) collective-permute-start(bf16[192,2048]{1,0:T(8,128)(2,1)S(1)} %pad_maximum_fusion.1.refs_2_), channel_id=1, source_target_pairs={{0,16},{16,0},{2,18},{18,2},{4,20},{20,4},{6,22},{22,6},{8,24},{24... | collective-permute-start | bytes 2359304 | tf_op jit(solution)/shard_map/ppermute | solution.py:328
  70.6 2.2 %collective-permute-start.14 = (bf16[192,2048]{1,0:T(8,128)(2,1)S(1)}, bf16[192,2048]{1,0:T(8,128)(2,1)S(1)}, u32[]{:S(2)}, u32[]{:S(2)}) collective-permute-start(bf16[192,2048]{1,0:T(8,128)(2,1)S(1)} %collective-permute-done.6.refs_3_), channel_id=1, source_target_pairs={{0,16},{16,0},{2,18},{18,2},{4,20},{20,4},{6,22},{22,6},{8,24},{24... | collective-permute-start | bytes 2359304 | tf_op jit(solution)/shard_map/ppermute | solution.py:328
  72.8 2.0 %collective-permute-done.14.refs_7_.refs_9_ = bf16[192,2048]{1,0:T(8,128)(2,1)S(1)} collective-permute-done((bf16[192,2048]{1,0:T(8,128)(2,1)S(1)}, bf16[192,2048]{1,0:T(8,128)(2,1)S(1)}, u32[]{:S(2)}, u32[]{:S(2)}) %collective-permute-start.14) | collective-permute-done | bytes 786464 | tf_op jit(solution)/shard_map/ppermute | solution.py:328
  74.7 3.2 %shard_map.68.refs_12_ = f32[8,768]{1,0:T(8,128)S(1)} custom-call(bf16[288,2048]{1,0:T(8,128)(2,1)S(1)} %constant_dynamic-update-slice_fusion.2.refs_0_, bf16[288,2048]{1,0:T(8,128)(2,1)S(1)} %collective-permute-done.3.refs_1_, bf16[192,2048]{1,0:T(8,128)(2,1)S(1)} %pad_maximum_fusion.1.refs_2_, bf16[192,2048]{1,0:T(8,128)(2,1)S(1)} %collective-permute-done.6.refs_3_, ...), custom_call_target="tpu_custom_call" | custom-call | flops 1887436800 | bytes 9830400 | tf_op jit(solution)/shard_map/pallas_call | solution.py:188
  78.0 3.6 %collective-permute-done.10.refs_5_ = bf16[288,2048]{1,0:T(8,128)(2,1)S(1)} collective-permute-done((bf16[288,2048]{1,0:T(8,128)(2,1)S(1)}, bf16[288,2048]{1,0:T(8,128)(2,1)S(1)}, u32[]{:S(2)}, u32[]{:S(2)}) %collective-permute-start.10) | collective-permute-done | bytes 1179680 | tf_op jit(solution)/shard_map/ppermute | solution.py:332
  81.6 2.5 %collective-permute-start.16 = (bf16[288,2048]{1,0:T(8,128)(2,1)S(1)}, bf16[288,2048]{1,0:T(8,128)(2,1)S(1)}, u32[]{:S(2)}, u32[]{:S(2)}) collective-permute-start(bf16[288,2048]{1,0:T(8,128)(2,1)S(1)} %collective-permute-done.10.refs_5_), channel_id=1, source_target_pairs={{0,16},{16,0},{2,18},{18,2},{4,20},{20,4},{6,22},{22,6},{8,24},{24... | collective-permute-start | bytes 3538952 | tf_op jit(solution)/shard_map/ppermute | solution.py:328
  84.1 2.3 %collective-permute-done.16.refs_11_ = bf16[288,2048]{1,0:T(8,128)(2,1)S(1)} collective-permute-done((bf16[288,2048]{1,0:T(8,128)(2,1)S(1)}, bf16[288,2048]{1,0:T(8,128)(2,1)S(1)}, u32[]{:S(2)}, u32[]{:S(2)}) %collective-permute-start.16) | collective-permute-done | bytes 1179680 | tf_op jit(solution)/shard_map/ppermute | solution.py:328
  86.3 7.9 %shard_map.69 = f32[16,6,8,128]{3,2,1,0:T(8,128)} custom-call(bf16[288,2048]{1,0:T(8,128)(2,1)S(1)} %constant_dynamic-update-slice_fusion.2.refs_0_, bf16[288,2048]{1,0:T(8,128)(2,1)S(1)} %collective-permute-done.3.refs_1_, bf16[192,2048]{1,0:T(8,128)(2,1)S(1)} %pad_maximum_fusion.1.refs_2_, bf16[192,2048]{1,0:T(8,128)(2,1)S(1)} %collective-permute-done.6.refs_3_, ...), custom_call_target="tpu_custom_call" | custom-call | flops 4152360960 | bytes 15728640 | tf_op jit(solution)/shard_map/pallas_call | solution.py:256
  94.2 8.5 %all-to-all-start = ((f32[16,6,8,128]{3,2,1,0:T(8,128)}), f32[16,6,8,128]{3,2,1,0:T(8,128)S(1)}, u32[]{:S(2)}, u32[]{:S(2)}) async-start(f32[16,6,8,128]{3,2,1,0:T(8,128)} %shard_map.69), calls=%async_computation | async-start | bytes 786432 | tf_op jit(solution)/shard_map/all_to_all | solution.py:360
  102.7 12.0 %all-to-all-done.parts = f32[16,6,8,128]{3,2,1,0:T(8,128)S(1)} async-done(((f32[16,6,8,128]{3,2,1,0:T(8,128)}), f32[16,6,8,128]{3,2,1,0:T(8,128)S(1)}, u32[]{:S(2)}, u32[]{:S(2)}) %all-to-all-start) | async-done | bytes 393248 | tf_op jit(solution)/shard_map/all_to_all | solution.py:360
  115.5 1.9 %collective-permute-start.17 = (f32[1,128]{1,0:T(1,128)S(1)}, f32[1,128]{1,0:T(1,128)S(1)}, u32[]{:S(2)}, u32[]{:S(2)}) collective-permute-start(f32[1,128]{1,0:T(1,128)S(1)} %get-tuple-element.15), channel_id=1, source_target_pairs={{0,16},{16,0},{2,18},{18,2},{4,20},{20,4},{6,22},{22,6},{8,24},{24... | collective-permute-start | bytes 1544 | tf_op jit(solution)/shard_map/ppermute | solution.py:328
  117.5 5.9 %all-to-all-start.1 = ((f32[32,1,128]{2,1,0:T(1,128)}), f32[32,1,128]{2,1,0:T(1,128)S(1)}, u32[]{:S(2)}, u32[]{:S(2)}) async-start(f32[32,1,128]{2,1,0:T(1,128)} %get-tuple-element.16), calls=%async_computation.1 | async-start | bytes 32768 | tf_op jit(solution)/shard_map/all_to_all | solution.py:365
  123.9 8.4 %all-to-all-done.1 = f32[32,1,128]{2,1,0:T(1,128)S(1)} async-done(((f32[32,1,128]{2,1,0:T(1,128)}), f32[32,1,128]{2,1,0:T(1,128)S(1)}, u32[]{:S(2)}, u32[]{:S(2)}) %all-to-all-start.1) | async-done | bytes 16416 | tf_op jit(solution)/shard_map/all_to_all | solution.py:365
  (20 shorter events, 4.5 us)
Async XLA Ops:
  2.5 10.1 %collective-permute-start = (bf16[48,2048]{1,0:T(8,128)(2,1)}, bf16[48,2048]{1,0:T(8,128)(2,1)S(1)}, u32[]{:S(2)}, u32[]{:S(2)}) collective-permute-start(bf16[48,2048]{1,0:T(8,128)(2,1)} %get-tuple-element.11), channel_id=1, source_target_pairs={{0,16},{16,0},{2,18},{18,2},{4,20},{20,4},{6,22},{22,6},{8,24},{24... | collective-permute-start | bytes 589832 | tf_op jit(solution)/shard_map/ppermute | solution.py:328
  12.6 10.0 %collective-permute-start.1 = (bf16[96,2048]{1,0:T(8,128)(2,1)S(1)}, bf16[96,2048]{1,0:T(8,128)(2,1)S(1)}, u32[]{:S(2)}, u32[]{:S(2)}) collective-permute-start(bf16[96,2048]{1,0:T(8,128)(2,1)S(1)} %get-tuple-element.17), channel_id=1, source_target_pairs={{0,2},{16,48},{2,4},{18,50},{4,6},{20,52},{6,8},{22,54},{8,10},{24... | collective-permute-start | bytes 1179656 | tf_op jit(solution)/shard_map/ppermute | solution.py:343
  14.5 9.3 %collective-permute-start.2 = (bf16[96,2048]{1,0:T(8,128)(2,1)S(1)}, bf16[96,2048]{1,0:T(8,128)(2,1)S(1)}, u32[]{:S(2)}, u32[]{:S(2)}) collective-permute-start(bf16[96,2048]{1,0:T(8,128)(2,1)S(1)} %get-tuple-element.17), channel_id=1, source_target_pairs={{0,14},{16,240},{2,0},{18,242},{4,2},{20,244},{6,4},{22,246},{8,6}... | collective-permute-start | bytes 1179656 | tf_op jit(solution)/shard_map/ppermute | solution.py:344
  23.8 20.6 %collective-permute-start.3 = (bf16[288,2048]{1,0:T(8,128)(2,1)S(1)}, bf16[288,2048]{1,0:T(8,128)(2,1)S(1)}, u32[]{:S(2)}, u32[]{:S(2)}) collective-permute-start(bf16[288,2048]{1,0:T(8,128)(2,1)S(1)} %constant_dynamic-update-slice_fusion.2.refs_0_), channel_id=1, source_target_pairs={{0,1},{16,273},{2,3},{18,275},{4,5},{20,277},{6,7},{22,279},{8,9},... | collective-permute-start | bytes 3538952 | tf_op jit(solution)/shard_map/ppermute | solution.py:332
  25.8 10.6 %collective-permute-start.4 = (bf16[96,2048]{1,0:T(8,128)(2,1)S(1)}, bf16[96,2048]{1,0:T(8,128)(2,1)S(1)}, u32[]{:S(2)}, u32[]{:S(2)}) collective-permute-start(bf16[96,2048]{1,0:T(8,128)(2,1)S(1)} %collective-permute-done.1), channel_id=1, source_target_pairs={{0,2},{16,48},{2,4},{18,50},{4,6},{20,52},{6,8},{22,54},{8,10},{24... | collective-permute-start | bytes 1179656 | tf_op jit(solution)/shard_map/ppermute | solution.py:343
  27.7 16.7 %collective-permute-start.5 = (bf16[96,2048]{1,0:T(8,128)(2,1)S(1)}, bf16[96,2048]{1,0:T(8,128)(2,1)S(1)}, u32[]{:S(2)}, u32[]{:S(2)}) collective-permute-start(bf16[96,2048]{1,0:T(8,128)(2,1)S(1)} %collective-permute-done.2), channel_id=1, source_target_pairs={{0,14},{16,240},{2,0},{18,242},{4,2},{20,244},{6,4},{22,246},{8,6}... | collective-permute-start | bytes 1179656 | tf_op jit(solution)/shard_map/ppermute | solution.py:344
  36.4 16.9 %collective-permute-start.7 = (bf16[96,2048]{1,0:T(8,128)(2,1)S(1)}, bf16[96,2048]{1,0:T(8,128)(2,1)S(1)}, u32[]{:S(2)}, u32[]{:S(2)}) collective-permute-start(bf16[96,2048]{1,0:T(8,128)(2,1)S(1)} %collective-permute-done.4), channel_id=1, source_target_pairs={{0,2},{16,48},{2,4},{18,50},{4,6},{20,52},{6,8},{22,54},{8,10},{24... | collective-permute-start | bytes 1179656 | tf_op jit(solution)/shard_map/ppermute | solution.py:343
  38.3 32.2 %collective-permute-start.11 = (bf16[288,2048]{1,0:T(8,128)(2,1)S(1)}, bf16[288,2048]{1,0:T(8,128)(2,1)S(1)}, u32[]{:S(2)}, u32[]{:S(2)}) collective-permute-start(bf16[288,2048]{1,0:T(8,128)(2,1)S(1)} %constant_dynamic-update-slice_fusion.2.refs_0_), channel_id=1, source_target_pairs={{0,16},{16,0},{2,18},{18,2},{4,20},{20,4},{6,22},{22,6},{8,24},{24... | collective-permute-start | bytes 3538952 | tf_op jit(solution)/shard_map/ppermute | solution.py:328
  44.4 19.0 %collective-permute-start.6 = (bf16[192,2048]{1,0:T(8,128)(2,1)S(1)}, bf16[192,2048]{1,0:T(8,128)(2,1)S(1)}, u32[]{:S(2)}, u32[]{:S(2)}) collective-permute-start(bf16[192,2048]{1,0:T(8,128)(2,1)S(1)} %pad_maximum_fusion.1.refs_2_), channel_id=1, source_target_pairs={{0,1},{16,273},{2,3},{18,275},{4,5},{20,277},{6,7},{22,279},{8,9},... | collective-permute-start | bytes 2359304 | tf_op jit(solution)/shard_map/ppermute | solution.py:332
  48.2 9.8 %collective-permute-start.8 = (bf16[96,2048]{1,0:T(8,128)(2,1)S(1)}, bf16[96,2048]{1,0:T(8,128)(2,1)S(1)}, u32[]{:S(2)}, u32[]{:S(2)}) collective-permute-start(bf16[96,2048]{1,0:T(8,128)(2,1)S(1)} %collective-permute-done.5), channel_id=1, source_target_pairs={{0,14},{16,240},{2,0},{18,242},{4,2},{20,244},{6,4},{22,246},{8,6}... | collective-permute-start | bytes 1179656 | tf_op jit(solution)/shard_map/ppermute | solution.py:344
  53.3 10.0 %collective-permute-start.9 = (bf16[96,2048]{1,0:T(8,128)(2,1)S(1)}, bf16[96,2048]{1,0:T(8,128)(2,1)S(1)}, u32[]{:S(2)}, u32[]{:S(2)}) collective-permute-start(bf16[96,2048]{1,0:T(8,128)(2,1)S(1)} %collective-permute-done.7), channel_id=1, source_target_pairs={{0,2},{16,48},{2,4},{18,50},{4,6},{20,52},{6,8},{22,54},{8,10},{24... | collective-permute-start | bytes 1179656 | tf_op jit(solution)/shard_map/ppermute | solution.py:349
  55.2 17.5 %collective-permute-start.12 = (bf16[288,2048]{1,0:T(8,128)(2,1)S(1)}, bf16[288,2048]{1,0:T(8,128)(2,1)S(1)}, u32[]{:S(2)}, u32[]{:S(2)}) collective-permute-start(bf16[288,2048]{1,0:T(8,128)(2,1)S(1)} %collective-permute-done.3.refs_1_), channel_id=1, source_target_pairs={{0,16},{16,0},{2,18},{18,2},{4,20},{20,4},{6,22},{22,6},{8,24},{24... | collective-permute-start | bytes 3538952 | tf_op jit(solution)/shard_map/ppermute | solution.py:328
  63.4 18.2 %collective-permute-start.10 = (bf16[288,2048]{1,0:T(8,128)(2,1)S(1)}, bf16[288,2048]{1,0:T(8,128)(2,1)S(1)}, u32[]{:S(2)}, u32[]{:S(2)}) collective-permute-start(bf16[288,2048]{1,0:T(8,128)(2,1)S(1)} %pad_maximum_fusion.refs_4_), channel_id=1, source_target_pairs={{0,1},{16,273},{2,3},{18,275},{4,5},{20,277},{6,7},{22,279},{8,9},... | collective-permute-start | bytes 3538952 | tf_op jit(solution)/shard_map/ppermute | solution.py:332
  66.2 15.4 %collective-permute-start.15 = (bf16[288,2048]{1,0:T(8,128)(2,1)S(1)}, bf16[288,2048]{1,0:T(8,128)(2,1)S(1)}, u32[]{:S(2)}, u32[]{:S(2)}) collective-permute-start(bf16[288,2048]{1,0:T(8,128)(2,1)S(1)} %pad_maximum_fusion.refs_4_), channel_id=1, source_target_pairs={{0,16},{16,0},{2,18},{18,2},{4,20},{20,4},{6,22},{22,6},{8,24},{24... | collective-permute-start | bytes 3538952 | tf_op jit(solution)/shard_map/ppermute | solution.py:328
  68.4 4.4 %collective-permute-start.13 = (bf16[192,2048]{1,0:T(8,128)(2,1)S(1)}, bf16[192,2048]{1,0:T(8,128)(2,1)S(1)}, u32[]{:S(2)}, u32[]{:S(2)}) collective-permute-start(bf16[192,2048]{1,0:T(8,128)(2,1)S(1)} %pad_maximum_fusion.1.refs_2_), channel_id=1, source_target_pairs={{0,16},{16,0},{2,18},{18,2},{4,20},{20,4},{6,22},{22,6},{8,24},{24... | collective-permute-start | bytes 2359304 | tf_op jit(solution)/shard_map/ppermute | solution.py:328
  70.6 4.2 %collective-permute-start.14 = (bf16[192,2048]{1,0:T(8,128)(2,1)S(1)}, bf16[192,2048]{1,0:T(8,128)(2,1)S(1)}, u32[]{:S(2)}, u32[]{:S(2)}) collective-permute-start(bf16[192,2048]{1,0:T(8,128)(2,1)S(1)} %collective-permute-done.6.refs_3_), channel_id=1, source_target_pairs={{0,16},{16,0},{2,18},{18,2},{4,20},{20,4},{6,22},{22,6},{8,24},{24... | collective-permute-start | bytes 2359304 | tf_op jit(solution)/shard_map/ppermute | solution.py:328
  81.6 4.7 %collective-permute-start.16 = (bf16[288,2048]{1,0:T(8,128)(2,1)S(1)}, bf16[288,2048]{1,0:T(8,128)(2,1)S(1)}, u32[]{:S(2)}, u32[]{:S(2)}) collective-permute-start(bf16[288,2048]{1,0:T(8,128)(2,1)S(1)} %collective-permute-done.10.refs_5_), channel_id=1, source_target_pairs={{0,16},{16,0},{2,18},{18,2},{4,20},{20,4},{6,22},{22,6},{8,24},{24... | collective-permute-start | bytes 3538952 | tf_op jit(solution)/shard_map/ppermute | solution.py:328
  94.2 20.4 %all-to-all-start = ((f32[16,6,8,128]{3,2,1,0:T(8,128)}), f32[16,6,8,128]{3,2,1,0:T(8,128)S(1)}, u32[]{:S(2)}, u32[]{:S(2)}) async-start(f32[16,6,8,128]{3,2,1,0:T(8,128)} %shard_map.69), calls=%async_computation | async-start | bytes 786432 | tf_op jit(solution)/shard_map/all_to_all | solution.py:360
  115.5 7.8 %collective-permute-start.17 = (f32[1,128]{1,0:T(1,128)S(1)}, f32[1,128]{1,0:T(1,128)S(1)}, u32[]{:S(2)}, u32[]{:S(2)}) collective-permute-start(f32[1,128]{1,0:T(1,128)S(1)} %get-tuple-element.15), channel_id=1, source_target_pairs={{0,16},{16,0},{2,18},{18,2},{4,20},{20,4},{6,22},{22,6},{8,24},{24... | collective-permute-start | bytes 1544 | tf_op jit(solution)/shard_map/ppermute | solution.py:328
  117.5 14.9 %all-to-all-start.1 = ((f32[32,1,128]{2,1,0:T(1,128)}), f32[32,1,128]{2,1,0:T(1,128)S(1)}, u32[]{:S(2)}, u32[]{:S(2)}) async-start(f32[32,1,128]{2,1,0:T(1,128)} %get-tuple-element.16), calls=%async_computation.1 | async-start | bytes 32768 | tf_op jit(solution)/shard_map/all_to_all | solution.py:365

commit v5 on v4

--- a/solution.py
+++ b/solution.py
@@ -344,10 +344,10 @@
         down.append(lax.ppermute(down[-1], AXES, DOWN))
     near = joined(chip, up[1], down[1])
     near_across = pass_on(near)
-    middle = after(joined(up[2], down[2]), near_across)
+    middle = joined(up[2], down[2])
     middle_across = pass_on(middle)
     last = lax.ppermute(up[3], AXES, UP)
-    end = after(joined(up[3], down[3], last), middle_across)
+    end = after(joined(up[3], down[3], last), near_across, middle_across)
     end_across = pass_on(end)
     own = [near, near_across, middle, middle_across]
     known = total_rows(own)

time: 136 us -> 131 us (0.963)
  waiting for transfers between devices: 42.9 us -> 35.9 us
  starting transfers between devices: 72.9 us -> 75.5 us
    ppermute x3, waiting for transfers between devices: 7.04 us -> 3.52 us  [shards(): up.append(lax.ppermute(up[-1], AXES, UP))]
    ppermute x8, starting transfers between devices: 27.6 us -> 30 us  [swap(): return lax.ppermute(v, AXES, CORE_PAIRS)]
    ppermute x3, starting transfers between devices: 14.9 us -> 13 us  [shards(): down.append(lax.ppermute(down[-1], AXES, DOWN))]
    ppermute x3, waiting for transfers between devices: 3.62 us -> 1.92 us  [pass_on(): return lax.ppermute(v, AXES, X_PAIRS)]
    ppermute x3, waiting for transfers between devices: 1.99 us -> 0.54 us  [shards(): down.append(lax.ppermute(down[-1], AXES, DOWN))]
  transfers between devices with their start and end apart: 20 -> 20, of which waited for: 11 -> 9; matrix products, arithmetic and copies ran while one was open for 1% -> 1% of each run, Pallas kernels for 2% -> 2%
where the time goes in v5:
time: 131 us; the launch traced here: 130 us
  starting transfers between devices  75.5 us (58%)
  waiting for transfers between devices  35.9 us (27%)
  Pallas kernels  13.8 us (11%)
  between operations  2.72 us (2%)
  other arithmetic  1.32 us (1%)
    ppermute x8, starting transfers between devices, swap(): return lax.ppermute(v, AXES, CORE_PAIRS)  30 us
    ppermute x3, starting transfers between devices, shards(): down.append(lax.ppermute(down[-1], AXES, DOWN))  13 us
    all_to_all x1, waiting for transfers between devices, shards(): parts = lax.all_to_all(stats, AXES, 0, 0, axis_index_groups=STAT_GROUPS)  12 us
    all_to_all x1, starting transfers between devices, shards(): parts = lax.all_to_all(stats, AXES, 0, 0, axis_index_groups=STAT_GROUPS)  9.12 us
    ppermute x3, starting transfers between devices, pass_on(): return lax.ppermute(v, AXES, X_PAIRS)  9 us
    all_to_all x1, waiting for transfers between devices, shards(): totals = lax.all_to_all(total, AXES, 0, 0, axis_index_groups=SUM_GROUPS)  8.44 us
    pallas_call x1, Pallas kernels, late(): pl.pallas_call(functools.partial(late_kernel, ds, dt, len(own), known), o...  7.87 us
    ppermute x3, starting transfers between devices, shards(): up.append(lax.ppermute(up[-1], AXES, UP))  7.03 us
  transfers between devices with their start and end apart: 20, of which 9 were waited for; matrix products, arithmetic and copies ran while one was open for 1% of the time, Pallas kernels for 2%

profile of v5, /device:TPU:1, one launch (start us, length us, event | category | flops | bytes accessed | tf_op | source)
XLA Modules:
  0.0 130.4 jit_solution(8517651453406256856)
XLA Ops:
  0.6 1.9 %shard_map.67 = (bf16[48,2048]{1,0:T(8,128)(2,1)}, bf16[48,2048]{1,0:T(8,128)(2,1)}) custom-call(bf16[48,512]{1,0:T(8,128)(2,1)} %image_s.1, bf16[48,512]{1,0:T(8,128)(2,1)} %text_s.1, bf16[48,768]{1,0:T(8,128)(2,1)} %image_t.1, bf16[48,768]{1,0:T(8,128)(2,1)} %text_t.1), custom_call_target="tpu_custom_call" | custom-call | tf_op jit(solution)/shard_map/pallas_call | solution.py:97
  2.5 8.8 %collective-permute-start = (bf16[48,2048]{1,0:T(8,128)(2,1)}, bf16[48,2048]{1,0:T(8,128)(2,1)S(1)}, u32[]{:S(2)}, u32[]{:S(2)}) collective-permute-start(bf16[48,2048]{1,0:T(8,128)(2,1)} %get-tuple-element.10), channel_id=1, source_target_pairs={{0,16},{16,0},{2,18},{18,2},{4,20},{20,4},{6,22},{22,6},{8,24},{24... | collective-permute-start | bytes 589832 | tf_op jit(solution)/shard_map/ppermute | solution.py:328
  11.3 1.0 constant_dynamic-update-slice_fusion.1
  12.6 1.9 %collective-permute-start.1 = (bf16[96,2048]{1,0:T(8,128)(2,1)S(1)}, bf16[96,2048]{1,0:T(8,128)(2,1)S(1)}, u32[]{:S(2)}, u32[]{:S(2)}) collective-permute-start(bf16[96,2048]{1,0:T(8,128)(2,1)S(1)} %get-tuple-element.15), channel_id=1, source_target_pairs={{0,2},{16,48},{2,4},{18,50},{4,6},{20,52},{6,8},{22,54},{8,10},{24... | collective-permute-start | bytes 1179656 | tf_op jit(solution)/shard_map/ppermute | solution.py:343
  14.5 4.6 %collective-permute-start.2 = (bf16[96,2048]{1,0:T(8,128)(2,1)S(1)}, bf16[96,2048]{1,0:T(8,128)(2,1)S(1)}, u32[]{:S(2)}, u32[]{:S(2)}) collective-permute-start(bf16[96,2048]{1,0:T(8,128)(2,1)S(1)} %get-tuple-element.15), channel_id=1, source_target_pairs={{0,14},{16,240},{2,0},{18,242},{4,2},{20,244},{6,4},{22,246},{8,6}... | collective-permute-start | bytes 1179656 | tf_op jit(solution)/shard_map/ppermute | solution.py:344
  19.1 3.5 %collective-permute-done.1 = bf16[96,2048]{1,0:T(8,128)(2,1)S(1)} collective-permute-done((bf16[96,2048]{1,0:T(8,128)(2,1)S(1)}, bf16[96,2048]{1,0:T(8,128)(2,1)S(1)}, u32[]{:S(2)}, u32[]{:S(2)}) %collective-permute-start.1) | collective-permute-done | bytes 393248 | tf_op jit(solution)/shard_map/ppermute | solution.py:343
  22.6 1.9 %collective-permute-start.4 = (bf16[96,2048]{1,0:T(8,128)(2,1)S(1)}, bf16[96,2048]{1,0:T(8,128)(2,1)S(1)}, u32[]{:S(2)}, u32[]{:S(2)}) collective-permute-start(bf16[96,2048]{1,0:T(8,128)(2,1)S(1)} %collective-permute-done.1), channel_id=1, source_target_pairs={{0,2},{16,48},{2,4},{18,50},{4,6},{20,52},{6,8},{22,54},{8,10},{24... | collective-permute-start | bytes 1179656 | tf_op jit(solution)/shard_map/ppermute | solution.py:343
  24.6 1.9 %collective-permute-start.3 = (bf16[288,2048]{1,0:T(8,128)(2,1)S(1)}, bf16[288,2048]{1,0:T(8,128)(2,1)S(1)}, u32[]{:S(2)}, u32[]{:S(2)}) collective-permute-start(bf16[288,2048]{1,0:T(8,128)(2,1)S(1)} %constant_dynamic-update-slice_fusion.2.refs_0_), channel_id=1, source_target_pairs={{0,1},{16,273},{2,3},{18,275},{4,5},{20,277},{6,7},{22,279},{8,9},... | collective-permute-start | bytes 3538952 | tf_op jit(solution)/shard_map/ppermute | solution.py:332
  26.5 4.6 %collective-permute-start.5 = (bf16[96,2048]{1,0:T(8,128)(2,1)S(1)}, bf16[96,2048]{1,0:T(8,128)(2,1)S(1)}, u32[]{:S(2)}, u32[]{:S(2)}) collective-permute-start(bf16[96,2048]{1,0:T(8,128)(2,1)S(1)} %collective-permute-done.2), channel_id=1, source_target_pairs={{0,14},{16,240},{2,0},{18,242},{4,2},{20,244},{6,4},{22,246},{8,6}... | collective-permute-start | bytes 1179656 | tf_op jit(solution)/shard_map/ppermute | solution.py:344
  31.1 5.6 %collective-permute-start.11 = (bf16[288,2048]{1,0:T(8,128)(2,1)S(1)}, bf16[288,2048]{1,0:T(8,128)(2,1)S(1)}, u32[]{:S(2)}, u32[]{:S(2)}) collective-permute-start(bf16[288,2048]{1,0:T(8,128)(2,1)S(1)} %constant_dynamic-update-slice_fusion.2.refs_0_), channel_id=1, source_target_pairs={{0,16},{16,0},{2,18},{18,2},{4,20},{20,4},{6,22},{22,6},{8,24},{24... | collective-permute-start | bytes 3538952 | tf_op jit(solution)/shard_map/ppermute | solution.py:328
  36.8 3.2 %collective-permute-start.7 = (bf16[96,2048]{1,0:T(8,128)(2,1)S(1)}, bf16[96,2048]{1,0:T(8,128)(2,1)S(1)}, u32[]{:S(2)}, u32[]{:S(2)}) collective-permute-start(bf16[96,2048]{1,0:T(8,128)(2,1)S(1)} %collective-permute-done.4), channel_id=1, source_target_pairs={{0,2},{16,48},{2,4},{18,50},{4,6},{20,52},{6,8},{22,54},{8,10},{24... | collective-permute-start | bytes 1179656 | tf_op jit(solution)/shard_map/ppermute | solution.py:343
  40.0 3.7 %collective-permute-start.6 = (bf16[192,2048]{1,0:T(8,128)(2,1)S(1)}, bf16[192,2048]{1,0:T(8,128)(2,1)S(1)}, u32[]{:S(2)}, u32[]{:S(2)}) collective-permute-start(bf16[192,2048]{1,0:T(8,128)(2,1)S(1)} %constant_dynamic-update-slice_fusion.6.refs_2_), channel_id=1, source_target_pairs={{0,1},{16,273},{2,3},{18,275},{4,5},{20,277},{6,7},{22,279},{8,9},... | collective-permute-start | bytes 2359304 | tf_op jit(solution)/shard_map/ppermute | solution.py:332
  43.8 3.8 %collective-permute-start.8 = (bf16[96,2048]{1,0:T(8,128)(2,1)S(1)}, bf16[96,2048]{1,0:T(8,128)(2,1)S(1)}, u32[]{:S(2)}, u32[]{:S(2)}) collective-permute-start(bf16[96,2048]{1,0:T(8,128)(2,1)S(1)} %collective-permute-done.5), channel_id=1, source_target_pairs={{0,14},{16,240},{2,0},{18,242},{4,2},{20,244},{6,4},{22,246},{8,6}... | collective-permute-start | bytes 1179656 | tf_op jit(solution)/shard_map/ppermute | solution.py:344
  47.6 1.9 %collective-permute-start.9 = (bf16[96,2048]{1,0:T(8,128)(2,1)S(1)}, bf16[96,2048]{1,0:T(8,128)(2,1)S(1)}, u32[]{:S(2)}, u32[]{:S(2)}) collective-permute-start(bf16[96,2048]{1,0:T(8,128)(2,1)S(1)} %collective-permute-done.7), channel_id=1, source_target_pairs={{0,2},{16,48},{2,4},{18,50},{4,6},{20,52},{6,8},{22,54},{8,10},{24... | collective-permute-start | bytes 1179656 | tf_op jit(solution)/shard_map/ppermute | solution.py:349
  49.5 2.5 %collective-permute-start.12 = (bf16[288,2048]{1,0:T(8,128)(2,1)S(1)}, bf16[288,2048]{1,0:T(8,128)(2,1)S(1)}, u32[]{:S(2)}, u32[]{:S(2)}) collective-permute-start(bf16[288,2048]{1,0:T(8,128)(2,1)S(1)} %collective-permute-done.3.refs_1_), channel_id=1, source_target_pairs={{0,16},{16,0},{2,18},{18,2},{4,20},{20,4},{6,22},{22,6},{8,24},{24... | collective-permute-start | bytes 3538952 | tf_op jit(solution)/shard_map/ppermute | solution.py:328
  52.6 5.0 %collective-permute-done.9 = bf16[96,2048]{1,0:T(8,128)(2,1)S(1)} collective-permute-done((bf16[96,2048]{1,0:T(8,128)(2,1)S(1)}, bf16[96,2048]{1,0:T(8,128)(2,1)S(1)}, u32[]{:S(2)}, u32[]{:S(2)}) %collective-permute-start.9) | collective-permute-done | bytes 393248 | tf_op jit(solution)/shard_map/ppermute | solution.py:349
  57.7 3.4 %collective-permute-start.10 = (bf16[288,2048]{1,0:T(8,128)(2,1)S(1)}, bf16[288,2048]{1,0:T(8,128)(2,1)S(1)}, u32[]{:S(2)}, u32[]{:S(2)}) collective-permute-start(bf16[288,2048]{1,0:T(8,128)(2,1)S(1)} %pad_maximum_fusion.refs_4_), channel_id=1, source_target_pairs={{0,1},{16,273},{2,3},{18,275},{4,5},{20,277},{6,7},{22,279},{8,9},... | collective-permute-start | bytes 3538952 | tf_op jit(solution)/shard_map/ppermute | solution.py:332
  61.1 3.4 %collective-permute-start.15 = (bf16[288,2048]{1,0:T(8,128)(2,1)S(1)}, bf16[288,2048]{1,0:T(8,128)(2,1)S(1)}, u32[]{:S(2)}, u32[]{:S(2)}) collective-permute-start(bf16[288,2048]{1,0:T(8,128)(2,1)S(1)} %pad_maximum_fusion.refs_4_), channel_id=1, source_target_pairs={{0,16},{16,0},{2,18},{18,2},{4,20},{20,4},{6,22},{22,6},{8,24},{24... | collective-permute-start | bytes 3538952 | tf_op jit(solution)/shard_map/ppermute | solution.py:328
  64.5 1.9 %collective-permute-start.13 = (bf16[192,2048]{1,0:T(8,128)(2,1)S(1)}, bf16[192,2048]{1,0:T(8,128)(2,1)S(1)}, u32[]{:S(2)}, u32[]{:S(2)}) collective-permute-start(bf16[192,2048]{1,0:T(8,128)(2,1)S(1)} %constant_dynamic-update-slice_fusion.6.refs_2_), channel_id=1, source_target_pairs={{0,16},{16,0},{2,18},{18,2},{4,20},{20,4},{6,22},{22,6},{8,24},{24... | collective-permute-start | bytes 2359304 | tf_op jit(solution)/shard_map/ppermute | solution.py:328
  66.5 2.4 %collective-permute-start.14 = (bf16[192,2048]{1,0:T(8,128)(2,1)S(1)}, bf16[192,2048]{1,0:T(8,128)(2,1)S(1)}, u32[]{:S(2)}, u32[]{:S(2)}) collective-permute-start(bf16[192,2048]{1,0:T(8,128)(2,1)S(1)} %collective-permute-done.6.refs_3_), channel_id=1, source_target_pairs={{0,16},{16,0},{2,18},{18,2},{4,20},{20,4},{6,22},{22,6},{8,24},{24... | collective-permute-start | bytes 2359304 | tf_op jit(solution)/shard_map/ppermute | solution.py:328
  68.9 1.9 %collective-permute-done.14.refs_7_.refs_9_ = bf16[192,2048]{1,0:T(8,128)(2,1)S(1)} collective-permute-done((bf16[192,2048]{1,0:T(8,128)(2,1)S(1)}, bf16[192,2048]{1,0:T(8,128)(2,1)S(1)}, u32[]{:S(2)}, u32[]{:S(2)}) %collective-permute-start.14) | collective-permute-done | bytes 786464 | tf_op jit(solution)/shard_map/ppermute | solution.py:328
  70.8 3.2 %shard_map.68.refs_12_ = f32[8,768]{1,0:T(8,128)S(1)} custom-call(bf16[288,2048]{1,0:T(8,128)(2,1)S(1)} %constant_dynamic-update-slice_fusion.2.refs_0_, bf16[288,2048]{1,0:T(8,128)(2,1)S(1)} %collective-permute-done.3.refs_1_, bf16[192,2048]{1,0:T(8,128)(2,1)S(1)} %constant_dynamic-update-slice_fusion.6.refs_2_, ...), custom_call_target="tpu_custom_call" | custom-call | flops 1887436800 | bytes 9830400 | tf_op jit(solution)/shard_map/pallas_call | solution.py:188
  74.0 1.9 %collective-permute-done.10.refs_5_ = bf16[288,2048]{1,0:T(8,128)(2,1)S(1)} collective-permute-done((bf16[288,2048]{1,0:T(8,128)(2,1)S(1)}, bf16[288,2048]{1,0:T(8,128)(2,1)S(1)}, u32[]{:S(2)}, u32[]{:S(2)}) %collective-permute-start.10) | collective-permute-done | bytes 1179680 | tf_op jit(solution)/shard_map/ppermute | solution.py:332
  75.9 3.5 %collective-permute-start.16 = (bf16[288,2048]{1,0:T(8,128)(2,1)S(1)}, bf16[288,2048]{1,0:T(8,128)(2,1)S(1)}, u32[]{:S(2)}, u32[]{:S(2)}) collective-permute-start(bf16[288,2048]{1,0:T(8,128)(2,1)S(1)} %collective-permute-done.10.refs_5_), channel_id=1, source_target_pairs={{0,16},{16,0},{2,18},{18,2},{4,20},{20,4},{6,22},{22,6},{8,24},{24... | collective-permute-start | bytes 3538952 | tf_op jit(solution)/shard_map/ppermute | solution.py:328
  79.4 2.3 %collective-permute-done.16.refs_11_ = bf16[288,2048]{1,0:T(8,128)(2,1)S(1)} collective-permute-done((bf16[288,2048]{1,0:T(8,128)(2,1)S(1)}, bf16[288,2048]{1,0:T(8,128)(2,1)S(1)}, u32[]{:S(2)}, u32[]{:S(2)}) %collective-permute-start.16) | collective-permute-done | bytes 1179680 | tf_op jit(solution)/shard_map/ppermute | solution.py:328
  81.7 7.9 %shard_map.69 = f32[16,6,8,128]{3,2,1,0:T(8,128)} custom-call(bf16[288,2048]{1,0:T(8,128)(2,1)S(1)} %constant_dynamic-update-slice_fusion.2.refs_0_, bf16[288,2048]{1,0:T(8,128)(2,1)S(1)} %collective-permute-done.3.refs_1_, bf16[192,2048]{1,0:T(8,128)(2,1)S(1)} %constant_dynamic-update-slice_fusion.6.refs_2_, ...), custom_call_target="tpu_custom_call" | custom-call | flops 4152360960 | bytes 15728640 | tf_op jit(solution)/shard_map/pallas_call | solution.py:256
  89.5 9.1 %all-to-all-start = ((f32[16,6,8,128]{3,2,1,0:T(8,128)}), f32[16,6,8,128]{3,2,1,0:T(8,128)S(1)}, u32[]{:S(2)}, u32[]{:S(2)}) async-start(f32[16,6,8,128]{3,2,1,0:T(8,128)} %shard_map.69), calls=%async_computation | async-start | bytes 786432 | tf_op jit(solution)/shard_map/all_to_all | solution.py:360
  98.7 12.0 %all-to-all-done.parts = f32[16,6,8,128]{3,2,1,0:T(8,128)S(1)} async-done(((f32[16,6,8,128]{3,2,1,0:T(8,128)}), f32[16,6,8,128]{3,2,1,0:T(8,128)S(1)}, u32[]{:S(2)}, u32[]{:S(2)}) %all-to-all-start) | async-done | bytes 393248 | tf_op jit(solution)/shard_map/all_to_all | solution.py:360
  110.6 0.9 shard_map.70
  111.5 1.9 %collective-permute-start.17 = (f32[1,128]{1,0:T(1,128)S(1)}, f32[1,128]{1,0:T(1,128)S(1)}, u32[]{:S(2)}, u32[]{:S(2)}) collective-permute-start(f32[1,128]{1,0:T(1,128)S(1)} %get-tuple-element.13), channel_id=1, source_target_pairs={{0,16},{16,0},{2,18},{18,2},{4,20},{20,4},{6,22},{22,6},{8,24},{24... | collective-permute-start | bytes 1544 | tf_op jit(solution)/shard_map/ppermute | solution.py:328
  113.4 5.5 %all-to-all-start.1 = ((f32[32,1,128]{2,1,0:T(1,128)}), f32[32,1,128]{2,1,0:T(1,128)S(1)}, u32[]{:S(2)}, u32[]{:S(2)}) async-start(f32[32,1,128]{2,1,0:T(1,128)} %get-tuple-element.14), calls=%async_computation.1 | async-start | bytes 32768 | tf_op jit(solution)/shard_map/all_to_all | solution.py:365
  119.5 8.4 %all-to-all-done.1 = f32[32,1,128]{2,1,0:T(1,128)S(1)} async-done(((f32[32,1,128]{2,1,0:T(1,128)}), f32[32,1,128]{2,1,0:T(1,128)S(1)}, u32[]{:S(2)}, u32[]{:S(2)}) %all-to-all-start.1) | async-done | bytes 16416 | tf_op jit(solution)/shard_map/all_to_all | solution.py:365
  (21 shorter events, 2.3 us)
Async XLA Ops:
  2.5 10.1 %collective-permute-start = (bf16[48,2048]{1,0:T(8,128)(2,1)}, bf16[48,2048]{1,0:T(8,128)(2,1)S(1)}, u32[]{:S(2)}, u32[]{:S(2)}) collective-permute-start(bf16[48,2048]{1,0:T(8,128)(2,1)} %get-tuple-element.10), channel_id=1, source_target_pairs={{0,16},{16,0},{2,18},{18,2},{4,20},{20,4},{6,22},{22,6},{8,24},{24... | collective-permute-start | bytes 589832 | tf_op jit(solution)/shard_map/ppermute | solution.py:328
  12.6 10.0 %collective-permute-start.1 = (bf16[96,2048]{1,0:T(8,128)(2,1)S(1)}, bf16[96,2048]{1,0:T(8,128)(2,1)S(1)}, u32[]{:S(2)}, u32[]{:S(2)}) collective-permute-start(bf16[96,2048]{1,0:T(8,128)(2,1)S(1)} %get-tuple-element.15), channel_id=1, source_target_pairs={{0,2},{16,48},{2,4},{18,50},{4,6},{20,52},{6,8},{22,54},{8,10},{24... | collective-permute-start | bytes 1179656 | tf_op jit(solution)/shard_map/ppermute | solution.py:343
  14.5 10.1 %collective-permute-start.2 = (bf16[96,2048]{1,0:T(8,128)(2,1)S(1)}, bf16[96,2048]{1,0:T(8,128)(2,1)S(1)}, u32[]{:S(2)}, u32[]{:S(2)}) collective-permute-start(bf16[96,2048]{1,0:T(8,128)(2,1)S(1)} %get-tuple-element.15), channel_id=1, source_target_pairs={{0,14},{16,240},{2,0},{18,242},{4,2},{20,244},{6,4},{22,246},{8,6}... | collective-permute-start | bytes 1179656 | tf_op jit(solution)/shard_map/ppermute | solution.py:344
  22.6 14.1 %collective-permute-start.4 = (bf16[96,2048]{1,0:T(8,128)(2,1)S(1)}, bf16[96,2048]{1,0:T(8,128)(2,1)S(1)}, u32[]{:S(2)}, u32[]{:S(2)}) collective-permute-start(bf16[96,2048]{1,0:T(8,128)(2,1)S(1)} %collective-permute-done.1), channel_id=1, source_target_pairs={{0,2},{16,48},{2,4},{18,50},{4,6},{20,52},{6,8},{22,54},{8,10},{24... | collective-permute-start | bytes 1179656 | tf_op jit(solution)/shard_map/ppermute | solution.py:343
  24.6 24.9 %collective-permute-start.3 = (bf16[288,2048]{1,0:T(8,128)(2,1)S(1)}, bf16[288,2048]{1,0:T(8,128)(2,1)S(1)}, u32[]{:S(2)}, u32[]{:S(2)}) collective-permute-start(bf16[288,2048]{1,0:T(8,128)(2,1)S(1)} %constant_dynamic-update-slice_fusion.2.refs_0_), channel_id=1, source_target_pairs={{0,1},{16,273},{2,3},{18,275},{4,5},{20,277},{6,7},{22,279},{8,9},... | collective-permute-start | bytes 3538952 | tf_op jit(solution)/shard_map/ppermute | solution.py:332
  26.5 13.5 %collective-permute-start.5 = (bf16[96,2048]{1,0:T(8,128)(2,1)S(1)}, bf16[96,2048]{1,0:T(8,128)(2,1)S(1)}, u32[]{:S(2)}, u32[]{:S(2)}) collective-permute-start(bf16[96,2048]{1,0:T(8,128)(2,1)S(1)} %collective-permute-done.2), channel_id=1, source_target_pairs={{0,14},{16,240},{2,0},{18,242},{4,2},{20,244},{6,4},{22,246},{8,6}... | collective-permute-start | bytes 1179656 | tf_op jit(solution)/shard_map/ppermute | solution.py:344
  31.1 35.3 %collective-permute-start.11 = (bf16[288,2048]{1,0:T(8,128)(2,1)S(1)}, bf16[288,2048]{1,0:T(8,128)(2,1)S(1)}, u32[]{:S(2)}, u32[]{:S(2)}) collective-permute-start(bf16[288,2048]{1,0:T(8,128)(2,1)S(1)} %constant_dynamic-update-slice_fusion.2.refs_0_), channel_id=1, source_target_pairs={{0,16},{16,0},{2,18},{18,2},{4,20},{20,4},{6,22},{22,6},{8,24},{24... | collective-permute-start | bytes 3538952 | tf_op jit(solution)/shard_map/ppermute | solution.py:328
  36.8 10.8 %collective-permute-start.7 = (bf16[96,2048]{1,0:T(8,128)(2,1)S(1)}, bf16[96,2048]{1,0:T(8,128)(2,1)S(1)}, u32[]{:S(2)}, u32[]{:S(2)}) collective-permute-start(bf16[96,2048]{1,0:T(8,128)(2,1)S(1)} %collective-permute-done.4), channel_id=1, source_target_pairs={{0,2},{16,48},{2,4},{18,50},{4,6},{20,52},{6,8},{22,54},{8,10},{24... | collective-permute-start | bytes 1179656 | tf_op jit(solution)/shard_map/ppermute | solution.py:343
  40.0 17.7 %collective-permute-start.6 = (bf16[192,2048]{1,0:T(8,128)(2,1)S(1)}, bf16[192,2048]{1,0:T(8,128)(2,1)S(1)}, u32[]{:S(2)}, u32[]{:S(2)}) collective-permute-start(bf16[192,2048]{1,0:T(8,128)(2,1)S(1)} %constant_dynamic-update-slice_fusion.6.refs_2_), channel_id=1, source_target_pairs={{0,1},{16,273},{2,3},{18,275},{4,5},{20,277},{6,7},{22,279},{8,9},... | collective-permute-start | bytes 2359304 | tf_op jit(solution)/shard_map/ppermute | solution.py:332
  43.8 8.8 %collective-permute-start.8 = (bf16[96,2048]{1,0:T(8,128)(2,1)S(1)}, bf16[96,2048]{1,0:T(8,128)(2,1)S(1)}, u32[]{:S(2)}, u32[]{:S(2)}) collective-permute-start(bf16[96,2048]{1,0:T(8,128)(2,1)S(1)} %collective-permute-done.5), channel_id=1, source_target_pairs={{0,14},{16,240},{2,0},{18,242},{4,2},{20,244},{6,4},{22,246},{8,6}... | collective-permute-start | bytes 1179656 | tf_op jit(solution)/shard_map/ppermute | solution.py:344
  47.6 10.0 %collective-permute-start.9 = (bf16[96,2048]{1,0:T(8,128)(2,1)S(1)}, bf16[96,2048]{1,0:T(8,128)(2,1)S(1)}, u32[]{:S(2)}, u32[]{:S(2)}) collective-permute-start(bf16[96,2048]{1,0:T(8,128)(2,1)S(1)} %collective-permute-done.7), channel_id=1, source_target_pairs={{0,2},{16,48},{2,4},{18,50},{4,6},{20,52},{6,8},{22,54},{8,10},{24... | collective-permute-start | bytes 1179656 | tf_op jit(solution)/shard_map/ppermute | solution.py:349
  49.5 21.2 %collective-permute-start.12 = (bf16[288,2048]{1,0:T(8,128)(2,1)S(1)}, bf16[288,2048]{1,0:T(8,128)(2,1)S(1)}, u32[]{:S(2)}, u32[]{:S(2)}) collective-permute-start(bf16[288,2048]{1,0:T(8,128)(2,1)S(1)} %collective-permute-done.3.refs_1_), channel_id=1, source_target_pairs={{0,16},{16,0},{2,18},{18,2},{4,20},{20,4},{6,22},{22,6},{8,24},{24... | collective-permute-start | bytes 3538952 | tf_op jit(solution)/shard_map/ppermute | solution.py:328
  57.7 18.2 %collective-permute-start.10 = (bf16[288,2048]{1,0:T(8,128)(2,1)S(1)}, bf16[288,2048]{1,0:T(8,128)(2,1)S(1)}, u32[]{:S(2)}, u32[]{:S(2)}) collective-permute-start(bf16[288,2048]{1,0:T(8,128)(2,1)S(1)} %pad_maximum_fusion.refs_4_), channel_id=1, source_target_pairs={{0,1},{16,273},{2,3},{18,275},{4,5},{20,277},{6,7},{22,279},{8,9},... | collective-permute-start | bytes 3538952 | tf_op jit(solution)/shard_map/ppermute | solution.py:332
  61.1 14.8 %collective-permute-start.15 = (bf16[288,2048]{1,0:T(8,128)(2,1)S(1)}, bf16[288,2048]{1,0:T(8,128)(2,1)S(1)}, u32[]{:S(2)}, u32[]{:S(2)}) collective-permute-start(bf16[288,2048]{1,0:T(8,128)(2,1)S(1)} %pad_maximum_fusion.refs_4_), channel_id=1, source_target_pairs={{0,16},{16,0},{2,18},{18,2},{4,20},{20,4},{6,22},{22,6},{8,24},{24... | collective-permute-start | bytes 3538952 | tf_op jit(solution)/shard_map/ppermute | solution.py:328
  64.5 4.4 %collective-permute-start.13 = (bf16[192,2048]{1,0:T(8,128)(2,1)S(1)}, bf16[192,2048]{1,0:T(8,128)(2,1)S(1)}, u32[]{:S(2)}, u32[]{:S(2)}) collective-permute-start(bf16[192,2048]{1,0:T(8,128)(2,1)S(1)} %constant_dynamic-update-slice_fusion.6.refs_2_), channel_id=1, source_target_pairs={{0,16},{16,0},{2,18},{18,2},{4,20},{20,4},{6,22},{22,6},{8,24},{24... | collective-permute-start | bytes 2359304 | tf_op jit(solution)/shard_map/ppermute | solution.py:328
  66.5 4.3 %collective-permute-start.14 = (bf16[192,2048]{1,0:T(8,128)(2,1)S(1)}, bf16[192,2048]{1,0:T(8,128)(2,1)S(1)}, u32[]{:S(2)}, u32[]{:S(2)}) collective-permute-start(bf16[192,2048]{1,0:T(8,128)(2,1)S(1)} %collective-permute-done.6.refs_3_), channel_id=1, source_target_pairs={{0,16},{16,0},{2,18},{18,2},{4,20},{20,4},{6,22},{22,6},{8,24},{24... | collective-permute-start | bytes 2359304 | tf_op jit(solution)/shard_map/ppermute | solution.py:328
  75.9 5.7 %collective-permute-start.16 = (bf16[288,2048]{1,0:T(8,128)(2,1)S(1)}, bf16[288,2048]{1,0:T(8,128)(2,1)S(1)}, u32[]{:S(2)}, u32[]{:S(2)}) collective-permute-start(bf16[288,2048]{1,0:T(8,128)(2,1)S(1)} %collective-permute-done.10.refs_5_), channel_id=1, source_target_pairs={{0,16},{16,0},{2,18},{18,2},{4,20},{20,4},{6,22},{22,6},{8,24},{24... | collective-permute-start | bytes 3538952 | tf_op jit(solution)/shard_map/ppermute | solution.py:328
  89.5 21.1 %all-to-all-start = ((f32[16,6,8,128]{3,2,1,0:T(8,128)}), f32[16,6,8,128]{3,2,1,0:T(8,128)S(1)}, u32[]{:S(2)}, u32[]{:S(2)}) async-start(f32[16,6,8,128]{3,2,1,0:T(8,128)} %shard_map.69), calls=%async_computation | async-start | bytes 786432 | tf_op jit(solution)/shard_map/all_to_all | solution.py:360
  111.5 7.4 %collective-permute-start.17 = (f32[1,128]{1,0:T(1,128)S(1)}, f32[1,128]{1,0:T(1,128)S(1)}, u32[]{:S(2)}, u32[]{:S(2)}) collective-permute-start(f32[1,128]{1,0:T(1,128)S(1)} %get-tuple-element.13), channel_id=1, source_target_pairs={{0,16},{16,0},{2,18},{18,2},{4,20},{20,4},{6,22},{22,6},{8,24},{24... | collective-permute-start | bytes 1544 | tf_op jit(solution)/shard_map/ppermute | solution.py:328
  113.4 14.6 %all-to-all-start.1 = ((f32[32,1,128]{2,1,0:T(1,128)}), f32[32,1,128]{2,1,0:T(1,128)S(1)}, u32[]{:S(2)}, u32[]{:S(2)}) async-start(f32[32,1,128]{2,1,0:T(1,128)} %get-tuple-element.14), calls=%async_computation.1 | async-start | bytes 32768 | tf_op jit(solution)/shard_map/all_to_all | solution.py:365

commit v6 on v5

--- a/solution.py
+++ b/solution.py
@@ -198,13 +198,10 @@
     )(*own, *other)
 
 
-def late_kernel(ds, dt, units, known, *refs):
-    own, other = refs[:units], refs[units : 2 * units]
-    before, out, l, g, ls, gs, stats = refs[2 * units :]
+def advance(ds, dt, own, other, before, known, stats, l, g, ls, gs):
     rows = total_rows(own)
     chunks = rows // CHUNK
     done = known // CHUNK
-    line, xi = where_am_i()
 
     def lanes(j):
         return j * CHUNK, (j + 1) * CHUNK
@@ -231,6 +228,43 @@
     for n, v in enumerate(summary(ds, dt, l.at[(chunks - 1) % 2], g.at[(chunks - 1) % 2], rows, False)):
         stats[n : n + 1, slice(*lanes(chunks - 1))] = v
 
+
+def scratch(rows, known):
+    return [pltpu.VMEM((2, rows, CHUNK), jnp.float32)] * 2 + [
+        pltpu.VMEM((known // CHUNK, rows - known, CHUNK), jnp.float32)
+    ] * 2
+
+
+def between_kernel(ds, dt, units, known, *refs):
+    own, other = refs[:units], refs[units : 2 * units]
+    before, out, *work = refs[2 * units :]
+    advance(ds, dt, own, other, before, known, out, *work)
+
+
+def between(own, other, before, known, ds, dt):
+    rows = total_rows(own)
+    lanes = rows // CHUNK * CHUNK
+    vmem = pl.BlockSpec(memory_space=pltpu.VMEM)
+    work = rows * lanes - known * before.shape[1]
+    return pl.pallas_call(
+        functools.partial(between_kernel, ds, dt, len(own), known),
+        out_shape=jax.ShapeDtypeStruct((8, lanes), jnp.float32),
+        in_specs=[vmem] * (len(own) + len(other) + 1),
+        out_specs=vmem,
+        scratch_shapes=scratch(rows, known),
+        compiler_params=pltpu.CompilerParams(vmem_limit_bytes=20 * 1024 * 1024),
+        cost_estimate=pl.CostEstimate(
+            flops=2 * work * (ds + dt), bytes_accessed=8 * rows * (ds + dt), transcendentals=2 * work
+        ),
+    )(*own, *other, before)
+
+
+def late_kernel(ds, dt, units, known, *refs):
+    own, other = refs[:units], refs[units : 2 * units]
+    before, out, l, g, ls, gs, stats = refs[2 * units :]
+    line, xi = where_am_i()
+    advance(ds, dt, own, other, before, known, stats, l, g, ls, gs)
+
     places = {}
     at = 0
     for steps, partner in ORDER:
@@ -258,9 +292,7 @@
         out_shape=jax.ShapeDtypeStruct((16, 6, 8, 128), jnp.float32),
         in_specs=[vmem] * (len(own) + len(other) + 1),
         out_specs=vmem,
-        scratch_shapes=[pltpu.VMEM((2, rows, CHUNK), jnp.float32)] * 2
-        + [pltpu.VMEM((done, rows - known, CHUNK), jnp.float32)] * 2
-        + [pltpu.VMEM((8, rows), jnp.float32)],
+        scratch_shapes=scratch(rows, known) + [pltpu.VMEM((8, rows), jnp.float32)],
         compiler_params=pltpu.CompilerParams(vmem_limit_bytes=20 * 1024 * 1024),
         cost_estimate=pl.CostEstimate(
             flops=2 * work * (ds + dt), bytes_accessed=8 * rows * (ds + dt), transcendentals=2 * work
@@ -354,9 +386,12 @@
     other = [swap(v) for v in own]
     before = early(own, other, ds, dt)
     end_other = swap(end)
-    own += [end, end_across]
-    other += [end_other, swap(after(end_across, before, end_other))]
-    stats = late(own, other, before, known, ds, dt)
+    across_other = swap(after(end_across, before, end_other))
+    own.append(end)
+    other.append(end_other)
+    before = between(own, other, before, known, ds, dt)
+    known = total_rows(own)
+    stats = late(own + [end_across], other + [across_other], before, known, ds, dt)
     parts = lax.all_to_all(stats, AXES, 0, 0, axis_index_groups=STAT_GROUPS)
     chip, total = finish(parts)
     first, second = chip[0, :SHARD], swap(chip)[0, SHARD : 2 * SHARD]

time: 131 us -> 131 us (level)
    pallas_call x0 -> x1, Pallas kernels: none -> 2.39 us  [between(): pl.pallas_call(functools.partial(between_kernel, ds, dt, len(own), known)...]
    ppermute x3, waiting for transfers between devices: 1.92 us -> 4.29 us  [pass_on(): return lax.ppermute(v, AXES, X_PAIRS)]
    pallas_call x1, Pallas kernels: 7.87 us -> 5.59 us  [late(): pl.pallas_call(functools.partial(late_kernel, ds, dt, len(own), known), o...]
    ppermute x8, waiting for transfers between devices: 4.47 us -> 2.43 us  [swap(): return lax.ppermute(v, AXES, CORE_PAIRS)]
    ppermute x8, starting transfers between devices: 30 us -> 28.6 us  [swap(): return lax.ppermute(v, AXES, CORE_PAIRS)]
  transfers between devices with their start and end apart: 20 -> 20, of which waited for: 9 -> 9; matrix products, arithmetic and copies ran while one was open for 1% -> 1% of each run, Pallas kernels for 2% -> 4%
where the time goes in v6:
time: 131 us; the launch traced here: 130 us
  starting transfers between devices  74.8 us (57%)
  waiting for transfers between devices  36.2 us (28%)
  Pallas kernels  13.9 us (11%)
  between operations  2.75 us (2%)
  other arithmetic  1.32 us (1%)
    ppermute x8, starting transfers between devices, swap(): return lax.ppermute(v, AXES, CORE_PAIRS)  28.6 us
    ppermute x3, starting transfers between devices, shards(): down.append(lax.ppermute(down[-1], AXES, DOWN))  13 us
    all_to_all x1, waiting for transfers between devices, shards(): parts = lax.all_to_all(stats, AXES, 0, 0, axis_index_groups=STAT_GROUPS)  12 us
    ppermute x3, starting transfers between devices, pass_on(): return lax.ppermute(v, AXES, X_PAIRS)  10 us
    all_to_all x1, starting transfers between devices, shards(): parts = lax.all_to_all(stats, AXES, 0, 0, axis_index_groups=STAT_GROUPS)  9.13 us
    all_to_all x1, waiting for transfers between devices, shards(): totals = lax.all_to_all(total, AXES, 0, 0, axis_index_groups=SUM_GROUPS)  8.44 us
    ppermute x3, starting transfers between devices, shards(): up.append(lax.ppermute(up[-1], AXES, UP))  7.03 us
    pallas_call x1, Pallas kernels, late(): pl.pallas_call(functools.partial(late_kernel, ds, dt, len(own), known), o...  5.59 us
  transfers between devices with their start and end apart: 20, of which 9 were waited for; matrix products, arithmetic and copies ran while one was open for 1% of the time, Pallas kernels for 4%

profile of v6, /device:TPU:1, one launch (start us, length us, event | category | flops | bytes accessed | tf_op | source)
XLA Modules:
  0.0 130.1 jit_solution(18059211948915032624)
XLA Ops:
  0.6 1.9 %shard_map.67 = (bf16[48,2048]{1,0:T(8,128)(2,1)}, bf16[48,2048]{1,0:T(8,128)(2,1)}) custom-call(bf16[48,512]{1,0:T(8,128)(2,1)} %image_s.1, bf16[48,512]{1,0:T(8,128)(2,1)} %text_s.1, bf16[48,768]{1,0:T(8,128)(2,1)} %image_t.1, bf16[48,768]{1,0:T(8,128)(2,1)} %text_t.1), custom_call_target="tpu_custom_call" | custom-call | tf_op jit(solution)/shard_map/pallas_call | solution.py:97
  2.5 8.8 %collective-permute-start = (bf16[48,2048]{1,0:T(8,128)(2,1)}, bf16[48,2048]{1,0:T(8,128)(2,1)S(1)}, u32[]{:S(2)}, u32[]{:S(2)}) collective-permute-start(bf16[48,2048]{1,0:T(8,128)(2,1)} %get-tuple-element.10), channel_id=1, source_target_pairs={{0,16},{16,0},{2,18},{18,2},{4,20},{20,4},{6,22},{22,6},{8,24},{24... | collective-permute-start | bytes 589832 | tf_op jit(solution)/shard_map/ppermute | solution.py:360
  11.3 1.0 constant_dynamic-update-slice_fusion.1
  12.6 1.9 %collective-permute-start.1 = (bf16[96,2048]{1,0:T(8,128)(2,1)S(1)}, bf16[96,2048]{1,0:T(8,128)(2,1)S(1)}, u32[]{:S(2)}, u32[]{:S(2)}) collective-permute-start(bf16[96,2048]{1,0:T(8,128)(2,1)S(1)} %get-tuple-element.15), channel_id=1, source_target_pairs={{0,2},{16,48},{2,4},{18,50},{4,6},{20,52},{6,8},{22,54},{8,10},{24... | collective-permute-start | bytes 1179656 | tf_op jit(solution)/shard_map/ppermute | solution.py:375
  14.5 4.6 %collective-permute-start.2 = (bf16[96,2048]{1,0:T(8,128)(2,1)S(1)}, bf16[96,2048]{1,0:T(8,128)(2,1)S(1)}, u32[]{:S(2)}, u32[]{:S(2)}) collective-permute-start(bf16[96,2048]{1,0:T(8,128)(2,1)S(1)} %get-tuple-element.15), channel_id=1, source_target_pairs={{0,14},{16,240},{2,0},{18,242},{4,2},{20,244},{6,4},{22,246},{8,6}... | collective-permute-start | bytes 1179656 | tf_op jit(solution)/shard_map/ppermute | solution.py:376
  19.1 3.5 %collective-permute-done.1 = bf16[96,2048]{1,0:T(8,128)(2,1)S(1)} collective-permute-done((bf16[96,2048]{1,0:T(8,128)(2,1)S(1)}, bf16[96,2048]{1,0:T(8,128)(2,1)S(1)}, u32[]{:S(2)}, u32[]{:S(2)}) %collective-permute-start.1) | collective-permute-done | bytes 393248 | tf_op jit(solution)/shard_map/ppermute | solution.py:375
  22.6 1.9 %collective-permute-start.4 = (bf16[96,2048]{1,0:T(8,128)(2,1)S(1)}, bf16[96,2048]{1,0:T(8,128)(2,1)S(1)}, u32[]{:S(2)}, u32[]{:S(2)}) collective-permute-start(bf16[96,2048]{1,0:T(8,128)(2,1)S(1)} %collective-permute-done.1), channel_id=1, source_target_pairs={{0,2},{16,48},{2,4},{18,50},{4,6},{20,52},{6,8},{22,54},{8,10},{24... | collective-permute-start | bytes 1179656 | tf_op jit(solution)/shard_map/ppermute | solution.py:375
  24.6 1.9 %collective-permute-start.3 = (bf16[288,2048]{1,0:T(8,128)(2,1)S(1)}, bf16[288,2048]{1,0:T(8,128)(2,1)S(1)}, u32[]{:S(2)}, u32[]{:S(2)}) collective-permute-start(bf16[288,2048]{1,0:T(8,128)(2,1)S(1)} %constant_dynamic-update-slice_fusion.2.refs_0_), channel_id=1, source_target_pairs={{0,1},{16,273},{2,3},{18,275},{4,5},{20,277},{6,7},{22,279},{8,9},... | collective-permute-start | bytes 3538952 | tf_op jit(solution)/shard_map/ppermute | solution.py:364
  26.5 4.6 %collective-permute-start.5 = (bf16[96,2048]{1,0:T(8,128)(2,1)S(1)}, bf16[96,2048]{1,0:T(8,128)(2,1)S(1)}, u32[]{:S(2)}, u32[]{:S(2)}) collective-permute-start(bf16[96,2048]{1,0:T(8,128)(2,1)S(1)} %collective-permute-done.2), channel_id=1, source_target_pairs={{0,14},{16,240},{2,0},{18,242},{4,2},{20,244},{6,4},{22,246},{8,6}... | collective-permute-start | bytes 1179656 | tf_op jit(solution)/shard_map/ppermute | solution.py:376
  31.1 5.6 %collective-permute-start.11 = (bf16[288,2048]{1,0:T(8,128)(2,1)S(1)}, bf16[288,2048]{1,0:T(8,128)(2,1)S(1)}, u32[]{:S(2)}, u32[]{:S(2)}) collective-permute-start(bf16[288,2048]{1,0:T(8,128)(2,1)S(1)} %constant_dynamic-update-slice_fusion.2.refs_0_), channel_id=1, source_target_pairs={{0,16},{16,0},{2,18},{18,2},{4,20},{20,4},{6,22},{22,6},{8,24},{24... | collective-permute-start | bytes 3538952 | tf_op jit(solution)/shard_map/ppermute | solution.py:360
  36.8 3.2 %collective-permute-start.7 = (bf16[96,2048]{1,0:T(8,128)(2,1)S(1)}, bf16[96,2048]{1,0:T(8,128)(2,1)S(1)}, u32[]{:S(2)}, u32[]{:S(2)}) collective-permute-start(bf16[96,2048]{1,0:T(8,128)(2,1)S(1)} %collective-permute-done.4), channel_id=1, source_target_pairs={{0,2},{16,48},{2,4},{18,50},{4,6},{20,52},{6,8},{22,54},{8,10},{24... | collective-permute-start | bytes 1179656 | tf_op jit(solution)/shard_map/ppermute | solution.py:375
  40.0 3.7 %collective-permute-start.6 = (bf16[192,2048]{1,0:T(8,128)(2,1)S(1)}, bf16[192,2048]{1,0:T(8,128)(2,1)S(1)}, u32[]{:S(2)}, u32[]{:S(2)}) collective-permute-start(bf16[192,2048]{1,0:T(8,128)(2,1)S(1)} %constant_dynamic-update-slice_fusion.6.refs_2_), channel_id=1, source_target_pairs={{0,1},{16,273},{2,3},{18,275},{4,5},{20,277},{6,7},{22,279},{8,9},... | collective-permute-start | bytes 2359304 | tf_op jit(solution)/shard_map/ppermute | solution.py:364
  43.8 3.8 %collective-permute-start.8 = (bf16[96,2048]{1,0:T(8,128)(2,1)S(1)}, bf16[96,2048]{1,0:T(8,128)(2,1)S(1)}, u32[]{:S(2)}, u32[]{:S(2)}) collective-permute-start(bf16[96,2048]{1,0:T(8,128)(2,1)S(1)} %collective-permute-done.5), channel_id=1, source_target_pairs={{0,14},{16,240},{2,0},{18,242},{4,2},{20,244},{6,4},{22,246},{8,6}... | collective-permute-start | bytes 1179656 | tf_op jit(solution)/shard_map/ppermute | solution.py:376
  47.6 1.9 %collective-permute-start.9 = (bf16[96,2048]{1,0:T(8,128)(2,1)S(1)}, bf16[96,2048]{1,0:T(8,128)(2,1)S(1)}, u32[]{:S(2)}, u32[]{:S(2)}) collective-permute-start(bf16[96,2048]{1,0:T(8,128)(2,1)S(1)} %collective-permute-done.7), channel_id=1, source_target_pairs={{0,2},{16,48},{2,4},{18,50},{4,6},{20,52},{6,8},{22,54},{8,10},{24... | collective-permute-start | bytes 1179656 | tf_op jit(solution)/shard_map/ppermute | solution.py:381
  49.6 2.5 %collective-permute-start.12 = (bf16[288,2048]{1,0:T(8,128)(2,1)S(1)}, bf16[288,2048]{1,0:T(8,128)(2,1)S(1)}, u32[]{:S(2)}, u32[]{:S(2)}) collective-permute-start(bf16[288,2048]{1,0:T(8,128)(2,1)S(1)} %collective-permute-done.3.refs_1_), channel_id=1, source_target_pairs={{0,16},{16,0},{2,18},{18,2},{4,20},{20,4},{6,22},{22,6},{8,24},{24... | collective-permute-start | bytes 3538952 | tf_op jit(solution)/shard_map/ppermute | solution.py:360
  52.6 5.0 %collective-permute-done.9 = bf16[96,2048]{1,0:T(8,128)(2,1)S(1)} collective-permute-done((bf16[96,2048]{1,0:T(8,128)(2,1)S(1)}, bf16[96,2048]{1,0:T(8,128)(2,1)S(1)}, u32[]{:S(2)}, u32[]{:S(2)}) %collective-permute-start.9) | collective-permute-done | bytes 393248 | tf_op jit(solution)/shard_map/ppermute | solution.py:381
  57.8 3.4 %collective-permute-start.15 = (bf16[288,2048]{1,0:T(8,128)(2,1)S(1)}, bf16[288,2048]{1,0:T(8,128)(2,1)S(1)}, u32[]{:S(2)}, u32[]{:S(2)}) collective-permute-start(bf16[288,2048]{1,0:T(8,128)(2,1)S(1)} %pad_maximum_fusion.refs_4_), channel_id=1, source_target_pairs={{0,16},{16,0},{2,18},{18,2},{4,20},{20,4},{6,22},{22,6},{8,24},{24... | collective-permute-start | bytes 3538952 | tf_op jit(solution)/shard_map/ppermute | solution.py:360
  61.1 4.4 %collective-permute-start.10 = (bf16[288,2048]{1,0:T(8,128)(2,1)S(1)}, bf16[288,2048]{1,0:T(8,128)(2,1)S(1)}, u32[]{:S(2)}, u32[]{:S(2)}) collective-permute-start(bf16[288,2048]{1,0:T(8,128)(2,1)S(1)} %pad_maximum_fusion.refs_4_), channel_id=1, source_target_pairs={{0,1},{16,273},{2,3},{18,275},{4,5},{20,277},{6,7},{22,279},{8,9},... | collective-permute-start | bytes 3538952 | tf_op jit(solution)/shard_map/ppermute | solution.py:364
  65.5 1.9 %collective-permute-start.13 = (bf16[192,2048]{1,0:T(8,128)(2,1)S(1)}, bf16[192,2048]{1,0:T(8,128)(2,1)S(1)}, u32[]{:S(2)}, u32[]{:S(2)}) collective-permute-start(bf16[192,2048]{1,0:T(8,128)(2,1)S(1)} %constant_dynamic-update-slice_fusion.6.refs_2_), channel_id=1, source_target_pairs={{0,16},{16,0},{2,18},{18,2},{4,20},{20,4},{6,22},{22,6},{8,24},{24... | collective-permute-start | bytes 2359304 | tf_op jit(solution)/shard_map/ppermute | solution.py:360
  67.4 2.4 %collective-permute-start.14 = (bf16[192,2048]{1,0:T(8,128)(2,1)S(1)}, bf16[192,2048]{1,0:T(8,128)(2,1)S(1)}, u32[]{:S(2)}, u32[]{:S(2)}) collective-permute-start(bf16[192,2048]{1,0:T(8,128)(2,1)S(1)} %collective-permute-done.6.refs_3_), channel_id=1, source_target_pairs={{0,16},{16,0},{2,18},{18,2},{4,20},{20,4},{6,22},{22,6},{8,24},{24... | collective-permute-start | bytes 2359304 | tf_op jit(solution)/shard_map/ppermute | solution.py:360
  69.9 1.9 %collective-permute-done.14.refs_7_.refs_8_.refs_9_ = bf16[192,2048]{1,0:T(8,128)(2,1)S(1)} collective-permute-done((bf16[192,2048]{1,0:T(8,128)(2,1)S(1)}, bf16[192,2048]{1,0:T(8,128)(2,1)S(1)}, u32[]{:S(2)}, u32[]{:S(2)}) %collective-permute-start.14) | collective-permute-done | bytes 786464 | tf_op jit(solution)/shard_map/ppermute | solution.py:360
  71.8 3.2 %shard_map.68.refs_10_ = f32[8,768]{1,0:T(8,128)S(1)} custom-call(bf16[288,2048]{1,0:T(8,128)(2,1)S(1)} %constant_dynamic-update-slice_fusion.2.refs_0_, bf16[288,2048]{1,0:T(8,128)(2,1)S(1)} %collective-permute-done.3.refs_1_, bf16[192,2048]{1,0:T(8,128)(2,1)S(1)} %constant_dynamic-update-slice_fusion.6.refs_2_, ...), custom_call_target="tpu_custom_call" | custom-call | flops 1887436800 | bytes 9830400 | tf_op jit(solution)/shard_map/pallas_call | solution.py:188
  75.0 4.3 %collective-permute-done.10.refs_5_ = bf16[288,2048]{1,0:T(8,128)(2,1)S(1)} collective-permute-done((bf16[288,2048]{1,0:T(8,128)(2,1)S(1)}, bf16[288,2048]{1,0:T(8,128)(2,1)S(1)}, u32[]{:S(2)}, u32[]{:S(2)}) %collective-permute-start.10) | collective-permute-done | bytes 1179680 | tf_op jit(solution)/shard_map/ppermute | solution.py:364
  79.3 2.1 %collective-permute-start.16 = (bf16[288,2048]{1,0:T(8,128)(2,1)S(1)}, bf16[288,2048]{1,0:T(8,128)(2,1)S(1)}, u32[]{:S(2)}, u32[]{:S(2)}) collective-permute-start(bf16[288,2048]{1,0:T(8,128)(2,1)S(1)} %collective-permute-done.10.refs_5_), channel_id=1, source_target_pairs={{0,16},{16,0},{2,18},{18,2},{4,20},{20,4},{6,22},{22,6},{8,24},{24... | collective-permute-start | bytes 3538952 | tf_op jit(solution)/shard_map/ppermute | solution.py:360
  81.4 2.4 %shard_map.69.refs_12_ = f32[8,1024]{1,0:T(8,128)S(1)} custom-call(bf16[288,2048]{1,0:T(8,128)(2,1)S(1)} %constant_dynamic-update-slice_fusion.2.refs_0_, bf16[288,2048]{1,0:T(8,128)(2,1)S(1)} %collective-permute-done.3.refs_1_, bf16[192,2048]{1,0:T(8,128)(2,1)S(1)} %constant_dynamic-update-slice_fusion.6.refs_2_, ...), custom_call_target="tpu_custom_call" | custom-call | flops 1384120320 | bytes 12779520 | tf_op jit(solution)/shard_map/pallas_call | solution.py:249
  84.0 5.6 %shard_map.70 = f32[16,6,8,128]{3,2,1,0:T(8,128)} custom-call(bf16[288,2048]{1,0:T(8,128)(2,1)S(1)} %constant_dynamic-update-slice_fusion.2.refs_0_, bf16[288,2048]{1,0:T(8,128)(2,1)S(1)} %collective-permute-done.3.refs_1_, bf16[192,2048]{1,0:T(8,128)(2,1)S(1)} %constant_dynamic-update-slice_fusion.6.refs_2_, ...), custom_call_target="tpu_custom_call" | custom-call | flops 2768240640 | bytes 15728640 | tf_op jit(solution)/shard_map/pallas_call | solution.py:290
  89.6 9.1 %all-to-all-start = ((f32[16,6,8,128]{3,2,1,0:T(8,128)}), f32[16,6,8,128]{3,2,1,0:T(8,128)S(1)}, u32[]{:S(2)}, u32[]{:S(2)}) async-start(f32[16,6,8,128]{3,2,1,0:T(8,128)} %shard_map.70), calls=%async_computation | async-start | bytes 786432 | tf_op jit(solution)/shard_map/all_to_all | solution.py:395
  98.7 12.0 %all-to-all-done.parts = f32[16,6,8,128]{3,2,1,0:T(8,128)S(1)} async-done(((f32[16,6,8,128]{3,2,1,0:T(8,128)}), f32[16,6,8,128]{3,2,1,0:T(8,128)S(1)}, u32[]{:S(2)}, u32[]{:S(2)}) %all-to-all-start) | async-done | bytes 393248 | tf_op jit(solution)/shard_map/all_to_all | solution.py:395
  110.7 0.9 shard_map.71
  111.6 1.9 %collective-permute-start.17 = (f32[1,128]{1,0:T(1,128)S(1)}, f32[1,128]{1,0:T(1,128)S(1)}, u32[]{:S(2)}, u32[]{:S(2)}) collective-permute-start(f32[1,128]{1,0:T(1,128)S(1)} %get-tuple-element.13), channel_id=1, source_target_pairs={{0,16},{16,0},{2,18},{18,2},{4,20},{20,4},{6,22},{22,6},{8,24},{24... | collective-permute-start | bytes 1544 | tf_op jit(solution)/shard_map/ppermute | solution.py:360
  113.5 5.1 %all-to-all-start.1 = ((f32[32,1,128]{2,1,0:T(1,128)}), f32[32,1,128]{2,1,0:T(1,128)S(1)}, u32[]{:S(2)}, u32[]{:S(2)}) async-start(f32[32,1,128]{2,1,0:T(1,128)} %get-tuple-element.14), calls=%async_computation.1 | async-start | bytes 32768 | tf_op jit(solution)/shard_map/all_to_all | solution.py:400
  119.3 8.4 %all-to-all-done.1 = f32[32,1,128]{2,1,0:T(1,128)S(1)} async-done(((f32[32,1,128]{2,1,0:T(1,128)}), f32[32,1,128]{2,1,0:T(1,128)S(1)}, u32[]{:S(2)}, u32[]{:S(2)}) %all-to-all-start.1) | async-done | bytes 16416 | tf_op jit(solution)/shard_map/all_to_all | solution.py:400
  (22 shorter events, 2.6 us)
Async XLA Ops:
  2.5 10.1 %collective-permute-start = (bf16[48,2048]{1,0:T(8,128)(2,1)}, bf16[48,2048]{1,0:T(8,128)(2,1)S(1)}, u32[]{:S(2)}, u32[]{:S(2)}) collective-permute-start(bf16[48,2048]{1,0:T(8,128)(2,1)} %get-tuple-element.10), channel_id=1, source_target_pairs={{0,16},{16,0},{2,18},{18,2},{4,20},{20,4},{6,22},{22,6},{8,24},{24... | collective-permute-start | bytes 589832 | tf_op jit(solution)/shard_map/ppermute | solution.py:360
  12.6 10.0 %collective-permute-start.1 = (bf16[96,2048]{1,0:T(8,128)(2,1)S(1)}, bf16[96,2048]{1,0:T(8,128)(2,1)S(1)}, u32[]{:S(2)}, u32[]{:S(2)}) collective-permute-start(bf16[96,2048]{1,0:T(8,128)(2,1)S(1)} %get-tuple-element.15), channel_id=1, source_target_pairs={{0,2},{16,48},{2,4},{18,50},{4,6},{20,52},{6,8},{22,54},{8,10},{24... | collective-permute-start | bytes 1179656 | tf_op jit(solution)/shard_map/ppermute | solution.py:375
  14.5 10.1 %collective-permute-start.2 = (bf16[96,2048]{1,0:T(8,128)(2,1)S(1)}, bf16[96,2048]{1,0:T(8,128)(2,1)S(1)}, u32[]{:S(2)}, u32[]{:S(2)}) collective-permute-start(bf16[96,2048]{1,0:T(8,128)(2,1)S(1)} %get-tuple-element.15), channel_id=1, source_target_pairs={{0,14},{16,240},{2,0},{18,242},{4,2},{20,244},{6,4},{22,246},{8,6}... | collective-permute-start | bytes 1179656 | tf_op jit(solution)/shard_map/ppermute | solution.py:376
  22.6 14.1 %collective-permute-start.4 = (bf16[96,2048]{1,0:T(8,128)(2,1)S(1)}, bf16[96,2048]{1,0:T(8,128)(2,1)S(1)}, u32[]{:S(2)}, u32[]{:S(2)}) collective-permute-start(bf16[96,2048]{1,0:T(8,128)(2,1)S(1)} %collective-permute-done.1), channel_id=1, source_target_pairs={{0,2},{16,48},{2,4},{18,50},{4,6},{20,52},{6,8},{22,54},{8,10},{24... | collective-permute-start | bytes 1179656 | tf_op jit(solution)/shard_map/ppermute | solution.py:375
  24.6 24.9 %collective-permute-start.3 = (bf16[288,2048]{1,0:T(8,128)(2,1)S(1)}, bf16[288,2048]{1,0:T(8,128)(2,1)S(1)}, u32[]{:S(2)}, u32[]{:S(2)}) collective-permute-start(bf16[288,2048]{1,0:T(8,128)(2,1)S(1)} %constant_dynamic-update-slice_fusion.2.refs_0_), channel_id=1, source_target_pairs={{0,1},{16,273},{2,3},{18,275},{4,5},{20,277},{6,7},{22,279},{8,9},... | collective-permute-start | bytes 3538952 | tf_op jit(solution)/shard_map/ppermute | solution.py:364
  26.5 13.5 %collective-permute-start.5 = (bf16[96,2048]{1,0:T(8,128)(2,1)S(1)}, bf16[96,2048]{1,0:T(8,128)(2,1)S(1)}, u32[]{:S(2)}, u32[]{:S(2)}) collective-permute-start(bf16[96,2048]{1,0:T(8,128)(2,1)S(1)} %collective-permute-done.2), channel_id=1, source_target_pairs={{0,14},{16,240},{2,0},{18,242},{4,2},{20,244},{6,4},{22,246},{8,6}... | collective-permute-start | bytes 1179656 | tf_op jit(solution)/shard_map/ppermute | solution.py:376
  31.1 36.3 %collective-permute-start.11 = (bf16[288,2048]{1,0:T(8,128)(2,1)S(1)}, bf16[288,2048]{1,0:T(8,128)(2,1)S(1)}, u32[]{:S(2)}, u32[]{:S(2)}) collective-permute-start(bf16[288,2048]{1,0:T(8,128)(2,1)S(1)} %constant_dynamic-update-slice_fusion.2.refs_0_), channel_id=1, source_target_pairs={{0,16},{16,0},{2,18},{18,2},{4,20},{20,4},{6,22},{22,6},{8,24},{24... | collective-permute-start | bytes 3538952 | tf_op jit(solution)/shard_map/ppermute | solution.py:360
  36.8 10.8 %collective-permute-start.7 = (bf16[96,2048]{1,0:T(8,128)(2,1)S(1)}, bf16[96,2048]{1,0:T(8,128)(2,1)S(1)}, u32[]{:S(2)}, u32[]{:S(2)}) collective-permute-start(bf16[96,2048]{1,0:T(8,128)(2,1)S(1)} %collective-permute-done.4), channel_id=1, source_target_pairs={{0,2},{16,48},{2,4},{18,50},{4,6},{20,52},{6,8},{22,54},{8,10},{24... | collective-permute-start | bytes 1179656 | tf_op jit(solution)/shard_map/ppermute | solution.py:375
  40.0 17.7 %collective-permute-start.6 = (bf16[192,2048]{1,0:T(8,128)(2,1)S(1)}, bf16[192,2048]{1,0:T(8,128)(2,1)S(1)}, u32[]{:S(2)}, u32[]{:S(2)}) collective-permute-start(bf16[192,2048]{1,0:T(8,128)(2,1)S(1)} %constant_dynamic-update-slice_fusion.6.refs_2_), channel_id=1, source_target_pairs={{0,1},{16,273},{2,3},{18,275},{4,5},{20,277},{6,7},{22,279},{8,9},... | collective-permute-start | bytes 2359304 | tf_op jit(solution)/shard_map/ppermute | solution.py:364
  43.8 8.8 %collective-permute-start.8 = (bf16[96,2048]{1,0:T(8,128)(2,1)S(1)}, bf16[96,2048]{1,0:T(8,128)(2,1)S(1)}, u32[]{:S(2)}, u32[]{:S(2)}) collective-permute-start(bf16[96,2048]{1,0:T(8,128)(2,1)S(1)} %collective-permute-done.5), channel_id=1, source_target_pairs={{0,14},{16,240},{2,0},{18,242},{4,2},{20,244},{6,4},{22,246},{8,6}... | collective-permute-start | bytes 1179656 | tf_op jit(solution)/shard_map/ppermute | solution.py:376
  47.6 10.0 %collective-permute-start.9 = (bf16[96,2048]{1,0:T(8,128)(2,1)S(1)}, bf16[96,2048]{1,0:T(8,128)(2,1)S(1)}, u32[]{:S(2)}, u32[]{:S(2)}) collective-permute-start(bf16[96,2048]{1,0:T(8,128)(2,1)S(1)} %collective-permute-done.7), channel_id=1, source_target_pairs={{0,2},{16,48},{2,4},{18,50},{4,6},{20,52},{6,8},{22,54},{8,10},{24... | collective-permute-start | bytes 1179656 | tf_op jit(solution)/shard_map/ppermute | solution.py:381
  49.6 22.2 %collective-permute-start.12 = (bf16[288,2048]{1,0:T(8,128)(2,1)S(1)}, bf16[288,2048]{1,0:T(8,128)(2,1)S(1)}, u32[]{:S(2)}, u32[]{:S(2)}) collective-permute-start(bf16[288,2048]{1,0:T(8,128)(2,1)S(1)} %collective-permute-done.3.refs_1_), channel_id=1, source_target_pairs={{0,16},{16,0},{2,18},{18,2},{4,20},{20,4},{6,22},{22,6},{8,24},{24... | collective-permute-start | bytes 3538952 | tf_op jit(solution)/shard_map/ppermute | solution.py:360
  57.8 17.2 %collective-permute-start.15 = (bf16[288,2048]{1,0:T(8,128)(2,1)S(1)}, bf16[288,2048]{1,0:T(8,128)(2,1)S(1)}, u32[]{:S(2)}, u32[]{:S(2)}) collective-permute-start(bf16[288,2048]{1,0:T(8,128)(2,1)S(1)} %pad_maximum_fusion.refs_4_), channel_id=1, source_target_pairs={{0,16},{16,0},{2,18},{18,2},{4,20},{20,4},{6,22},{22,6},{8,24},{24... | collective-permute-start | bytes 3538952 | tf_op jit(solution)/shard_map/ppermute | solution.py:360
  61.1 18.2 %collective-permute-start.10 = (bf16[288,2048]{1,0:T(8,128)(2,1)S(1)}, bf16[288,2048]{1,0:T(8,128)(2,1)S(1)}, u32[]{:S(2)}, u32[]{:S(2)}) collective-permute-start(bf16[288,2048]{1,0:T(8,128)(2,1)S(1)} %pad_maximum_fusion.refs_4_), channel_id=1, source_target_pairs={{0,1},{16,273},{2,3},{18,275},{4,5},{20,277},{6,7},{22,279},{8,9},... | collective-permute-start | bytes 3538952 | tf_op jit(solution)/shard_map/ppermute | solution.py:364
  65.5 4.4 %collective-permute-start.13 = (bf16[192,2048]{1,0:T(8,128)(2,1)S(1)}, bf16[192,2048]{1,0:T(8,128)(2,1)S(1)}, u32[]{:S(2)}, u32[]{:S(2)}) collective-permute-start(bf16[192,2048]{1,0:T(8,128)(2,1)S(1)} %constant_dynamic-update-slice_fusion.6.refs_2_), channel_id=1, source_target_pairs={{0,16},{16,0},{2,18},{18,2},{4,20},{20,4},{6,22},{22,6},{8,24},{24... | collective-permute-start | bytes 2359304 | tf_op jit(solution)/shard_map/ppermute | solution.py:360
  67.4 4.3 %collective-permute-start.14 = (bf16[192,2048]{1,0:T(8,128)(2,1)S(1)}, bf16[192,2048]{1,0:T(8,128)(2,1)S(1)}, u32[]{:S(2)}, u32[]{:S(2)}) collective-permute-start(bf16[192,2048]{1,0:T(8,128)(2,1)S(1)} %collective-permute-done.6.refs_3_), channel_id=1, source_target_pairs={{0,16},{16,0},{2,18},{18,2},{4,20},{20,4},{6,22},{22,6},{8,24},{24... | collective-permute-start | bytes 2359304 | tf_op jit(solution)/shard_map/ppermute | solution.py:360
  79.3 4.7 %collective-permute-start.16 = (bf16[288,2048]{1,0:T(8,128)(2,1)S(1)}, bf16[288,2048]{1,0:T(8,128)(2,1)S(1)}, u32[]{:S(2)}, u32[]{:S(2)}) collective-permute-start(bf16[288,2048]{1,0:T(8,128)(2,1)S(1)} %collective-permute-done.10.refs_5_), channel_id=1, source_target_pairs={{0,16},{16,0},{2,18},{18,2},{4,20},{20,4},{6,22},{22,6},{8,24},{24... | collective-permute-start | bytes 3538952 | tf_op jit(solution)/shard_map/ppermute | solution.py:360
  89.6 21.1 %all-to-all-start = ((f32[16,6,8,128]{3,2,1,0:T(8,128)}), f32[16,6,8,128]{3,2,1,0:T(8,128)S(1)}, u32[]{:S(2)}, u32[]{:S(2)}) async-start(f32[16,6,8,128]{3,2,1,0:T(8,128)} %shard_map.70), calls=%async_computation | async-start | bytes 786432 | tf_op jit(solution)/shard_map/all_to_all | solution.py:395
  111.6 7.1 %collective-permute-start.17 = (f32[1,128]{1,0:T(1,128)S(1)}, f32[1,128]{1,0:T(1,128)S(1)}, u32[]{:S(2)}, u32[]{:S(2)}) collective-permute-start(f32[1,128]{1,0:T(1,128)S(1)} %get-tuple-element.13), channel_id=1, source_target_pairs={{0,16},{16,0},{2,18},{18,2},{4,20},{20,4},{6,22},{22,6},{8,24},{24... | collective-permute-start | bytes 1544 | tf_op jit(solution)/shard_map/ppermute | solution.py:360
  113.5 14.2 %all-to-all-start.1 = ((f32[32,1,128]{2,1,0:T(1,128)}), f32[32,1,128]{2,1,0:T(1,128)S(1)}, u32[]{:S(2)}, u32[]{:S(2)}) async-start(f32[32,1,128]{2,1,0:T(1,128)} %get-tuple-element.14), calls=%async_computation.1 | async-start | bytes 32768 | tf_op jit(solution)/shard_map/all_to_all | solution.py:400

commit v7 on v6

--- a/solution.py
+++ b/solution.py
@@ -386,7 +386,7 @@
     other = [swap(v) for v in own]
     before = early(own, other, ds, dt)
     end_other = swap(end)
-    across_other = swap(after(end_across, before, end_other))
+    across_other = swap(after(end_across, before))
     own.append(end)
     other.append(end_other)
     before = between(own, other, before, known, ds, dt)

time: 131 us -> 129 us (0.985)
  waiting for transfers between devices: 36.2 us -> 30.2 us
  starting transfers between devices: 74.8 us -> 78.8 us
    ppermute x8, starting transfers between devices: 28.6 us -> 33.2 us  [swap(): return lax.ppermute(v, AXES, CORE_PAIRS)]
    ppermute x1, waiting for transfers between devices: 5.04 us -> 1.51 us  [shards(): last = lax.ppermute(up[3], AXES, UP)]
    ppermute x3, waiting for transfers between devices: 4.29 us -> 1.66 us  [pass_on(): return lax.ppermute(v, AXES, X_PAIRS)]
    ppermute x8, waiting for transfers between devices: 2.43 us -> 0.32 us  [swap(): return lax.ppermute(v, AXES, CORE_PAIRS)]
    ppermute x3, waiting for transfers between devices: 3.52 us -> 5.03 us  [shards(): up.append(lax.ppermute(up[-1], AXES, UP))]
  transfers between devices with their start and end apart: 20 -> 20, of which waited for: 9 -> 8; matrix products, arithmetic and copies ran while one was open for 1% -> 1% of each run, Pallas kernels for 4% -> 4%
where the time goes in v7:
time: 129 us; the launch traced here: 128 us
  starting transfers between devices  78.8 us (61%)
  waiting for transfers between devices  30.2 us (23%)
  Pallas kernels  14 us (11%)
  between operations  2.75 us (2%)
  other arithmetic  1.32 us (1%)
    ppermute x8, starting transfers between devices, swap(): return lax.ppermute(v, AXES, CORE_PAIRS)  33.2 us
    ppermute x3, starting transfers between devices, shards(): down.append(lax.ppermute(down[-1], AXES, DOWN))  14.2 us
    all_to_all x1, waiting for transfers between devices, shards(): parts = lax.all_to_all(stats, AXES, 0, 0, axis_index_groups=STAT_GROUPS)  12 us
    ppermute x3, starting transfers between devices, pass_on(): return lax.ppermute(v, AXES, X_PAIRS)  9.39 us
    all_to_all x1, starting transfers between devices, shards(): parts = lax.all_to_all(stats, AXES, 0, 0, axis_index_groups=STAT_GROUPS)  9.11 us
    all_to_all x1, waiting for transfers between devices, shards(): totals = lax.all_to_all(total, AXES, 0, 0, axis_index_groups=SUM_GROUPS)  8.44 us
    ppermute x3, starting transfers between devices, shards(): up.append(lax.ppermute(up[-1], AXES, UP))  5.74 us
    pallas_call x1, Pallas kernels, late(): pl.pallas_call(functools.partial(late_kernel, ds, dt, len(own), known), o...  5.61 us
  transfers between devices with their start and end apart: 20, of which 8 were waited for; matrix products, arithmetic and copies ran while one was open for 1% of the time, Pallas kernels for 4%

profile of v7, /device:TPU:1, one launch (start us, length us, event | category | flops | bytes accessed | tf_op | source)
XLA Modules:
  0.0 128.1 jit_solution(1672243445995600433)
XLA Ops:
  0.6 1.9 %shard_map.67 = (bf16[48,2048]{1,0:T(8,128)(2,1)}, bf16[48,2048]{1,0:T(8,128)(2,1)}) custom-call(bf16[48,512]{1,0:T(8,128)(2,1)} %image_s.1, bf16[48,512]{1,0:T(8,128)(2,1)} %text_s.1, bf16[48,768]{1,0:T(8,128)(2,1)} %image_t.1, bf16[48,768]{1,0:T(8,128)(2,1)} %text_t.1), custom_call_target="tpu_custom_call" | custom-call | tf_op jit(solution)/shard_map/pallas_call | solution.py:97
  2.5 8.8 %collective-permute-start = (bf16[48,2048]{1,0:T(8,128)(2,1)}, bf16[48,2048]{1,0:T(8,128)(2,1)S(1)}, u32[]{:S(2)}, u32[]{:S(2)}) collective-permute-start(bf16[48,2048]{1,0:T(8,128)(2,1)} %get-tuple-element.10), channel_id=1, source_target_pairs={{0,16},{16,0},{2,18},{18,2},{4,20},{20,4},{6,22},{22,6},{8,24},{24... | collective-permute-start | bytes 589832 | tf_op jit(solution)/shard_map/ppermute | solution.py:360
  11.3 1.0 constant_dynamic-update-slice_fusion.1
  12.6 1.9 %collective-permute-start.1 = (bf16[96,2048]{1,0:T(8,128)(2,1)S(1)}, bf16[96,2048]{1,0:T(8,128)(2,1)S(1)}, u32[]{:S(2)}, u32[]{:S(2)}) collective-permute-start(bf16[96,2048]{1,0:T(8,128)(2,1)S(1)} %get-tuple-element.15), channel_id=1, source_target_pairs={{0,2},{16,48},{2,4},{18,50},{4,6},{20,52},{6,8},{22,54},{8,10},{24... | collective-permute-start | bytes 1179656 | tf_op jit(solution)/shard_map/ppermute | solution.py:375
  14.5 4.6 %collective-permute-start.2 = (bf16[96,2048]{1,0:T(8,128)(2,1)S(1)}, bf16[96,2048]{1,0:T(8,128)(2,1)S(1)}, u32[]{:S(2)}, u32[]{:S(2)}) collective-permute-start(bf16[96,2048]{1,0:T(8,128)(2,1)S(1)} %get-tuple-element.15), channel_id=1, source_target_pairs={{0,14},{16,240},{2,0},{18,242},{4,2},{20,244},{6,4},{22,246},{8,6}... | collective-permute-start | bytes 1179656 | tf_op jit(solution)/shard_map/ppermute | solution.py:376
  19.1 3.5 %collective-permute-done.1 = bf16[96,2048]{1,0:T(8,128)(2,1)S(1)} collective-permute-done((bf16[96,2048]{1,0:T(8,128)(2,1)S(1)}, bf16[96,2048]{1,0:T(8,128)(2,1)S(1)}, u32[]{:S(2)}, u32[]{:S(2)}) %collective-permute-start.1) | collective-permute-done | bytes 393248 | tf_op jit(solution)/shard_map/ppermute | solution.py:375
  22.6 1.9 %collective-permute-start.4 = (bf16[96,2048]{1,0:T(8,128)(2,1)S(1)}, bf16[96,2048]{1,0:T(8,128)(2,1)S(1)}, u32[]{:S(2)}, u32[]{:S(2)}) collective-permute-start(bf16[96,2048]{1,0:T(8,128)(2,1)S(1)} %collective-permute-done.1), channel_id=1, source_target_pairs={{0,2},{16,48},{2,4},{18,50},{4,6},{20,52},{6,8},{22,54},{8,10},{24... | collective-permute-start | bytes 1179656 | tf_op jit(solution)/shard_map/ppermute | solution.py:375
  24.6 1.9 %collective-permute-start.3 = (bf16[288,2048]{1,0:T(8,128)(2,1)S(1)}, bf16[288,2048]{1,0:T(8,128)(2,1)S(1)}, u32[]{:S(2)}, u32[]{:S(2)}) collective-permute-start(bf16[288,2048]{1,0:T(8,128)(2,1)S(1)} %constant_dynamic-update-slice_fusion.2.refs_0_), channel_id=1, source_target_pairs={{0,1},{16,273},{2,3},{18,275},{4,5},{20,277},{6,7},{22,279},{8,9},... | collective-permute-start | bytes 3538952 | tf_op jit(solution)/shard_map/ppermute | solution.py:364
  26.5 4.6 %collective-permute-start.5 = (bf16[96,2048]{1,0:T(8,128)(2,1)S(1)}, bf16[96,2048]{1,0:T(8,128)(2,1)S(1)}, u32[]{:S(2)}, u32[]{:S(2)}) collective-permute-start(bf16[96,2048]{1,0:T(8,128)(2,1)S(1)} %collective-permute-done.2), channel_id=1, source_target_pairs={{0,14},{16,240},{2,0},{18,242},{4,2},{20,244},{6,4},{22,246},{8,6}... | collective-permute-start | bytes 1179656 | tf_op jit(solution)/shard_map/ppermute | solution.py:376
  31.1 1.5 %collective-permute-done.4 = bf16[96,2048]{1,0:T(8,128)(2,1)S(1)} collective-permute-done((bf16[96,2048]{1,0:T(8,128)(2,1)S(1)}, bf16[96,2048]{1,0:T(8,128)(2,1)S(1)}, u32[]{:S(2)}, u32[]{:S(2)}) %collective-permute-start.4) | collective-permute-done | bytes 393248 | tf_op jit(solution)/shard_map/ppermute | solution.py:375
  32.6 1.9 %collective-permute-start.7 = (bf16[96,2048]{1,0:T(8,128)(2,1)S(1)}, bf16[96,2048]{1,0:T(8,128)(2,1)S(1)}, u32[]{:S(2)}, u32[]{:S(2)}) collective-permute-start(bf16[96,2048]{1,0:T(8,128)(2,1)S(1)} %collective-permute-done.4), channel_id=1, source_target_pairs={{0,2},{16,48},{2,4},{18,50},{4,6},{20,52},{6,8},{22,54},{8,10},{24... | collective-permute-start | bytes 1179656 | tf_op jit(solution)/shard_map/ppermute | solution.py:375
  34.6 1.2 collective-permute-done.5
  35.8 4.6 %collective-permute-start.6 = (bf16[192,2048]{1,0:T(8,128)(2,1)S(1)}, bf16[192,2048]{1,0:T(8,128)(2,1)S(1)}, u32[]{:S(2)}, u32[]{:S(2)}) collective-permute-start(bf16[192,2048]{1,0:T(8,128)(2,1)S(1)} %constant_dynamic-update-slice_fusion.6.refs_2_), channel_id=1, source_target_pairs={{0,1},{16,273},{2,3},{18,275},{4,5},{20,277},{6,7},{22,279},{8,9},... | collective-permute-start | bytes 2359304 | tf_op jit(solution)/shard_map/ppermute | solution.py:364
  40.4 5.0 %collective-permute-start.8 = (bf16[96,2048]{1,0:T(8,128)(2,1)S(1)}, bf16[96,2048]{1,0:T(8,128)(2,1)S(1)}, u32[]{:S(2)}, u32[]{:S(2)}) collective-permute-start(bf16[96,2048]{1,0:T(8,128)(2,1)S(1)} %collective-permute-done.5), channel_id=1, source_target_pairs={{0,14},{16,240},{2,0},{18,242},{4,2},{20,244},{6,4},{22,246},{8,6}... | collective-permute-start | bytes 1179656 | tf_op jit(solution)/shard_map/ppermute | solution.py:376
  45.5 1.9 %collective-permute-start.9 = (bf16[96,2048]{1,0:T(8,128)(2,1)S(1)}, bf16[96,2048]{1,0:T(8,128)(2,1)S(1)}, u32[]{:S(2)}, u32[]{:S(2)}) collective-permute-start(bf16[96,2048]{1,0:T(8,128)(2,1)S(1)} %collective-permute-done.7), channel_id=1, source_target_pairs={{0,2},{16,48},{2,4},{18,50},{4,6},{20,52},{6,8},{22,54},{8,10},{24... | collective-permute-start | bytes 1179656 | tf_op jit(solution)/shard_map/ppermute | solution.py:381
  47.4 4.6 %collective-permute-start.11 = (bf16[288,2048]{1,0:T(8,128)(2,1)S(1)}, bf16[288,2048]{1,0:T(8,128)(2,1)S(1)}, u32[]{:S(2)}, u32[]{:S(2)}) collective-permute-start(bf16[288,2048]{1,0:T(8,128)(2,1)S(1)} %constant_dynamic-update-slice_fusion.2.refs_0_), channel_id=1, source_target_pairs={{0,16},{16,0},{2,18},{18,2},{4,20},{20,4},{6,22},{22,6},{8,24},{24... | collective-permute-start | bytes 3538952 | tf_op jit(solution)/shard_map/ppermute | solution.py:360
  52.1 1.9 %collective-permute-start.12 = (bf16[288,2048]{1,0:T(8,128)(2,1)S(1)}, bf16[288,2048]{1,0:T(8,128)(2,1)S(1)}, u32[]{:S(2)}, u32[]{:S(2)}) collective-permute-start(bf16[288,2048]{1,0:T(8,128)(2,1)S(1)} %collective-permute-done.3.refs_1_), channel_id=1, source_target_pairs={{0,16},{16,0},{2,18},{18,2},{4,20},{20,4},{6,22},{22,6},{8,24},{24... | collective-permute-start | bytes 3538952 | tf_op jit(solution)/shard_map/ppermute | solution.py:360
  54.0 1.5 %collective-permute-done.9 = bf16[96,2048]{1,0:T(8,128)(2,1)S(1)} collective-permute-done((bf16[96,2048]{1,0:T(8,128)(2,1)S(1)}, bf16[96,2048]{1,0:T(8,128)(2,1)S(1)}, u32[]{:S(2)}, u32[]{:S(2)}) %collective-permute-start.9) | collective-permute-done | bytes 393248 | tf_op jit(solution)/shard_map/ppermute | solution.py:381
  55.6 2.9 %collective-permute-start.10 = (bf16[288,2048]{1,0:T(8,128)(2,1)S(1)}, bf16[288,2048]{1,0:T(8,128)(2,1)S(1)}, u32[]{:S(2)}, u32[]{:S(2)}) collective-permute-start(bf16[288,2048]{1,0:T(8,128)(2,1)S(1)} %pad_maximum_fusion.refs_4_), channel_id=1, source_target_pairs={{0,1},{16,273},{2,3},{18,275},{4,5},{20,277},{6,7},{22,279},{8,9},... | collective-permute-start | bytes 3538952 | tf_op jit(solution)/shard_map/ppermute | solution.py:364
  58.5 6.0 %collective-permute-start.13 = (bf16[192,2048]{1,0:T(8,128)(2,1)S(1)}, bf16[192,2048]{1,0:T(8,128)(2,1)S(1)}, u32[]{:S(2)}, u32[]{:S(2)}) collective-permute-start(bf16[192,2048]{1,0:T(8,128)(2,1)S(1)} %constant_dynamic-update-slice_fusion.6.refs_2_), channel_id=1, source_target_pairs={{0,16},{16,0},{2,18},{18,2},{4,20},{20,4},{6,22},{22,6},{8,24},{24... | collective-permute-start | bytes 2359304 | tf_op jit(solution)/shard_map/ppermute | solution.py:360
  64.5 1.9 %collective-permute-start.14 = (bf16[192,2048]{1,0:T(8,128)(2,1)S(1)}, bf16[192,2048]{1,0:T(8,128)(2,1)S(1)}, u32[]{:S(2)}, u32[]{:S(2)}) collective-permute-start(bf16[192,2048]{1,0:T(8,128)(2,1)S(1)} %collective-permute-done.6.refs_3_), channel_id=1, source_target_pairs={{0,16},{16,0},{2,18},{18,2},{4,20},{20,4},{6,22},{22,6},{8,24},{24... | collective-permute-start | bytes 2359304 | tf_op jit(solution)/shard_map/ppermute | solution.py:360
  66.5 2.4 %collective-permute-start.15 = (bf16[288,2048]{1,0:T(8,128)(2,1)S(1)}, bf16[288,2048]{1,0:T(8,128)(2,1)S(1)}, u32[]{:S(2)}, u32[]{:S(2)}) collective-permute-start(bf16[288,2048]{1,0:T(8,128)(2,1)S(1)} %pad_maximum_fusion.refs_4_), channel_id=1, source_target_pairs={{0,16},{16,0},{2,18},{18,2},{4,20},{20,4},{6,22},{22,6},{8,24},{24... | collective-permute-start | bytes 3538952 | tf_op jit(solution)/shard_map/ppermute | solution.py:360
  68.9 3.2 %shard_map.68.refs_10_ = f32[8,768]{1,0:T(8,128)S(1)} custom-call(bf16[288,2048]{1,0:T(8,128)(2,1)S(1)} %constant_dynamic-update-slice_fusion.2.refs_0_, bf16[288,2048]{1,0:T(8,128)(2,1)S(1)} %collective-permute-done.3.refs_1_, bf16[192,2048]{1,0:T(8,128)(2,1)S(1)} %constant_dynamic-update-slice_fusion.6.refs_2_, ...), custom_call_target="tpu_custom_call" | custom-call | flops 1887436800 | bytes 9830400 | tf_op jit(solution)/shard_map/pallas_call | solution.py:188
  72.1 1.7 %collective-permute-done.10.refs_5_ = bf16[288,2048]{1,0:T(8,128)(2,1)S(1)} collective-permute-done((bf16[288,2048]{1,0:T(8,128)(2,1)S(1)}, bf16[288,2048]{1,0:T(8,128)(2,1)S(1)}, u32[]{:S(2)}, u32[]{:S(2)}) %collective-permute-start.10) | collective-permute-done | bytes 1179680 | tf_op jit(solution)/shard_map/ppermute | solution.py:364
  73.8 5.6 %collective-permute-start.16 = (bf16[288,2048]{1,0:T(8,128)(2,1)S(1)}, bf16[288,2048]{1,0:T(8,128)(2,1)S(1)}, u32[]{:S(2)}, u32[]{:S(2)}) collective-permute-start(bf16[288,2048]{1,0:T(8,128)(2,1)S(1)} %collective-permute-done.10.refs_5_), channel_id=1, source_target_pairs={{0,16},{16,0},{2,18},{18,2},{4,20},{20,4},{6,22},{22,6},{8,24},{24... | collective-permute-start | bytes 3538952 | tf_op jit(solution)/shard_map/ppermute | solution.py:360
  79.4 2.4 %shard_map.69.refs_12_ = f32[8,1024]{1,0:T(8,128)S(1)} custom-call(bf16[288,2048]{1,0:T(8,128)(2,1)S(1)} %constant_dynamic-update-slice_fusion.2.refs_0_, bf16[288,2048]{1,0:T(8,128)(2,1)S(1)} %collective-permute-done.3.refs_1_, bf16[192,2048]{1,0:T(8,128)(2,1)S(1)} %constant_dynamic-update-slice_fusion.6.refs_2_, ...), custom_call_target="tpu_custom_call" | custom-call | flops 1384120320 | bytes 12779520 | tf_op jit(solution)/shard_map/pallas_call | solution.py:249
  81.8 5.6 %shard_map.70 = f32[16,6,8,128]{3,2,1,0:T(8,128)} custom-call(bf16[288,2048]{1,0:T(8,128)(2,1)S(1)} %constant_dynamic-update-slice_fusion.2.refs_0_, bf16[288,2048]{1,0:T(8,128)(2,1)S(1)} %collective-permute-done.3.refs_1_, bf16[192,2048]{1,0:T(8,128)(2,1)S(1)} %constant_dynamic-update-slice_fusion.6.refs_2_, ...), custom_call_target="tpu_custom_call" | custom-call | flops 2768240640 | bytes 15728640 | tf_op jit(solution)/shard_map/pallas_call | solution.py:290
  87.4 9.1 %all-to-all-start = ((f32[16,6,8,128]{3,2,1,0:T(8,128)}), f32[16,6,8,128]{3,2,1,0:T(8,128)S(1)}, u32[]{:S(2)}, u32[]{:S(2)}) async-start(f32[16,6,8,128]{3,2,1,0:T(8,128)} %shard_map.70), calls=%async_computation | async-start | bytes 786432 | tf_op jit(solution)/shard_map/all_to_all | solution.py:395
  96.5 12.0 %all-to-all-done.parts = f32[16,6,8,128]{3,2,1,0:T(8,128)S(1)} async-done(((f32[16,6,8,128]{3,2,1,0:T(8,128)}), f32[16,6,8,128]{3,2,1,0:T(8,128)S(1)}, u32[]{:S(2)}, u32[]{:S(2)}) %all-to-all-start) | async-done | bytes 393248 | tf_op jit(solution)/shard_map/all_to_all | solution.py:395
  109.4 1.9 %collective-permute-start.17 = (f32[1,128]{1,0:T(1,128)S(1)}, f32[1,128]{1,0:T(1,128)S(1)}, u32[]{:S(2)}, u32[]{:S(2)}) collective-permute-start(f32[1,128]{1,0:T(1,128)S(1)} %get-tuple-element.13), channel_id=1, source_target_pairs={{0,16},{16,0},{2,18},{18,2},{4,20},{20,4},{6,22},{22,6},{8,24},{24... | collective-permute-start | bytes 1544 | tf_op jit(solution)/shard_map/ppermute | solution.py:360
  111.3 5.3 %all-to-all-start.1 = ((f32[32,1,128]{2,1,0:T(1,128)}), f32[32,1,128]{2,1,0:T(1,128)S(1)}, u32[]{:S(2)}, u32[]{:S(2)}) async-start(f32[32,1,128]{2,1,0:T(1,128)} %get-tuple-element.14), calls=%async_computation.1 | async-start | bytes 32768 | tf_op jit(solution)/shard_map/all_to_all | solution.py:400
  117.3 8.4 %all-to-all-done.1 = f32[32,1,128]{2,1,0:T(1,128)S(1)} async-done(((f32[32,1,128]{2,1,0:T(1,128)}), f32[32,1,128]{2,1,0:T(1,128)S(1)}, u32[]{:S(2)}, u32[]{:S(2)}) %all-to-all-start.1) | async-done | bytes 16416 | tf_op jit(solution)/shard_map/all_to_all | solution.py:400
  (22 shorter events, 2.7 us)
Async XLA Ops:
  2.5 10.1 %collective-permute-start = (bf16[48,2048]{1,0:T(8,128)(2,1)}, bf16[48,2048]{1,0:T(8,128)(2,1)S(1)}, u32[]{:S(2)}, u32[]{:S(2)}) collective-permute-start(bf16[48,2048]{1,0:T(8,128)(2,1)} %get-tuple-element.10), channel_id=1, source_target_pairs={{0,16},{16,0},{2,18},{18,2},{4,20},{20,4},{6,22},{22,6},{8,24},{24... | collective-permute-start | bytes 589832 | tf_op jit(solution)/shard_map/ppermute | solution.py:360
  12.6 10.0 %collective-permute-start.1 = (bf16[96,2048]{1,0:T(8,128)(2,1)S(1)}, bf16[96,2048]{1,0:T(8,128)(2,1)S(1)}, u32[]{:S(2)}, u32[]{:S(2)}) collective-permute-start(bf16[96,2048]{1,0:T(8,128)(2,1)S(1)} %get-tuple-element.15), channel_id=1, source_target_pairs={{0,2},{16,48},{2,4},{18,50},{4,6},{20,52},{6,8},{22,54},{8,10},{24... | collective-permute-start | bytes 1179656 | tf_op jit(solution)/shard_map/ppermute | solution.py:375
  14.5 10.1 %collective-permute-start.2 = (bf16[96,2048]{1,0:T(8,128)(2,1)S(1)}, bf16[96,2048]{1,0:T(8,128)(2,1)S(1)}, u32[]{:S(2)}, u32[]{:S(2)}) collective-permute-start(bf16[96,2048]{1,0:T(8,128)(2,1)S(1)} %get-tuple-element.15), channel_id=1, source_target_pairs={{0,14},{16,240},{2,0},{18,242},{4,2},{20,244},{6,4},{22,246},{8,6}... | collective-permute-start | bytes 1179656 | tf_op jit(solution)/shard_map/ppermute | solution.py:376
  22.6 10.0 %collective-permute-start.4 = (bf16[96,2048]{1,0:T(8,128)(2,1)S(1)}, bf16[96,2048]{1,0:T(8,128)(2,1)S(1)}, u32[]{:S(2)}, u32[]{:S(2)}) collective-permute-start(bf16[96,2048]{1,0:T(8,128)(2,1)S(1)} %collective-permute-done.1), channel_id=1, source_target_pairs={{0,2},{16,48},{2,4},{18,50},{4,6},{20,52},{6,8},{22,54},{8,10},{24... | collective-permute-start | bytes 1179656 | tf_op jit(solution)/shard_map/ppermute | solution.py:375
  24.6 27.4 %collective-permute-start.3 = (bf16[288,2048]{1,0:T(8,128)(2,1)S(1)}, bf16[288,2048]{1,0:T(8,128)(2,1)S(1)}, u32[]{:S(2)}, u32[]{:S(2)}) collective-permute-start(bf16[288,2048]{1,0:T(8,128)(2,1)S(1)} %constant_dynamic-update-slice_fusion.2.refs_0_), channel_id=1, source_target_pairs={{0,1},{16,273},{2,3},{18,275},{4,5},{20,277},{6,7},{22,279},{8,9},... | collective-permute-start | bytes 3538952 | tf_op jit(solution)/shard_map/ppermute | solution.py:364
  26.5 9.3 %collective-permute-start.5 = (bf16[96,2048]{1,0:T(8,128)(2,1)S(1)}, bf16[96,2048]{1,0:T(8,128)(2,1)S(1)}, u32[]{:S(2)}, u32[]{:S(2)}) collective-permute-start(bf16[96,2048]{1,0:T(8,128)(2,1)S(1)} %collective-permute-done.2), channel_id=1, source_target_pairs={{0,14},{16,240},{2,0},{18,242},{4,2},{20,244},{6,4},{22,246},{8,6}... | collective-permute-start | bytes 1179656 | tf_op jit(solution)/shard_map/ppermute | solution.py:376
  32.6 12.8 %collective-permute-start.7 = (bf16[96,2048]{1,0:T(8,128)(2,1)S(1)}, bf16[96,2048]{1,0:T(8,128)(2,1)S(1)}, u32[]{:S(2)}, u32[]{:S(2)}) collective-permute-start(bf16[96,2048]{1,0:T(8,128)(2,1)S(1)} %collective-permute-done.4), channel_id=1, source_target_pairs={{0,2},{16,48},{2,4},{18,50},{4,6},{20,52},{6,8},{22,54},{8,10},{24... | collective-permute-start | bytes 1179656 | tf_op jit(solution)/shard_map/ppermute | solution.py:375
  35.8 19.8 %collective-permute-start.6 = (bf16[192,2048]{1,0:T(8,128)(2,1)S(1)}, bf16[192,2048]{1,0:T(8,128)(2,1)S(1)}, u32[]{:S(2)}, u32[]{:S(2)}) collective-permute-start(bf16[192,2048]{1,0:T(8,128)(2,1)S(1)} %constant_dynamic-update-slice_fusion.6.refs_2_), channel_id=1, source_target_pairs={{0,1},{16,273},{2,3},{18,275},{4,5},{20,277},{6,7},{22,279},{8,9},... | collective-permute-start | bytes 2359304 | tf_op jit(solution)/shard_map/ppermute | solution.py:364
  40.4 13.6 %collective-permute-start.8 = (bf16[96,2048]{1,0:T(8,128)(2,1)S(1)}, bf16[96,2048]{1,0:T(8,128)(2,1)S(1)}, u32[]{:S(2)}, u32[]{:S(2)}) collective-permute-start(bf16[96,2048]{1,0:T(8,128)(2,1)S(1)} %collective-permute-done.5), channel_id=1, source_target_pairs={{0,14},{16,240},{2,0},{18,242},{4,2},{20,244},{6,4},{22,246},{8,6}... | collective-permute-start | bytes 1179656 | tf_op jit(solution)/shard_map/ppermute | solution.py:376
  45.5 10.0 %collective-permute-start.9 = (bf16[96,2048]{1,0:T(8,128)(2,1)S(1)}, bf16[96,2048]{1,0:T(8,128)(2,1)S(1)}, u32[]{:S(2)}, u32[]{:S(2)}) collective-permute-start(bf16[96,2048]{1,0:T(8,128)(2,1)S(1)} %collective-permute-done.7), channel_id=1, source_target_pairs={{0,2},{16,48},{2,4},{18,50},{4,6},{20,52},{6,8},{22,54},{8,10},{24... | collective-permute-start | bytes 1179656 | tf_op jit(solution)/shard_map/ppermute | solution.py:381
  47.4 19.0 %collective-permute-start.11 = (bf16[288,2048]{1,0:T(8,128)(2,1)S(1)}, bf16[288,2048]{1,0:T(8,128)(2,1)S(1)}, u32[]{:S(2)}, u32[]{:S(2)}) collective-permute-start(bf16[288,2048]{1,0:T(8,128)(2,1)S(1)} %constant_dynamic-update-slice_fusion.2.refs_0_), channel_id=1, source_target_pairs={{0,16},{16,0},{2,18},{18,2},{4,20},{20,4},{6,22},{22,6},{8,24},{24... | collective-permute-start | bytes 3538952 | tf_op jit(solution)/shard_map/ppermute | solution.py:360
  52.1 16.8 %collective-permute-start.12 = (bf16[288,2048]{1,0:T(8,128)(2,1)S(1)}, bf16[288,2048]{1,0:T(8,128)(2,1)S(1)}, u32[]{:S(2)}, u32[]{:S(2)}) collective-permute-start(bf16[288,2048]{1,0:T(8,128)(2,1)S(1)} %collective-permute-done.3.refs_1_), channel_id=1, source_target_pairs={{0,16},{16,0},{2,18},{18,2},{4,20},{20,4},{6,22},{22,6},{8,24},{24... | collective-permute-start | bytes 3538952 | tf_op jit(solution)/shard_map/ppermute | solution.py:360
  55.6 18.2 %collective-permute-start.10 = (bf16[288,2048]{1,0:T(8,128)(2,1)S(1)}, bf16[288,2048]{1,0:T(8,128)(2,1)S(1)}, u32[]{:S(2)}, u32[]{:S(2)}) collective-permute-start(bf16[288,2048]{1,0:T(8,128)(2,1)S(1)} %pad_maximum_fusion.refs_4_), channel_id=1, source_target_pairs={{0,1},{16,273},{2,3},{18,275},{4,5},{20,277},{6,7},{22,279},{8,9},... | collective-permute-start | bytes 3538952 | tf_op jit(solution)/shard_map/ppermute | solution.py:364
  58.5 10.4 %collective-permute-start.13 = (bf16[192,2048]{1,0:T(8,128)(2,1)S(1)}, bf16[192,2048]{1,0:T(8,128)(2,1)S(1)}, u32[]{:S(2)}, u32[]{:S(2)}) collective-permute-start(bf16[192,2048]{1,0:T(8,128)(2,1)S(1)} %constant_dynamic-update-slice_fusion.6.refs_2_), channel_id=1, source_target_pairs={{0,16},{16,0},{2,18},{18,2},{4,20},{20,4},{6,22},{22,6},{8,24},{24... | collective-permute-start | bytes 2359304 | tf_op jit(solution)/shard_map/ppermute | solution.py:360
  64.5 4.4 %collective-permute-start.14 = (bf16[192,2048]{1,0:T(8,128)(2,1)S(1)}, bf16[192,2048]{1,0:T(8,128)(2,1)S(1)}, u32[]{:S(2)}, u32[]{:S(2)}) collective-permute-start(bf16[192,2048]{1,0:T(8,128)(2,1)S(1)} %collective-permute-done.6.refs_3_), channel_id=1, source_target_pairs={{0,16},{16,0},{2,18},{18,2},{4,20},{20,4},{6,22},{22,6},{8,24},{24... | collective-permute-start | bytes 2359304 | tf_op jit(solution)/shard_map/ppermute | solution.py:360
  66.5 12.9 %collective-permute-start.15 = (bf16[288,2048]{1,0:T(8,128)(2,1)S(1)}, bf16[288,2048]{1,0:T(8,128)(2,1)S(1)}, u32[]{:S(2)}, u32[]{:S(2)}) collective-permute-start(bf16[288,2048]{1,0:T(8,128)(2,1)S(1)} %pad_maximum_fusion.refs_4_), channel_id=1, source_target_pairs={{0,16},{16,0},{2,18},{18,2},{4,20},{20,4},{6,22},{22,6},{8,24},{24... | collective-permute-start | bytes 3538952 | tf_op jit(solution)/shard_map/ppermute | solution.py:360
  73.8 8.0 %collective-permute-start.16 = (bf16[288,2048]{1,0:T(8,128)(2,1)S(1)}, bf16[288,2048]{1,0:T(8,128)(2,1)S(1)}, u32[]{:S(2)}, u32[]{:S(2)}) collective-permute-start(bf16[288,2048]{1,0:T(8,128)(2,1)S(1)} %collective-permute-done.10.refs_5_), channel_id=1, source_target_pairs={{0,16},{16,0},{2,18},{18,2},{4,20},{20,4},{6,22},{22,6},{8,24},{24... | collective-permute-start | bytes 3538952 | tf_op jit(solution)/shard_map/ppermute | solution.py:360
  87.4 21.1 %all-to-all-start = ((f32[16,6,8,128]{3,2,1,0:T(8,128)}), f32[16,6,8,128]{3,2,1,0:T(8,128)S(1)}, u32[]{:S(2)}, u32[]{:S(2)}) async-start(f32[16,6,8,128]{3,2,1,0:T(8,128)} %shard_map.70), calls=%async_computation | async-start | bytes 786432 | tf_op jit(solution)/shard_map/all_to_all | solution.py:395
  109.4 7.3 %collective-permute-start.17 = (f32[1,128]{1,0:T(1,128)S(1)}, f32[1,128]{1,0:T(1,128)S(1)}, u32[]{:S(2)}, u32[]{:S(2)}) collective-permute-start(f32[1,128]{1,0:T(1,128)S(1)} %get-tuple-element.13), channel_id=1, source_target_pairs={{0,16},{16,0},{2,18},{18,2},{4,20},{20,4},{6,22},{22,6},{8,24},{24... | collective-permute-start | bytes 1544 | tf_op jit(solution)/shard_map/ppermute | solution.py:360
  111.3 14.4 %all-to-all-start.1 = ((f32[32,1,128]{2,1,0:T(1,128)}), f32[32,1,128]{2,1,0:T(1,128)S(1)}, u32[]{:S(2)}, u32[]{:S(2)}) async-start(f32[32,1,128]{2,1,0:T(1,128)} %get-tuple-element.14), calls=%async_computation.1 | async-start | bytes 32768 | tf_op jit(solution)/shard_map/all_to_all | solution.py:400

commit v8 on v7

--- a/solution.py
+++ b/solution.py
@@ -275,9 +275,10 @@
         mine, across = (stats[:4, places[step, p] : places[step, p] + 2 * SHARD] for p in (0, 1))
         v = jnp.concatenate([jnp.where(xi == 0, mine, across), jnp.where(xi == 0, across, mine)], axis=1)
         row = pl.ds(lax.rem(line + step, 8), 1)
-        for n in range(4):
+        for n in range(3):
             out[0, n, row, :] = v[n : n + 1, :128]
-            out[0, 4 + n // 2, row, (n % 2) * 64 : (n % 2 + 1) * 64] = v[n : n + 1, 128:]
+            out[0, 3 + n // 2, row, (n % 2) * 64 : (n % 2 + 1) * 64] = v[n : n + 1, 128:]
+        out[0, 4, row, 64:] = v[3:4, :64] + v[3:4, 64:128] + v[3:4, 128:]
     for k in range(1, out.shape[0]):
         out[k] = out[0]
 
@@ -289,7 +290,7 @@
     work = rows * rows - known * done * CHUNK
     return pl.pallas_call(
         functools.partial(late_kernel, ds, dt, len(own), known),
-        out_shape=jax.ShapeDtypeStruct((16, 6, 8, 128), jnp.float32),
+        out_shape=jax.ShapeDtypeStruct((16, 5, 8, 128), jnp.float32),
         in_specs=[vmem] * (len(own) + len(other) + 1),
         out_specs=vmem,
         scratch_shapes=scratch(rows, known) + [pltpu.VMEM((8, rows), jnp.float32)],
@@ -300,29 +301,26 @@
     )(*own, *other, before)
 
 
-def losses(parts, count, lse, mark, mean, diagonal):
+def losses(count, lse, mark, mean):
     top, high = lse(0), mark(0)
     for k in range(1, count):
         top = jnp.maximum(top, lse(k))
         high = jnp.maximum(high, mark(k))
-    spread = mass = weighted = own = jnp.zeros_like(top)
+    spread = mass = weighted = jnp.zeros_like(top)
     for k in range(count):
         e = jnp.exp(mark(k) - high)
         spread += jnp.exp(lse(k) - top)
         mass += e
         weighted += e * mean(k)
-        own += diagonal(k)
-    return top + jnp.log(spread) - 0.5 * own - 0.5 * weighted / mass
+    return top + jnp.log(spread) - 0.5 * weighted / mass
 
 
 def halves(parts, rows):
     count = parts.shape[0]
     return (
-        losses(parts, count, *(lambda k, n=n: parts[k, n, rows, :] for n in range(4))),
+        losses(count, *(lambda k, n=n: parts[k, n, rows, :] for n in range(3))),
         losses(
-            parts,
-            count,
-            *(lambda k, n=n: parts[k, 4 + n // 2, rows, (n % 2) * 64 : (n % 2 + 1) * 64] for n in range(4)),
+            count, *(lambda k, n=n: parts[k, 3 + n // 2, rows, (n % 2) * 64 : (n % 2 + 1) * 64] for n in range(3))
         ),
     )
 
@@ -330,11 +328,12 @@
 def finish_kernel(parts, mine, total, held):
     line, xi = where_am_i()
     one, two = halves(parts, slice(0, 8))
+    diagonal = jnp.sum(sum(parts[k, 4, :, 64:] for k in range(parts.shape[0])))
     held[:, :128] = one
     held[:, 128:] = jnp.concatenate([two, two], axis=1)
     v = held[pl.ds(line, 1), :]
     mine[...] = jnp.where(xi == 0, v[:, :128], v[:, 2 * SHARD : 2 * SHARD + 128])
-    total[...] = jnp.full(total.shape, jnp.sum(one) + jnp.sum(two), jnp.float32)
+    total[...] = jnp.full(total.shape, jnp.sum(one) + jnp.sum(two) - 0.5 * diagonal, jnp.float32)
 
 
 def finish(parts):
@@ -395,8 +394,10 @@
     parts = lax.all_to_all(stats, AXES, 0, 0, axis_index_groups=STAT_GROUPS)
     chip, total = finish(parts)
     first, second = chip[0, :SHARD], swap(chip)[0, SHARD : 2 * SHARD]
-    image_loss = jnp.where(core == 0, first, second)
-    text_loss = jnp.where(core == 0, second, first)
+    diagonal = jnp.sum(image_student.astype(jnp.float32) * text_student.astype(jnp.float32), axis=1)
+    diagonal *= 1.0 / math.sqrt(ds)
+    image_loss = jnp.where(core == 0, first, second) - diagonal
+    text_loss = jnp.where(core == 0, second, first) - diagonal
     totals = lax.all_to_all(total, AXES, 0, 0, axis_index_groups=SUM_GROUPS)
     return image_loss, text_loss, jnp.sum(totals[:, 0, 0]) / (2.0 * SHARD * 512)
 

time: 129 us -> 128 us (level)
  no operation moved by 1% of the time
where the time goes in v8:
time: 128 us
  starting transfers between devices  78.8 us (62%)
  waiting for transfers between devices  29.4 us (23%)
  Pallas kernels  14.1 us (11%)
  between operations  2.78 us (2%)
  other arithmetic  1.43 us (1%)
    ppermute x8, starting transfers between devices, swap(): return lax.ppermute(v, AXES, CORE_PAIRS)  33.2 us
    ppermute x3, starting transfers between devices, shards(): down.append(lax.ppermute(down[-1], AXES, DOWN))  14.2 us
    all_to_all x1, waiting for transfers between devices, shards(): parts = lax.all_to_all(stats, AXES, 0, 0, axis_index_groups=STAT_GROUPS)  11.2 us
    ppermute x3, starting transfers between devices, pass_on(): return lax.ppermute(v, AXES, X_PAIRS)  9.39 us
    all_to_all x1, starting transfers between devices, shards(): parts = lax.all_to_all(stats, AXES, 0, 0, axis_index_groups=STAT_GROUPS)  9.12 us
    all_to_all x1, waiting for transfers between devices, shards(): totals = lax.all_to_all(total, AXES, 0, 0, axis_index_groups=SUM_GROUPS)  8.45 us
    ppermute x3, starting transfers between devices, shards(): up.append(lax.ppermute(up[-1], AXES, UP))  5.74 us
    pallas_call x1, Pallas kernels, late(): pl.pallas_call(functools.partial(late_kernel, ds, dt, len(own), known), o...  5.71 us
  transfers between devices with their start and end apart: 20, of which 8 were waited for; matrix products, arithmetic and copies ran while one was open for 1% of the time, Pallas kernels for 4%

profile of v8, /device:TPU:1, one launch (start us, length us, event | category | flops | bytes accessed | tf_op | source)
XLA Modules:
  0.0 127.7 jit_solution(16281156775163481869)
XLA Ops:
  0.6 1.9 %shard_map.67 = (bf16[48,2048]{1,0:T(8,128)(2,1)}, bf16[48,2048]{1,0:T(8,128)(2,1)}) custom-call(bf16[48,512]{1,0:T(8,128)(2,1)} %image_s.1, bf16[48,512]{1,0:T(8,128)(2,1)} %text_s.1, bf16[48,768]{1,0:T(8,128)(2,1)} %image_t.1, bf16[48,768]{1,0:T(8,128)(2,1)} %text_t.1), custom_call_target="tpu_custom_call" | custom-call | tf_op jit(solution)/shard_map/pallas_call | solution.py:97
  2.5 8.8 %collective-permute-start = (bf16[48,2048]{1,0:T(8,128)(2,1)}, bf16[48,2048]{1,0:T(8,128)(2,1)S(1)}, u32[]{:S(2)}, u32[]{:S(2)}) collective-permute-start(bf16[48,2048]{1,0:T(8,128)(2,1)} %get-tuple-element.10), channel_id=1, source_target_pairs={{0,16},{16,0},{2,18},{18,2},{4,20},{20,4},{6,22},{22,6},{8,24},{24... | collective-permute-start | bytes 589832 | tf_op jit(solution)/shard_map/ppermute | solution.py:359
  11.3 1.0 constant_dynamic-update-slice_fusion.1
  12.6 1.9 %collective-permute-start.1 = (bf16[96,2048]{1,0:T(8,128)(2,1)S(1)}, bf16[96,2048]{1,0:T(8,128)(2,1)S(1)}, u32[]{:S(2)}, u32[]{:S(2)}) collective-permute-start(bf16[96,2048]{1,0:T(8,128)(2,1)S(1)} %get-tuple-element.15), channel_id=1, source_target_pairs={{0,2},{16,48},{2,4},{18,50},{4,6},{20,52},{6,8},{22,54},{8,10},{24... | collective-permute-start | bytes 1179656 | tf_op jit(solution)/shard_map/ppermute | solution.py:374
  14.5 4.6 %collective-permute-start.2 = (bf16[96,2048]{1,0:T(8,128)(2,1)S(1)}, bf16[96,2048]{1,0:T(8,128)(2,1)S(1)}, u32[]{:S(2)}, u32[]{:S(2)}) collective-permute-start(bf16[96,2048]{1,0:T(8,128)(2,1)S(1)} %get-tuple-element.15), channel_id=1, source_target_pairs={{0,14},{16,240},{2,0},{18,242},{4,2},{20,244},{6,4},{22,246},{8,6}... | collective-permute-start | bytes 1179656 | tf_op jit(solution)/shard_map/ppermute | solution.py:375
  19.1 3.5 %collective-permute-done.1 = bf16[96,2048]{1,0:T(8,128)(2,1)S(1)} collective-permute-done((bf16[96,2048]{1,0:T(8,128)(2,1)S(1)}, bf16[96,2048]{1,0:T(8,128)(2,1)S(1)}, u32[]{:S(2)}, u32[]{:S(2)}) %collective-permute-start.1) | collective-permute-done | bytes 393248 | tf_op jit(solution)/shard_map/ppermute | solution.py:374
  22.6 1.9 %collective-permute-start.4 = (bf16[96,2048]{1,0:T(8,128)(2,1)S(1)}, bf16[96,2048]{1,0:T(8,128)(2,1)S(1)}, u32[]{:S(2)}, u32[]{:S(2)}) collective-permute-start(bf16[96,2048]{1,0:T(8,128)(2,1)S(1)} %collective-permute-done.1), channel_id=1, source_target_pairs={{0,2},{16,48},{2,4},{18,50},{4,6},{20,52},{6,8},{22,54},{8,10},{24... | collective-permute-start | bytes 1179656 | tf_op jit(solution)/shard_map/ppermute | solution.py:374
  24.6 1.9 %collective-permute-start.3 = (bf16[288,2048]{1,0:T(8,128)(2,1)S(1)}, bf16[288,2048]{1,0:T(8,128)(2,1)S(1)}, u32[]{:S(2)}, u32[]{:S(2)}) collective-permute-start(bf16[288,2048]{1,0:T(8,128)(2,1)S(1)} %constant_dynamic-update-slice_fusion.2.refs_0_), channel_id=1, source_target_pairs={{0,1},{16,273},{2,3},{18,275},{4,5},{20,277},{6,7},{22,279},{8,9},... | collective-permute-start | bytes 3538952 | tf_op jit(solution)/shard_map/ppermute | solution.py:363
  26.5 4.6 %collective-permute-start.5 = (bf16[96,2048]{1,0:T(8,128)(2,1)S(1)}, bf16[96,2048]{1,0:T(8,128)(2,1)S(1)}, u32[]{:S(2)}, u32[]{:S(2)}) collective-permute-start(bf16[96,2048]{1,0:T(8,128)(2,1)S(1)} %collective-permute-done.2), channel_id=1, source_target_pairs={{0,14},{16,240},{2,0},{18,242},{4,2},{20,244},{6,4},{22,246},{8,6}... | collective-permute-start | bytes 1179656 | tf_op jit(solution)/shard_map/ppermute | solution.py:375
  31.1 1.5 %collective-permute-done.4 = bf16[96,2048]{1,0:T(8,128)(2,1)S(1)} collective-permute-done((bf16[96,2048]{1,0:T(8,128)(2,1)S(1)}, bf16[96,2048]{1,0:T(8,128)(2,1)S(1)}, u32[]{:S(2)}, u32[]{:S(2)}) %collective-permute-start.4) | collective-permute-done | bytes 393248 | tf_op jit(solution)/shard_map/ppermute | solution.py:374
  32.6 1.9 %collective-permute-start.7 = (bf16[96,2048]{1,0:T(8,128)(2,1)S(1)}, bf16[96,2048]{1,0:T(8,128)(2,1)S(1)}, u32[]{:S(2)}, u32[]{:S(2)}) collective-permute-start(bf16[96,2048]{1,0:T(8,128)(2,1)S(1)} %collective-permute-done.4), channel_id=1, source_target_pairs={{0,2},{16,48},{2,4},{18,50},{4,6},{20,52},{6,8},{22,54},{8,10},{24... | collective-permute-start | bytes 1179656 | tf_op jit(solution)/shard_map/ppermute | solution.py:374
  34.6 1.2 collective-permute-done.5
  35.8 4.6 %collective-permute-start.6 = (bf16[192,2048]{1,0:T(8,128)(2,1)S(1)}, bf16[192,2048]{1,0:T(8,128)(2,1)S(1)}, u32[]{:S(2)}, u32[]{:S(2)}) collective-permute-start(bf16[192,2048]{1,0:T(8,128)(2,1)S(1)} %constant_dynamic-update-slice_fusion.6.refs_2_), channel_id=1, source_target_pairs={{0,1},{16,273},{2,3},{18,275},{4,5},{20,277},{6,7},{22,279},{8,9},... | collective-permute-start | bytes 2359304 | tf_op jit(solution)/shard_map/ppermute | solution.py:363
  40.4 5.0 %collective-permute-start.8 = (bf16[96,2048]{1,0:T(8,128)(2,1)S(1)}, bf16[96,2048]{1,0:T(8,128)(2,1)S(1)}, u32[]{:S(2)}, u32[]{:S(2)}) collective-permute-start(bf16[96,2048]{1,0:T(8,128)(2,1)S(1)} %collective-permute-done.5), channel_id=1, source_target_pairs={{0,14},{16,240},{2,0},{18,242},{4,2},{20,244},{6,4},{22,246},{8,6}... | collective-permute-start | bytes 1179656 | tf_op jit(solution)/shard_map/ppermute | solution.py:375
  45.5 1.9 %collective-permute-start.9 = (bf16[96,2048]{1,0:T(8,128)(2,1)S(1)}, bf16[96,2048]{1,0:T(8,128)(2,1)S(1)}, u32[]{:S(2)}, u32[]{:S(2)}) collective-permute-start(bf16[96,2048]{1,0:T(8,128)(2,1)S(1)} %collective-permute-done.7), channel_id=1, source_target_pairs={{0,2},{16,48},{2,4},{18,50},{4,6},{20,52},{6,8},{22,54},{8,10},{24... | collective-permute-start | bytes 1179656 | tf_op jit(solution)/shard_map/ppermute | solution.py:380
  47.4 4.6 %collective-permute-start.11 = (bf16[288,2048]{1,0:T(8,128)(2,1)S(1)}, bf16[288,2048]{1,0:T(8,128)(2,1)S(1)}, u32[]{:S(2)}, u32[]{:S(2)}) collective-permute-start(bf16[288,2048]{1,0:T(8,128)(2,1)S(1)} %constant_dynamic-update-slice_fusion.2.refs_0_), channel_id=1, source_target_pairs={{0,16},{16,0},{2,18},{18,2},{4,20},{20,4},{6,22},{22,6},{8,24},{24... | collective-permute-start | bytes 3538952 | tf_op jit(solution)/shard_map/ppermute | solution.py:359
  52.1 1.9 %collective-permute-start.12 = (bf16[288,2048]{1,0:T(8,128)(2,1)S(1)}, bf16[288,2048]{1,0:T(8,128)(2,1)S(1)}, u32[]{:S(2)}, u32[]{:S(2)}) collective-permute-start(bf16[288,2048]{1,0:T(8,128)(2,1)S(1)} %collective-permute-done.3.refs_1_), channel_id=1, source_target_pairs={{0,16},{16,0},{2,18},{18,2},{4,20},{20,4},{6,22},{22,6},{8,24},{24... | collective-permute-start | bytes 3538952 | tf_op jit(solution)/shard_map/ppermute | solution.py:359
  54.0 1.5 %collective-permute-done.9 = bf16[96,2048]{1,0:T(8,128)(2,1)S(1)} collective-permute-done((bf16[96,2048]{1,0:T(8,128)(2,1)S(1)}, bf16[96,2048]{1,0:T(8,128)(2,1)S(1)}, u32[]{:S(2)}, u32[]{:S(2)}) %collective-permute-start.9) | collective-permute-done | bytes 393248 | tf_op jit(solution)/shard_map/ppermute | solution.py:380
  55.6 2.9 %collective-permute-start.10 = (bf16[288,2048]{1,0:T(8,128)(2,1)S(1)}, bf16[288,2048]{1,0:T(8,128)(2,1)S(1)}, u32[]{:S(2)}, u32[]{:S(2)}) collective-permute-start(bf16[288,2048]{1,0:T(8,128)(2,1)S(1)} %pad_maximum_fusion.refs_4_), channel_id=1, source_target_pairs={{0,1},{16,273},{2,3},{18,275},{4,5},{20,277},{6,7},{22,279},{8,9},... | collective-permute-start | bytes 3538952 | tf_op jit(solution)/shard_map/ppermute | solution.py:363
  58.5 6.0 %collective-permute-start.13 = (bf16[192,2048]{1,0:T(8,128)(2,1)S(1)}, bf16[192,2048]{1,0:T(8,128)(2,1)S(1)}, u32[]{:S(2)}, u32[]{:S(2)}) collective-permute-start(bf16[192,2048]{1,0:T(8,128)(2,1)S(1)} %constant_dynamic-update-slice_fusion.6.refs_2_), channel_id=1, source_target_pairs={{0,16},{16,0},{2,18},{18,2},{4,20},{20,4},{6,22},{22,6},{8,24},{24... | collective-permute-start | bytes 2359304 | tf_op jit(solution)/shard_map/ppermute | solution.py:359
  64.5 1.9 %collective-permute-start.14 = (bf16[192,2048]{1,0:T(8,128)(2,1)S(1)}, bf16[192,2048]{1,0:T(8,128)(2,1)S(1)}, u32[]{:S(2)}, u32[]{:S(2)}) collective-permute-start(bf16[192,2048]{1,0:T(8,128)(2,1)S(1)} %collective-permute-done.6.refs_3_), channel_id=1, source_target_pairs={{0,16},{16,0},{2,18},{18,2},{4,20},{20,4},{6,22},{22,6},{8,24},{24... | collective-permute-start | bytes 2359304 | tf_op jit(solution)/shard_map/ppermute | solution.py:359
  66.5 2.4 %collective-permute-start.15 = (bf16[288,2048]{1,0:T(8,128)(2,1)S(1)}, bf16[288,2048]{1,0:T(8,128)(2,1)S(1)}, u32[]{:S(2)}, u32[]{:S(2)}) collective-permute-start(bf16[288,2048]{1,0:T(8,128)(2,1)S(1)} %pad_maximum_fusion.refs_4_), channel_id=1, source_target_pairs={{0,16},{16,0},{2,18},{18,2},{4,20},{20,4},{6,22},{22,6},{8,24},{24... | collective-permute-start | bytes 3538952 | tf_op jit(solution)/shard_map/ppermute | solution.py:359
  68.9 3.2 %shard_map.68.refs_10_ = f32[8,768]{1,0:T(8,128)S(1)} custom-call(bf16[288,2048]{1,0:T(8,128)(2,1)S(1)} %constant_dynamic-update-slice_fusion.2.refs_0_, bf16[288,2048]{1,0:T(8,128)(2,1)S(1)} %collective-permute-done.3.refs_1_, bf16[192,2048]{1,0:T(8,128)(2,1)S(1)} %constant_dynamic-update-slice_fusion.6.refs_2_, ...), custom_call_target="tpu_custom_call" | custom-call | flops 1887436800 | bytes 9830400 | tf_op jit(solution)/shard_map/pallas_call | solution.py:188
  72.1 1.7 %collective-permute-done.10.refs_5_ = bf16[288,2048]{1,0:T(8,128)(2,1)S(1)} collective-permute-done((bf16[288,2048]{1,0:T(8,128)(2,1)S(1)}, bf16[288,2048]{1,0:T(8,128)(2,1)S(1)}, u32[]{:S(2)}, u32[]{:S(2)}) %collective-permute-start.10) | collective-permute-done | bytes 1179680 | tf_op jit(solution)/shard_map/ppermute | solution.py:363
  73.8 5.6 %collective-permute-start.16 = (bf16[288,2048]{1,0:T(8,128)(2,1)S(1)}, bf16[288,2048]{1,0:T(8,128)(2,1)S(1)}, u32[]{:S(2)}, u32[]{:S(2)}) collective-permute-start(bf16[288,2048]{1,0:T(8,128)(2,1)S(1)} %collective-permute-done.10.refs_5_), channel_id=1, source_target_pairs={{0,16},{16,0},{2,18},{18,2},{4,20},{20,4},{6,22},{22,6},{8,24},{24... | collective-permute-start | bytes 3538952 | tf_op jit(solution)/shard_map/ppermute | solution.py:359
  79.4 2.4 %shard_map.69.refs_12_ = f32[8,1024]{1,0:T(8,128)S(1)} custom-call(bf16[288,2048]{1,0:T(8,128)(2,1)S(1)} %constant_dynamic-update-slice_fusion.2.refs_0_, bf16[288,2048]{1,0:T(8,128)(2,1)S(1)} %collective-permute-done.3.refs_1_, bf16[192,2048]{1,0:T(8,128)(2,1)S(1)} %constant_dynamic-update-slice_fusion.6.refs_2_, ...), custom_call_target="tpu_custom_call" | custom-call | flops 1384120320 | bytes 12779520 | tf_op jit(solution)/shard_map/pallas_call | solution.py:249
  81.8 5.7 %shard_map.70 = f32[16,5,8,128]{3,2,1,0:T(8,128)} custom-call(bf16[288,2048]{1,0:T(8,128)(2,1)S(1)} %constant_dynamic-update-slice_fusion.2.refs_0_, bf16[288,2048]{1,0:T(8,128)(2,1)S(1)} %collective-permute-done.3.refs_1_, bf16[192,2048]{1,0:T(8,128)(2,1)S(1)} %constant_dynamic-update-slice_fusion.6.refs_2_, ...), custom_call_target="tpu_custom_call" | custom-call | flops 2768240640 | bytes 15728640 | tf_op jit(solution)/shard_map/pallas_call | solution.py:291
  87.5 9.1 %all-to-all-start = ((f32[16,5,8,128]{3,2,1,0:T(8,128)}), f32[16,5,8,128]{3,2,1,0:T(8,128)S(1)}, u32[]{:S(2)}, u32[]{:S(2)}) async-start(f32[16,5,8,128]{3,2,1,0:T(8,128)} %shard_map.70), calls=%async_computation | async-start | bytes 655360 | tf_op jit(solution)/shard_map/all_to_all | solution.py:394
  96.8 11.2 %all-to-all-done.parts = f32[16,5,8,128]{3,2,1,0:T(8,128)S(1)} async-done(((f32[16,5,8,128]{3,2,1,0:T(8,128)}), f32[16,5,8,128]{3,2,1,0:T(8,128)S(1)}, u32[]{:S(2)}, u32[]{:S(2)}) %all-to-all-start) | async-done | bytes 327712 | tf_op jit(solution)/shard_map/all_to_all | solution.py:394
  108.9 1.9 %collective-permute-start.17 = (f32[1,128]{1,0:T(1,128)S(1)}, f32[1,128]{1,0:T(1,128)S(1)}, u32[]{:S(2)}, u32[]{:S(2)}) collective-permute-start(f32[1,128]{1,0:T(1,128)S(1)} %get-tuple-element.13), channel_id=1, source_target_pairs={{0,16},{16,0},{2,18},{18,2},{4,20},{20,4},{6,22},{22,6},{8,24},{24... | collective-permute-start | bytes 1544 | tf_op jit(solution)/shard_map/ppermute | solution.py:359
  110.9 5.3 %all-to-all-start.1 = ((f32[32,1,128]{2,1,0:T(1,128)}), f32[32,1,128]{2,1,0:T(1,128)S(1)}, u32[]{:S(2)}, u32[]{:S(2)}) async-start(f32[32,1,128]{2,1,0:T(1,128)} %get-tuple-element.14), calls=%async_computation.1 | async-start | bytes 32768 | tf_op jit(solution)/shard_map/all_to_all | solution.py:401
  116.8 8.4 %all-to-all-done.1 = f32[32,1,128]{2,1,0:T(1,128)S(1)} async-done(((f32[32,1,128]{2,1,0:T(1,128)}), f32[32,1,128]{2,1,0:T(1,128)S(1)}, u32[]{:S(2)}, u32[]{:S(2)}) %all-to-all-start.1) | async-done | bytes 16416 | tf_op jit(solution)/shard_map/all_to_all | solution.py:401
  (27 shorter events, 2.8 us)
Async XLA Ops:
  2.5 10.1 %collective-permute-start = (bf16[48,2048]{1,0:T(8,128)(2,1)}, bf16[48,2048]{1,0:T(8,128)(2,1)S(1)}, u32[]{:S(2)}, u32[]{:S(2)}) collective-permute-start(bf16[48,2048]{1,0:T(8,128)(2,1)} %get-tuple-element.10), channel_id=1, source_target_pairs={{0,16},{16,0},{2,18},{18,2},{4,20},{20,4},{6,22},{22,6},{8,24},{24... | collective-permute-start | bytes 589832 | tf_op jit(solution)/shard_map/ppermute | solution.py:359
  12.6 10.0 %collective-permute-start.1 = (bf16[96,2048]{1,0:T(8,128)(2,1)S(1)}, bf16[96,2048]{1,0:T(8,128)(2,1)S(1)}, u32[]{:S(2)}, u32[]{:S(2)}) collective-permute-start(bf16[96,2048]{1,0:T(8,128)(2,1)S(1)} %get-tuple-element.15), channel_id=1, source_target_pairs={{0,2},{16,48},{2,4},{18,50},{4,6},{20,52},{6,8},{22,54},{8,10},{24... | collective-permute-start | bytes 1179656 | tf_op jit(solution)/shard_map/ppermute | solution.py:374
  14.5 10.1 %collective-permute-start.2 = (bf16[96,2048]{1,0:T(8,128)(2,1)S(1)}, bf16[96,2048]{1,0:T(8,128)(2,1)S(1)}, u32[]{:S(2)}, u32[]{:S(2)}) collective-permute-start(bf16[96,2048]{1,0:T(8,128)(2,1)S(1)} %get-tuple-element.15), channel_id=1, source_target_pairs={{0,14},{16,240},{2,0},{18,242},{4,2},{20,244},{6,4},{22,246},{8,6}... | collective-permute-start | bytes 1179656 | tf_op jit(solution)/shard_map/ppermute | solution.py:375
  22.6 10.0 %collective-permute-start.4 = (bf16[96,2048]{1,0:T(8,128)(2,1)S(1)}, bf16[96,2048]{1,0:T(8,128)(2,1)S(1)}, u32[]{:S(2)}, u32[]{:S(2)}) collective-permute-start(bf16[96,2048]{1,0:T(8,128)(2,1)S(1)} %collective-permute-done.1), channel_id=1, source_target_pairs={{0,2},{16,48},{2,4},{18,50},{4,6},{20,52},{6,8},{22,54},{8,10},{24... | collective-permute-start | bytes 1179656 | tf_op jit(solution)/shard_map/ppermute | solution.py:374
  24.6 27.4 %collective-permute-start.3 = (bf16[288,2048]{1,0:T(8,128)(2,1)S(1)}, bf16[288,2048]{1,0:T(8,128)(2,1)S(1)}, u32[]{:S(2)}, u32[]{:S(2)}) collective-permute-start(bf16[288,2048]{1,0:T(8,128)(2,1)S(1)} %constant_dynamic-update-slice_fusion.2.refs_0_), channel_id=1, source_target_pairs={{0,1},{16,273},{2,3},{18,275},{4,5},{20,277},{6,7},{22,279},{8,9},... | collective-permute-start | bytes 3538952 | tf_op jit(solution)/shard_map/ppermute | solution.py:363
  26.5 9.3 %collective-permute-start.5 = (bf16[96,2048]{1,0:T(8,128)(2,1)S(1)}, bf16[96,2048]{1,0:T(8,128)(2,1)S(1)}, u32[]{:S(2)}, u32[]{:S(2)}) collective-permute-start(bf16[96,2048]{1,0:T(8,128)(2,1)S(1)} %collective-permute-done.2), channel_id=1, source_target_pairs={{0,14},{16,240},{2,0},{18,242},{4,2},{20,244},{6,4},{22,246},{8,6}... | collective-permute-start | bytes 1179656 | tf_op jit(solution)/shard_map/ppermute | solution.py:375
  32.6 12.8 %collective-permute-start.7 = (bf16[96,2048]{1,0:T(8,128)(2,1)S(1)}, bf16[96,2048]{1,0:T(8,128)(2,1)S(1)}, u32[]{:S(2)}, u32[]{:S(2)}) collective-permute-start(bf16[96,2048]{1,0:T(8,128)(2,1)S(1)} %collective-permute-done.4), channel_id=1, source_target_pairs={{0,2},{16,48},{2,4},{18,50},{4,6},{20,52},{6,8},{22,54},{8,10},{24... | collective-permute-start | bytes 1179656 | tf_op jit(solution)/shard_map/ppermute | solution.py:374
  35.8 19.8 %collective-permute-start.6 = (bf16[192,2048]{1,0:T(8,128)(2,1)S(1)}, bf16[192,2048]{1,0:T(8,128)(2,1)S(1)}, u32[]{:S(2)}, u32[]{:S(2)}) collective-permute-start(bf16[192,2048]{1,0:T(8,128)(2,1)S(1)} %constant_dynamic-update-slice_fusion.6.refs_2_), channel_id=1, source_target_pairs={{0,1},{16,273},{2,3},{18,275},{4,5},{20,277},{6,7},{22,279},{8,9},... | collective-permute-start | bytes 2359304 | tf_op jit(solution)/shard_map/ppermute | solution.py:363
  40.4 13.6 %collective-permute-start.8 = (bf16[96,2048]{1,0:T(8,128)(2,1)S(1)}, bf16[96,2048]{1,0:T(8,128)(2,1)S(1)}, u32[]{:S(2)}, u32[]{:S(2)}) collective-permute-start(bf16[96,2048]{1,0:T(8,128)(2,1)S(1)} %collective-permute-done.5), channel_id=1, source_target_pairs={{0,14},{16,240},{2,0},{18,242},{4,2},{20,244},{6,4},{22,246},{8,6}... | collective-permute-start | bytes 1179656 | tf_op jit(solution)/shard_map/ppermute | solution.py:375
  45.5 10.0 %collective-permute-start.9 = (bf16[96,2048]{1,0:T(8,128)(2,1)S(1)}, bf16[96,2048]{1,0:T(8,128)(2,1)S(1)}, u32[]{:S(2)}, u32[]{:S(2)}) collective-permute-start(bf16[96,2048]{1,0:T(8,128)(2,1)S(1)} %collective-permute-done.7), channel_id=1, source_target_pairs={{0,2},{16,48},{2,4},{18,50},{4,6},{20,52},{6,8},{22,54},{8,10},{24... | collective-permute-start | bytes 1179656 | tf_op jit(solution)/shard_map/ppermute | solution.py:380
  47.4 19.0 %collective-permute-start.11 = (bf16[288,2048]{1,0:T(8,128)(2,1)S(1)}, bf16[288,2048]{1,0:T(8,128)(2,1)S(1)}, u32[]{:S(2)}, u32[]{:S(2)}) collective-permute-start(bf16[288,2048]{1,0:T(8,128)(2,1)S(1)} %constant_dynamic-update-slice_fusion.2.refs_0_), channel_id=1, source_target_pairs={{0,16},{16,0},{2,18},{18,2},{4,20},{20,4},{6,22},{22,6},{8,24},{24... | collective-permute-start | bytes 3538952 | tf_op jit(solution)/shard_map/ppermute | solution.py:359
  52.1 16.8 %collective-permute-start.12 = (bf16[288,2048]{1,0:T(8,128)(2,1)S(1)}, bf16[288,2048]{1,0:T(8,128)(2,1)S(1)}, u32[]{:S(2)}, u32[]{:S(2)}) collective-permute-start(bf16[288,2048]{1,0:T(8,128)(2,1)S(1)} %collective-permute-done.3.refs_1_), channel_id=1, source_target_pairs={{0,16},{16,0},{2,18},{18,2},{4,20},{20,4},{6,22},{22,6},{8,24},{24... | collective-permute-start | bytes 3538952 | tf_op jit(solution)/shard_map/ppermute | solution.py:359
  55.6 18.2 %collective-permute-start.10 = (bf16[288,2048]{1,0:T(8,128)(2,1)S(1)}, bf16[288,2048]{1,0:T(8,128)(2,1)S(1)}, u32[]{:S(2)}, u32[]{:S(2)}) collective-permute-start(bf16[288,2048]{1,0:T(8,128)(2,1)S(1)} %pad_maximum_fusion.refs_4_), channel_id=1, source_target_pairs={{0,1},{16,273},{2,3},{18,275},{4,5},{20,277},{6,7},{22,279},{8,9},... | collective-permute-start | bytes 3538952 | tf_op jit(solution)/shard_map/ppermute | solution.py:363
  58.5 10.4 %collective-permute-start.13 = (bf16[192,2048]{1,0:T(8,128)(2,1)S(1)}, bf16[192,2048]{1,0:T(8,128)(2,1)S(1)}, u32[]{:S(2)}, u32[]{:S(2)}) collective-permute-start(bf16[192,2048]{1,0:T(8,128)(2,1)S(1)} %constant_dynamic-update-slice_fusion.6.refs_2_), channel_id=1, source_target_pairs={{0,16},{16,0},{2,18},{18,2},{4,20},{20,4},{6,22},{22,6},{8,24},{24... | collective-permute-start | bytes 2359304 | tf_op jit(solution)/shard_map/ppermute | solution.py:359
  64.5 4.4 %collective-permute-start.14 = (bf16[192,2048]{1,0:T(8,128)(2,1)S(1)}, bf16[192,2048]{1,0:T(8,128)(2,1)S(1)}, u32[]{:S(2)}, u32[]{:S(2)}) collective-permute-start(bf16[192,2048]{1,0:T(8,128)(2,1)S(1)} %collective-permute-done.6.refs_3_), channel_id=1, source_target_pairs={{0,16},{16,0},{2,18},{18,2},{4,20},{20,4},{6,22},{22,6},{8,24},{24... | collective-permute-start | bytes 2359304 | tf_op jit(solution)/shard_map/ppermute | solution.py:359
  66.5 12.9 %collective-permute-start.15 = (bf16[288,2048]{1,0:T(8,128)(2,1)S(1)}, bf16[288,2048]{1,0:T(8,128)(2,1)S(1)}, u32[]{:S(2)}, u32[]{:S(2)}) collective-permute-start(bf16[288,2048]{1,0:T(8,128)(2,1)S(1)} %pad_maximum_fusion.refs_4_), channel_id=1, source_target_pairs={{0,16},{16,0},{2,18},{18,2},{4,20},{20,4},{6,22},{22,6},{8,24},{24... | collective-permute-start | bytes 3538952 | tf_op jit(solution)/shard_map/ppermute | solution.py:359
  73.8 8.1 %collective-permute-start.16 = (bf16[288,2048]{1,0:T(8,128)(2,1)S(1)}, bf16[288,2048]{1,0:T(8,128)(2,1)S(1)}, u32[]{:S(2)}, u32[]{:S(2)}) collective-permute-start(bf16[288,2048]{1,0:T(8,128)(2,1)S(1)} %collective-permute-done.10.refs_5_), channel_id=1, source_target_pairs={{0,16},{16,0},{2,18},{18,2},{4,20},{20,4},{6,22},{22,6},{8,24},{24... | collective-permute-start | bytes 3538952 | tf_op jit(solution)/shard_map/ppermute | solution.py:359
  81.8 14.9 %copy-start = (bf16[48,512]{1,0:T(8,128)(2,1)S(1)}, bf16[48,512]{1,0:T(8,128)(2,1)}, u32[]{:S(2)}) copy-start(bf16[48,512]{1,0:T(8,128)(2,1)} %text_s.1) | copy-start | bytes 147460
  81.8 14.9 %copy-start.1 = (bf16[48,512]{1,0:T(8,128)(2,1)S(1)}, bf16[48,512]{1,0:T(8,128)(2,1)}, u32[]{:S(2)}) copy-start(bf16[48,512]{1,0:T(8,128)(2,1)} %image_s.1) | copy-start | bytes 147460
  87.5 20.5 %all-to-all-start = ((f32[16,5,8,128]{3,2,1,0:T(8,128)}), f32[16,5,8,128]{3,2,1,0:T(8,128)S(1)}, u32[]{:S(2)}, u32[]{:S(2)}) async-start(f32[16,5,8,128]{3,2,1,0:T(8,128)} %shard_map.70), calls=%async_computation | async-start | bytes 655360 | tf_op jit(solution)/shard_map/all_to_all | solution.py:394
  108.9 7.3 %collective-permute-start.17 = (f32[1,128]{1,0:T(1,128)S(1)}, f32[1,128]{1,0:T(1,128)S(1)}, u32[]{:S(2)}, u32[]{:S(2)}) collective-permute-start(f32[1,128]{1,0:T(1,128)S(1)} %get-tuple-element.13), channel_id=1, source_target_pairs={{0,16},{16,0},{2,18},{18,2},{4,20},{20,4},{6,22},{22,6},{8,24},{24... | collective-permute-start | bytes 1544 | tf_op jit(solution)/shard_map/ppermute | solution.py:359
  110.9 14.4 %all-to-all-start.1 = ((f32[32,1,128]{2,1,0:T(1,128)}), f32[32,1,128]{2,1,0:T(1,128)S(1)}, u32[]{:S(2)}, u32[]{:S(2)}) async-start(f32[32,1,128]{2,1,0:T(1,128)} %get-tuple-element.14), calls=%async_computation.1 | async-start | bytes 32768 | tf_op jit(solution)/shard_map/all_to_all | solution.py:401
